TPU v7x, 32 devices: a whole 2x2x4 slice. The times are simulated.
32 devices in a mesh: groups: 2 (over x), col: 16 (over z, y, core).
Axes of the slice: x: 2, y: 2, z: 4, core: 2. Of those that a mesh axis runs over, the one named last changes fastest.
Arguments:
- probes: int32 [32, 16384], P(None, ('groups', 'col')), parts along dimension 1, may hold values from 0 to 1
- diag_tiles: float32 [16384, 512], P(('groups', 'col')), parts along dimension 0, as said below
- forward_tiles: float32 [32, 5, 512, 512], P(('groups', 'col')), parts along dimension 0, as said below
- tile_columns: int32 [32, 5], P(('groups', 'col')), parts along dimension 0, may hold values from 0 to 15, as said below
Outputs:
- next_basis: float32 [32, 16384], P(None, ('groups', 'col')), parts along dimension 1
- lanczos_blocks: float32 [8, 32, 32], P('groups'), parts along dimension 0
There are 2 independent parts, one for each index of `groups`. A program takes and returns all parts, laid end to end along the dimension named above; each array names one. Nothing has to cross between parts.
Inputs may be any that keep to these rules, and one draw needn't show every extreme that they name: `tile_columns`: the 5 entries of row block r are distinct and each is (r + d) mod 16 for some d from 1 to 7. `diag_tiles`: each diagonal tile is symmetric. `forward_tiles`: entries of any size and sign.
All inputs are finite; a program needn't handle non-finite values.
Results may differ from a plain program's by a relative error of at most 0.0003.
Values sent between devices are 32-bit elements; how exact they have to be, the bound alone decides.
No kernel may reach another device: no remote copies, remote signals or barrier semaphores. Data moves between devices by JAX's collectives and lax.ppermute only.
A program may use at most 64 MiB of HBM per device.

v0:
```python
import jax
import jax.numpy as jnp
from jax import lax
from jax.sharding import PartitionSpec as P

REACH = 7


precise = lax.Precision.HIGHEST


def from_behind(block, axis, distance):
    devices = range(lax.axis_size(axis))
    route = [((i - distance) % len(devices), i) for i in devices]
    return lax.ppermute(block, axis, route)


def gram_of(vectors):
    return jnp.einsum("pi,qi->pq", vectors, vectors, precision=precise)


def orthonormal(vectors, matrix):
    factor = jnp.linalg.cholesky(matrix)
    return (jax.scipy.linalg.solve_triangular(factor, vectors, lower=True), factor)


def apply_kernel(vectors, diagonal, forward, chooser):
    product = jnp.einsum("pi,ij->pj", vectors, diagonal, precision=precise)
    nearby = []
    for offset in range(1, REACH + 1):
        nearby.append(from_behind(vectors, "col", -offset))
    needed = jnp.einsum("ed,dpj->pej", chooser, jnp.stack(nearby), precision=precise)
    product = product + jnp.einsum("pej,eij->pi", needed, forward, precision=precise)
    outgoing = jnp.einsum("pi,eij->epj", vectors, forward, precision=precise)
    routed = jnp.einsum("ed,epj->dpj", chooser, outgoing, precision=precise)
    for offset in range(1, REACH + 1):
        product = product + from_behind(routed[offset - 1], "col", offset)
    return product


def project(image, basis):
    alpha = lax.psum(jnp.einsum("pi,qi->pq", image, basis, precision=precise), "col")
    remainder = image - jnp.einsum("pq,qi->pi", alpha, basis, precision=precise)
    matrix = lax.psum(gram_of(remainder), "col")
    return (alpha, remainder, matrix)


def body(probes, diag_tiles, forward_tiles, tile_columns):
    forward = forward_tiles[0]
    columns = tile_columns[0]
    cycle_size = lax.axis_size("col")
    position = lax.axis_index("col")
    distance = (columns - position) % cycle_size
    chooser = (distance[:, None] == jnp.arange(1, REACH + 1, dtype=jnp.int32)[None, :]).astype(
        jnp.float32
    )
    signs = 2.0 * probes.astype(jnp.float32) - 1.0
    first_basis = orthonormal(signs, lax.psum(gram_of(signs), "col"))[0]
    image = apply_kernel(first_basis, diag_tiles, forward, chooser)
    alpha_one, remainder, matrix = project(image, first_basis)
    second_basis, beta_one = orthonormal(remainder, matrix)
    image = apply_kernel(second_basis, diag_tiles, forward, chooser)
    image = image - jnp.einsum("qp,qi->pi", beta_one, first_basis, precision=precise)
    alpha_two, remainder, matrix = project(image, second_basis)
    next_basis, beta_two = orthonormal(remainder, matrix)
    return (next_basis, jnp.stack([alpha_one, beta_one, alpha_two, beta_two]))


def solution(mesh):
    placed = (
        P(None, ("groups", "col")),
        P(("groups", "col"), None),
        P(("groups", "col"), None, None, None),
        P(("groups", "col"), None),
    )
    return jax.shard_map(
        body,
        mesh=mesh,
        in_specs=placed,
        out_specs=(P(None, ("groups", "col")), P("groups", None, None)),
        check_vma=False,
    )
```

profile of v0, /device:TPU:0, one launch (start us, length us, event | category | flops | bytes accessed | tf_op | source)
XLA Modules:
  0.0 389.6 jit_solution(15253737478086740471)
XLA Ops:
  0.7 1.2 fusion.46
  1.8 63.0 %psum.35 = f32[32,32]{0,1:T(8,128)S(1)} all-reduce(f32[32,32]{0,1:T(8,128)S(1)} %fusion.46), channel_id=1, replica_groups=mesh['groups'=2,'col'=16] {'col'}, use_global_device_ids=true, to_apply=%region_0.1 | all-reduce | flops 1024 | bytes 8192 | tf_op jit(solution)/shard_map/psum | solution.py:58
  64.9 2.9 cholesky.59
  69.1 2.4 custom-call.7
  71.6 1.1 fusion.45
  73.7 5.7 %fusion.4 = f32[32,5,512]{2,0,1:T(8,128)S(1)} fusion(f32[1,5,512,512]{3,2,1,0:T(8,128)} %param.9, f32[32,512]{1,0:T(8,128)S(1)} %fusion.45), kind=kOutput, calls=%fused_computation.4 | convolution fusion | flops 503316480 | bytes 5636096 | tf_op jit(solution)/shard_map/pi,eij->epj/dot_general | solution.py:34
  80.4 4.7 %collective-permute-start.5 = (f32[32,512]{1,0:T(8,128)S(1)}, f32[32,512]{1,0:T(8,128)S(1)}, u32[]{:S(2)}, u32[]{:S(2)}) collective-permute-start(f32[32,512]{1,0:T(8,128)S(1)} %fusion.45), channel_id=1, source_target_pairs={{6,0},{7,1},{8,2},{9,3},{10,4},{11,5},{12,6},{13,7},{14,8},{15,9},... | collective-permute-start | bytes 196616 | tf_op jit(solution)/shard_map/ppermute | solution.py:15
  85.3 1.8 collective-permute-start.10
  87.1 1.9 collective-permute-start.11
  89.0 0.8 collective-permute-start.12
  89.9 1.8 collective-permute-start.13
  93.1 5.1 %collective-permute-start.8 = (f32[32,512]{1,0:T(8,128)S(1)}, f32[32,512]{1,0:T(8,128)S(1)}, u32[]{:S(2)}, u32[]{:S(2)}) collective-permute-start(f32[32,512]{1,0:T(8,128)S(1)} %bitcast.177), channel_id=1, source_target_pairs={{14,0},{15,1},{0,2},{1,3},{2,4},{3,5},{4,6},{5,7},{6,8},{7,9},{8,1... | collective-permute-start | bytes 196616 | tf_op jit(solution)/shard_map/ppermute | solution.py:15
  98.3 1.2 collective-permute-done.11
  99.9 4.9 %fusion.8 = f32[32,512]{1,0:T(8,128)S(1)} fusion(f32[1,5,512,512]{3,2,1,0:T(8,128)S(1)} %bitcast.169, f32[32,512,5]{1,2,0:T(8,128)S(1)} %fusion.37), kind=kOutput, calls=%fused_computation.8 | convolution fusion | flops 503316480 | bytes 5636096 | tf_op jit(solution)/shard_map/pej,eij->pi/dot_general | solution.py:33
  105.9 60.7 %psum.36 = f32[32,32]{1,0:T(8,128)S(1)} all-reduce(f32[32,32]{1,0:T(8,128)S(1)} %fusion.100), channel_id=1, replica_groups=mesh['groups'=2,'col'=16] {'col'}, use_global_device_ids=true, to_apply=%region_3.6 | all-reduce | flops 1024 | bytes 8192 | tf_op jit(solution)/shard_map/psum | solution.py:42
  167.0 57.8 %psum.37 = f32[32,32]{0,1:T(8,128)S(1)} all-reduce(f32[32,32]{0,1:T(8,128)S(1)} %fusion.101), channel_id=1, replica_groups=mesh['groups'=2,'col'=16] {'col'}, use_global_device_ids=true, to_apply=%region_4.7 | all-reduce | flops 1024 | bytes 8192 | tf_op jit(solution)/shard_map/psum | solution.py:44
  224.8 2.9 cholesky.70
  229.1 2.4 custom-call.8
  232.9 5.8 %fusion = f32[32,5,512]{2,0,1:T(8,128)S(1)} fusion(f32[1,5,512,512]{3,2,1,0:T(8,128)} %param.9, f32[32,512]{1,0:T(8,128)S(1)} %fusion.55), kind=kOutput, calls=%fused_computation | convolution fusion | flops 503316480 | bytes 5636096 | tf_op jit(solution)/shard_map/pi,eij->epj/dot_general | solution.py:34
  239.6 0.9 fusion.70
  240.6 4.4 %collective-permute-start.19 = (f32[32,512]{1,0:T(8,128)S(1)}, f32[32,512]{1,0:T(8,128)S(1)}, u32[]{:S(2)}, u32[]{:S(2)}) collective-permute-start(f32[32,512]{1,0:T(8,128)S(1)} %fusion.55), channel_id=1, source_target_pairs={{6,0},{7,1},{8,2},{9,3},{10,4},{11,5},{12,6},{13,7},{14,8},{15,9},... | collective-permute-start | bytes 196616 | tf_op jit(solution)/shard_map/ppermute | solution.py:15
  245.3 1.8 collective-permute-start.22
  247.1 1.2 collective-permute-start.23
  248.3 2.3 collective-permute-start.24
  251.9 3.2 collective-permute-start.26
  255.2 2.4 collective-permute-start.27
  257.6 5.0 %fusion.11 = f32[32,512]{1,0:T(8,128)S(1)} fusion(f32[1,5,512,512]{3,2,1,0:T(8,128)S(1)} %bitcast.171, f32[32,512,5]{1,2,0:T(8,128)S(1)} %fusion.34), kind=kOutput, calls=%fused_computation.9 | convolution fusion | flops 503316480 | bytes 5636096 | tf_op jit(solution)/shard_map/pej,eij->pi/dot_general | solution.py:33
  263.5 59.8 %psum.38 = f32[32,32]{1,0:T(8,128)S(1)} all-reduce(f32[32,32]{1,0:T(8,128)S(1)} %fusion.102), channel_id=1, replica_groups=mesh['groups'=2,'col'=16] {'col'}, use_global_device_ids=true, to_apply=%region_5.8 | all-reduce | flops 1024 | bytes 8192 | tf_op jit(solution)/shard_map/psum | solution.py:42
  323.7 57.6 %psum.39 = f32[32,32]{0,1:T(8,128)S(1)} all-reduce(f32[32,32]{0,1:T(8,128)S(1)} %fusion.103), channel_id=1, replica_groups=mesh['groups'=2,'col'=16] {'col'}, use_global_device_ids=true, to_apply=%region_6.9 | all-reduce | flops 1024 | bytes 8192 | tf_op jit(solution)/shard_map/psum | solution.py:44
  381.4 2.9 cholesky.81
  385.7 2.4 custom-call.9
  388.1 0.9 fusion.52
  (118 shorter events, 15.2 us)
Async XLA Ops:
  0.6 104.3 %copy-start = (f32[512,512]{1,0:T(8,128)S(1)}, f32[512,512]{1,0:T(8,128)}, u32[]{:S(2)}) copy-start(f32[512,512]{1,0:T(8,128)} %param.8) | copy-start | bytes 3145732
  0.6 78.8 %copy-start.1 = (s32[1,5]{1,0:T(1,128)S(1)}, s32[1,5]{1,0:T(1,128)}, u32[]{:S(2)}) copy-start(s32[1,5]{1,0:T(1,128)} %param.10) | copy-start | bytes 64
  72.7 7.8 %collective-permute-start = (f32[32,512]{1,0:T(8,128)S(1)}, f32[32,512]{1,0:T(8,128)S(1)}, u32[]{:S(2)}, u32[]{:S(2)}) collective-permute-start(f32[32,512]{1,0:T(8,128)S(1)} %fusion.45), channel_id=1, source_target_pairs={{1,0},{2,1},{3,2},{4,3},{5,4},{6,5},{7,6},{8,7},{9,8},{10,9},{11,1... | collective-permute-start | bytes 196616 | tf_op jit(solution)/shard_map/ppermute | solution.py:15
  72.7 12.4 %collective-permute-start.1 = (f32[32,512]{1,0:T(8,128)S(1)}, f32[32,512]{1,0:T(8,128)S(1)}, u32[]{:S(2)}, u32[]{:S(2)}) collective-permute-start(f32[32,512]{1,0:T(8,128)S(1)} %fusion.45), channel_id=1, source_target_pairs={{2,0},{3,1},{4,2},{5,3},{6,4},{7,5},{8,6},{9,7},{10,8},{11,9},{12,... | collective-permute-start | bytes 196616 | tf_op jit(solution)/shard_map/ppermute | solution.py:15
  72.8 12.4 %collective-permute-start.2 = (f32[32,512]{1,0:T(8,128)S(1)}, f32[32,512]{1,0:T(8,128)S(1)}, u32[]{:S(2)}, u32[]{:S(2)}) collective-permute-start(f32[32,512]{1,0:T(8,128)S(1)} %fusion.45), channel_id=1, source_target_pairs={{3,0},{4,1},{5,2},{6,3},{7,4},{8,5},{9,6},{10,7},{11,8},{12,9},{13... | collective-permute-start | bytes 196616 | tf_op jit(solution)/shard_map/ppermute | solution.py:15
  72.9 14.2 %collective-permute-start.3 = (f32[32,512]{1,0:T(8,128)S(1)}, f32[32,512]{1,0:T(8,128)S(1)}, u32[]{:S(2)}, u32[]{:S(2)}) collective-permute-start(f32[32,512]{1,0:T(8,128)S(1)} %fusion.45), channel_id=1, source_target_pairs={{4,0},{5,1},{6,2},{7,3},{8,4},{9,5},{10,6},{11,7},{12,8},{13,9},{1... | collective-permute-start | bytes 196616 | tf_op jit(solution)/shard_map/ppermute | solution.py:15
  72.9 16.1 %collective-permute-start.4 = (f32[32,512]{1,0:T(8,128)S(1)}, f32[32,512]{1,0:T(8,128)S(1)}, u32[]{:S(2)}, u32[]{:S(2)}) collective-permute-start(f32[32,512]{1,0:T(8,128)S(1)} %fusion.45), channel_id=1, source_target_pairs={{5,0},{6,1},{7,2},{8,3},{9,4},{10,5},{11,6},{12,7},{13,8},{14,9},{... | collective-permute-start | bytes 196616 | tf_op jit(solution)/shard_map/ppermute | solution.py:15
  73.7 26.2 %slice-start = ((s8[5242880]{0:T(1024)(128)(4,1)}), s8[1048576]{0:T(1024)(128)(4,1)S(1)}, s32[]{:S(2)}) async-start(s8[5242880]{0:T(1024)(128)(4,1)} %bitcast.168), calls=%async_computation | async-start | bytes 2097152
  73.7 26.2 %slice-start.1 = ((s8[5242880]{0:T(1024)(128)(4,1)}), s8[4194304]{0:T(1024)(128)(4,1)S(1)}, s32[]{:S(2)}) async-start(s8[5242880]{0:T(1024)(128)(4,1)} %bitcast.168), calls=%async_computation.1 | async-start | bytes 8388608
  80.4 9.4 %collective-permute-start.5 = (f32[32,512]{1,0:T(8,128)S(1)}, f32[32,512]{1,0:T(8,128)S(1)}, u32[]{:S(2)}, u32[]{:S(2)}) collective-permute-start(f32[32,512]{1,0:T(8,128)S(1)} %fusion.45), channel_id=1, source_target_pairs={{6,0},{7,1},{8,2},{9,3},{10,4},{11,5},{12,6},{13,7},{14,8},{15,9},... | collective-permute-start | bytes 196616 | tf_op jit(solution)/shard_map/ppermute | solution.py:15
  85.2 6.5 %collective-permute-start.6 = (f32[32,512]{1,0:T(8,128)S(1)}, f32[32,512]{1,0:T(8,128)S(1)}, u32[]{:S(2)}, u32[]{:S(2)}) collective-permute-start(f32[32,512]{1,0:T(8,128)S(1)} %fusion.45), channel_id=1, source_target_pairs={{7,0},{8,1},{9,2},{10,3},{11,4},{12,5},{13,6},{14,7},{15,8},{0,9},... | collective-permute-start | bytes 196616 | tf_op jit(solution)/shard_map/ppermute | solution.py:15
  85.3 7.9 %collective-permute-start.10 = (f32[32,512]{1,0:T(8,128)S(1)}, f32[32,512]{1,0:T(8,128)S(1)}, u32[]{:S(2)}, u32[]{:S(2)}) collective-permute-start(f32[32,512]{1,0:T(8,128)S(1)} %bitcast.187), channel_id=1, source_target_pairs={{12,0},{13,1},{14,2},{15,3},{0,4},{1,5},{2,6},{3,7},{4,8},{5,9},{6... | collective-permute-start | bytes 196616 | tf_op jit(solution)/shard_map/ppermute | solution.py:15
  87.1 12.3 %collective-permute-start.11 = (f32[32,512]{1,0:T(8,128)S(1)}, f32[32,512]{1,0:T(8,128)S(1)}, u32[]{:S(2)}, u32[]{:S(2)}) collective-permute-start(f32[32,512]{1,0:T(8,128)S(1)} %bitcast.185), channel_id=1, source_target_pairs={{11,0},{12,1},{13,2},{14,3},{15,4},{0,5},{1,6},{2,7},{3,8},{4,9},{... | collective-permute-start | bytes 196616 | tf_op jit(solution)/shard_map/ppermute | solution.py:15
  89.0 15.9 %collective-permute-start.12 = (f32[32,512]{1,0:T(8,128)S(1)}, f32[32,512]{1,0:T(8,128)S(1)}, u32[]{:S(2)}, u32[]{:S(2)}) collective-permute-start(f32[32,512]{1,0:T(8,128)S(1)} %bitcast.183), channel_id=1, source_target_pairs={{10,0},{11,1},{12,2},{13,3},{14,4},{15,5},{0,6},{1,7},{2,8},{3,9},... | collective-permute-start | bytes 196616 | tf_op jit(solution)/shard_map/ppermute | solution.py:15
  89.9 15.0 %collective-permute-start.13 = (f32[32,512]{1,0:T(8,128)S(1)}, f32[32,512]{1,0:T(8,128)S(1)}, u32[]{:S(2)}, u32[]{:S(2)}) collective-permute-start(f32[32,512]{1,0:T(8,128)S(1)} %bitcast.181), channel_id=1, source_target_pairs={{9,0},{10,1},{11,2},{12,3},{13,4},{14,5},{15,6},{0,7},{1,8},{2,9},... | collective-permute-start | bytes 196616 | tf_op jit(solution)/shard_map/ppermute | solution.py:15
  91.7 13.2 %collective-permute-start.7 = (f32[32,512]{1,0:T(8,128)S(1)}, f32[32,512]{1,0:T(8,128)S(1)}, u32[]{:S(2)}, u32[]{:S(2)}) collective-permute-start(f32[32,512]{1,0:T(8,128)S(1)} %bitcast.179), channel_id=1, source_target_pairs={{15,0},{0,1},{1,2},{2,3},{3,4},{4,5},{5,6},{6,7},{7,8},{8,9},{9,10... | collective-permute-start | bytes 196616 | tf_op jit(solution)/shard_map/ppermute | solution.py:15
  93.1 11.8 %collective-permute-start.8 = (f32[32,512]{1,0:T(8,128)S(1)}, f32[32,512]{1,0:T(8,128)S(1)}, u32[]{:S(2)}, u32[]{:S(2)}) collective-permute-start(f32[32,512]{1,0:T(8,128)S(1)} %bitcast.177), channel_id=1, source_target_pairs={{14,0},{15,1},{0,2},{1,3},{2,4},{3,5},{4,6},{5,7},{6,8},{7,9},{8,1... | collective-permute-start | bytes 196616 | tf_op jit(solution)/shard_map/ppermute | solution.py:15
  99.4 5.5 %collective-permute-start.9 = (f32[32,512]{1,0:T(8,128)S(1)}, f32[32,512]{1,0:T(8,128)S(1)}, u32[]{:S(2)}, u32[]{:S(2)}) collective-permute-start(f32[32,512]{1,0:T(8,128)S(1)} %bitcast.176), channel_id=1, source_target_pairs={{13,0},{14,1},{15,2},{0,3},{1,4},{2,5},{3,6},{4,7},{5,8},{6,9},{7,... | collective-permute-start | bytes 196616 | tf_op jit(solution)/shard_map/ppermute | solution.py:15
  231.8 8.8 %collective-permute-start.14 = (f32[32,512]{1,0:T(8,128)S(1)}, f32[32,512]{1,0:T(8,128)S(1)}, u32[]{:S(2)}, u32[]{:S(2)}) collective-permute-start(f32[32,512]{1,0:T(8,128)S(1)} %fusion.55), channel_id=1, source_target_pairs={{1,0},{2,1},{3,2},{4,3},{5,4},{6,5},{7,6},{8,7},{9,8},{10,9},{11,1... | collective-permute-start | bytes 196616 | tf_op jit(solution)/shard_map/ppermute | solution.py:15
  231.9 13.2 %collective-permute-start.15 = (f32[32,512]{1,0:T(8,128)S(1)}, f32[32,512]{1,0:T(8,128)S(1)}, u32[]{:S(2)}, u32[]{:S(2)}) collective-permute-start(f32[32,512]{1,0:T(8,128)S(1)} %fusion.55), channel_id=1, source_target_pairs={{2,0},{3,1},{4,2},{5,3},{6,4},{7,5},{8,6},{9,7},{10,8},{11,9},{12,... | collective-permute-start | bytes 196616 | tf_op jit(solution)/shard_map/ppermute | solution.py:15
  232.0 13.2 %collective-permute-start.16 = (f32[32,512]{1,0:T(8,128)S(1)}, f32[32,512]{1,0:T(8,128)S(1)}, u32[]{:S(2)}, u32[]{:S(2)}) collective-permute-start(f32[32,512]{1,0:T(8,128)S(1)} %fusion.55), channel_id=1, source_target_pairs={{3,0},{4,1},{5,2},{6,3},{7,4},{8,5},{9,6},{10,7},{11,8},{12,9},{13... | collective-permute-start | bytes 196616 | tf_op jit(solution)/shard_map/ppermute | solution.py:15
  232.0 13.3 %collective-permute-start.17 = (f32[32,512]{1,0:T(8,128)S(1)}, f32[32,512]{1,0:T(8,128)S(1)}, u32[]{:S(2)}, u32[]{:S(2)}) collective-permute-start(f32[32,512]{1,0:T(8,128)S(1)} %fusion.55), channel_id=1, source_target_pairs={{4,0},{5,1},{6,2},{7,3},{8,4},{9,5},{10,6},{11,7},{12,8},{13,9},{1... | collective-permute-start | bytes 196616 | tf_op jit(solution)/shard_map/ppermute | solution.py:15
  232.1 15.0 %collective-permute-start.18 = (f32[32,512]{1,0:T(8,128)S(1)}, f32[32,512]{1,0:T(8,128)S(1)}, u32[]{:S(2)}, u32[]{:S(2)}) collective-permute-start(f32[32,512]{1,0:T(8,128)S(1)} %fusion.55), channel_id=1, source_target_pairs={{5,0},{6,1},{7,2},{8,3},{9,4},{10,5},{11,6},{12,7},{13,8},{14,9},{... | collective-permute-start | bytes 196616 | tf_op jit(solution)/shard_map/ppermute | solution.py:15
  240.6 7.7 %collective-permute-start.19 = (f32[32,512]{1,0:T(8,128)S(1)}, f32[32,512]{1,0:T(8,128)S(1)}, u32[]{:S(2)}, u32[]{:S(2)}) collective-permute-start(f32[32,512]{1,0:T(8,128)S(1)} %fusion.55), channel_id=1, source_target_pairs={{6,0},{7,1},{8,2},{9,3},{10,4},{11,5},{12,6},{13,7},{14,8},{15,9},... | collective-permute-start | bytes 196616 | tf_op jit(solution)/shard_map/ppermute | solution.py:15
  245.1 5.6 %collective-permute-start.20 = (f32[32,512]{1,0:T(8,128)S(1)}, f32[32,512]{1,0:T(8,128)S(1)}, u32[]{:S(2)}, u32[]{:S(2)}) collective-permute-start(f32[32,512]{1,0:T(8,128)S(1)} %fusion.55), channel_id=1, source_target_pairs={{7,0},{8,1},{9,2},{10,3},{11,4},{12,5},{13,6},{14,7},{15,8},{0,9},... | collective-permute-start | bytes 196616 | tf_op jit(solution)/shard_map/ppermute | solution.py:15
  245.2 6.8 %collective-permute-start.21 = (f32[32,512]{1,0:T(8,128)S(1)}, f32[32,512]{1,0:T(8,128)S(1)}, u32[]{:S(2)}, u32[]{:S(2)}) collective-permute-start(f32[32,512]{1,0:T(8,128)S(1)} %bitcast.186), channel_id=1, source_target_pairs={{15,0},{0,1},{1,2},{2,3},{3,4},{4,5},{5,6},{6,7},{7,8},{8,9},{9,10... | collective-permute-start | bytes 196616 | tf_op jit(solution)/shard_map/ppermute | solution.py:15
  245.3 9.8 %collective-permute-start.22 = (f32[32,512]{1,0:T(8,128)S(1)}, f32[32,512]{1,0:T(8,128)S(1)}, u32[]{:S(2)}, u32[]{:S(2)}) collective-permute-start(f32[32,512]{1,0:T(8,128)S(1)} %bitcast.184), channel_id=1, source_target_pairs={{14,0},{15,1},{0,2},{1,3},{2,4},{3,5},{4,6},{5,7},{6,8},{7,9},{8,1... | collective-permute-start | bytes 196616 | tf_op jit(solution)/shard_map/ppermute | solution.py:15
  247.1 15.4 %collective-permute-start.23 = (f32[32,512]{1,0:T(8,128)S(1)}, f32[32,512]{1,0:T(8,128)S(1)}, u32[]{:S(2)}, u32[]{:S(2)}) collective-permute-start(f32[32,512]{1,0:T(8,128)S(1)} %bitcast.182), channel_id=1, source_target_pairs={{13,0},{14,1},{15,2},{0,3},{1,4},{2,5},{3,6},{4,7},{5,8},{6,9},{7,... | collective-permute-start | bytes 196616 | tf_op jit(solution)/shard_map/ppermute | solution.py:15
  248.3 14.2 %collective-permute-start.24 = (f32[32,512]{1,0:T(8,128)S(1)}, f32[32,512]{1,0:T(8,128)S(1)}, u32[]{:S(2)}, u32[]{:S(2)}) collective-permute-start(f32[32,512]{1,0:T(8,128)S(1)} %bitcast.180), channel_id=1, source_target_pairs={{12,0},{13,1},{14,2},{15,3},{0,4},{1,5},{2,6},{3,7},{4,8},{5,9},{6... | collective-permute-start | bytes 196616 | tf_op jit(solution)/shard_map/ppermute | solution.py:15
  250.6 11.9 %collective-permute-start.25 = (f32[32,512]{1,0:T(8,128)S(1)}, f32[32,512]{1,0:T(8,128)S(1)}, u32[]{:S(2)}, u32[]{:S(2)}) collective-permute-start(f32[32,512]{1,0:T(8,128)S(1)} %bitcast.178), channel_id=1, source_target_pairs={{11,0},{12,1},{13,2},{14,3},{15,4},{0,5},{1,6},{2,7},{3,8},{4,9},{... | collective-permute-start | bytes 196616 | tf_op jit(solution)/shard_map/ppermute | solution.py:15
  251.9 10.6 %collective-permute-start.26 = (f32[32,512]{1,0:T(8,128)S(1)}, f32[32,512]{1,0:T(8,128)S(1)}, u32[]{:S(2)}, u32[]{:S(2)}) collective-permute-start(f32[32,512]{1,0:T(8,128)S(1)} %bitcast.175), channel_id=1, source_target_pairs={{10,0},{11,1},{12,2},{13,3},{14,4},{15,5},{0,6},{1,7},{2,8},{3,9},... | collective-permute-start | bytes 196616 | tf_op jit(solution)/shard_map/ppermute | solution.py:15
  255.2 7.4 %collective-permute-start.27 = (f32[32,512]{1,0:T(8,128)S(1)}, f32[32,512]{1,0:T(8,128)S(1)}, u32[]{:S(2)}, u32[]{:S(2)}) collective-permute-start(f32[32,512]{1,0:T(8,128)S(1)} %bitcast.174), channel_id=1, source_target_pairs={{9,0},{10,1},{11,2},{12,3},{13,4},{14,5},{15,6},{0,7},{1,8},{2,9},... | collective-permute-start | bytes 196616 | tf_op jit(solution)/shard_map/ppermute | solution.py:15
  (2 other events, 51.7 us)
where the time goes:
time: 390 us
  blocking collectives  299 us (77%)
  starting transfers between devices  35.6 us (9%)
  matrix products  30.9 us (8%)
  other arithmetic  20.7 us (5%)
    psum x2, blocking collectives, project(): lax.psum(jnp.einsum('pi,qi->pq', image, basis, precision=precise), 'col')  120 us
    psum x2, blocking collectives, project(): matrix = lax.psum(gram_of(remainder), 'col')  115 us
    psum x1, blocking collectives, body(): first_basis = orthonormal(signs, lax.psum(gram_of(signs), 'col'))[0]  63 us
    ppermute x28, starting transfers between devices, from_behind(): return lax.ppermute(block, axis, route)  35.6 us
    dot_general x2, matrix products, apply_kernel(): outgoing = jnp.einsum('pi,eij->epj', vectors, forward, precision=precise)  11.5 us
    another operation x9, other arithmetic, orthonormal(): factor = jnp.linalg.cholesky(matrix)  10.8 us
    dot_general x2, matrix products, apply_kernel(): jnp.einsum('pej,eij->pi', needed, forward, precision=precise)  9.9 us
    another operation x4, other arithmetic, orthonormal(): jax.scipy.linalg.solve_triangular(factor, vectors, lower=True)  7.96 us
  transfers between devices with their start and end apart: 28, of which 1 were waited for; matrix products, arithmetic and copies ran while one was open for 7% of the time, Pallas kernels for 0%

commit v1 on v0

--- a/solution.py
+++ b/solution.py
@@ -13,6 +13,17 @@
     devices = range(lax.axis_size(axis))
     route = [((i - distance) % len(devices), i) for i in devices]
     return lax.ppermute(block, axis, route)
+
+
+def total(block, axis):
+    devices = lax.axis_size(axis)
+    if devices & (devices - 1):
+        return lax.psum(block, axis)
+    stride = 1
+    while stride < devices:
+        block = block + lax.ppermute(block, axis, [(i ^ stride, i) for i in range(devices)])
+        stride *= 2
+    return block
 
 
 def gram_of(vectors):
@@ -39,9 +50,9 @@
 
 
 def project(image, basis):
-    alpha = lax.psum(jnp.einsum("pi,qi->pq", image, basis, precision=precise), "col")
+    alpha = total(jnp.einsum("pi,qi->pq", image, basis, precision=precise), "col")
     remainder = image - jnp.einsum("pq,qi->pi", alpha, basis, precision=precise)
-    matrix = lax.psum(gram_of(remainder), "col")
+    matrix = total(gram_of(remainder), "col")
     return (alpha, remainder, matrix)
 
 
@@ -55,7 +66,7 @@
         jnp.float32
     )
     signs = 2.0 * probes.astype(jnp.float32) - 1.0
-    first_basis = orthonormal(signs, lax.psum(gram_of(signs), "col"))[0]
+    first_basis = orthonormal(signs, total(gram_of(signs), "col"))[0]
     image = apply_kernel(first_basis, diag_tiles, forward, chooser)
     alpha_one, remainder, matrix = project(image, first_basis)
     second_basis, beta_one = orthonormal(remainder, matrix)

time: 390 us -> 165 us (0.42)
  blocking collectives: 299 us -> 0 us
  waiting for transfers between devices: 1.23 us -> 49.3 us
  starting transfers between devices: 35.6 us -> 61.3 us
    psum x5 -> x0, blocking collectives: 299 us -> none  [the longest x2 120 us: project(): lax.psum(jnp.einsum('pi,qi->pq', image, basis, precision=precise), 'col')]
    ppermute x0 -> x20, waiting for transfers between devices: none -> 49.1 us  [total(): lax.ppermute(block, axis, [(i ^ stride, i) for i in range(devices)])]
    ppermute x0 -> x20, starting transfers between devices: none -> 19.7 us  [total(): lax.ppermute(block, axis, [(i ^ stride, i) for i in range(devices)])]
    ppermute x28, starting transfers between devices: 35.6 us -> 41.5 us  [from_behind(): return lax.ppermute(block, axis, route)]
  transfers between devices with their start and end apart: 28 -> 48, of which waited for: 1 -> 21; matrix products, arithmetic and copies ran while one was open for 7% -> 16% of each run, Pallas kernels for 0% -> 0%
where the time goes in v1:
time: 165 us
  starting transfers between devices  61.3 us (37%)
  waiting for transfers between devices  49.3 us (30%)
  matrix products  30.6 us (19%)
  other arithmetic  21.5 us (13%)
    ppermute x20, waiting for transfers between devices, total(): lax.ppermute(block, axis, [(i ^ stride, i) for i in range(devices)])  49.1 us
    ppermute x28, starting transfers between devices, from_behind(): return lax.ppermute(block, axis, route)  41.5 us
    ppermute x20, starting transfers between devices, total(): lax.ppermute(block, axis, [(i ^ stride, i) for i in range(devices)])  19.7 us
    dot_general x2, matrix products, apply_kernel(): outgoing = jnp.einsum('pi,eij->epj', vectors, forward, precision=precise)  11.1 us
    another operation x9, other arithmetic, orthonormal(): factor = jnp.linalg.cholesky(matrix)  10.8 us
    dot_general x2, matrix products, apply_kernel(): jnp.einsum('pej,eij->pi', needed, forward, precision=precise)  9.92 us
    another operation x4, other arithmetic, orthonormal(): jax.scipy.linalg.solve_triangular(factor, vectors, lower=True)  7.96 us
  transfers between devices with their start and end apart: 48, of which 21 were waited for; matrix products, arithmetic and copies ran while one was open for 16% of the time, Pallas kernels for 0%

profile of v1, /device:TPU:0, one launch (start us, length us, event | category | flops | bytes accessed | tf_op | source)
XLA Modules:
  0.0 164.9 jit_solution(14755625434844459658)
XLA Ops:
  3.2 2.9 %collective-permute-start.1 = (f32[32,32]{0,1:T(8,128)S(1)}, f32[32,32]{0,1:T(8,128)S(1)}, u32[]{:S(2)}, u32[]{:S(2)}) collective-permute-start(f32[32,32]{0,1:T(8,128)S(1)} %add.135), channel_id=1, source_target_pairs={{2,0},{3,1},{0,2},{1,3},{6,4},{7,5},{4,6},{5,7},{10,8},{11,9},{8,1... | collective-permute-start | bytes 12296 | tf_op jit(solution)/shard_map/ppermute | solution.py:24
  7.8 2.1 %collective-permute-start.2 = (f32[32,32]{0,1:T(8,128)S(1)}, f32[32,32]{0,1:T(8,128)S(1)}, u32[]{:S(2)}, u32[]{:S(2)}) collective-permute-start(f32[32,32]{0,1:T(8,128)S(1)} %add.136), channel_id=1, source_target_pairs={{4,0},{5,1},{6,2},{7,3},{0,4},{1,5},{2,6},{3,7},{12,8},{13,9},{14,... | collective-permute-start | bytes 12296 | tf_op jit(solution)/shard_map/ppermute | solution.py:24
  11.6 3.0 %collective-permute-start.3 = (f32[32,32]{0,1:T(8,128)S(1)}, f32[32,32]{0,1:T(8,128)S(1)}, u32[]{:S(2)}, u32[]{:S(2)}) collective-permute-start(f32[32,32]{0,1:T(8,128)S(1)} %add.137), channel_id=1, source_target_pairs={{8,0},{9,1},{10,2},{11,3},{12,4},{13,5},{14,6},{15,7},{0,8},{1,9},... | collective-permute-start | bytes 12296 | tf_op jit(solution)/shard_map/ppermute | solution.py:24
  16.4 2.9 %cholesky.59 = f32[32,32]{1,0:T(8,128)S(1)} custom-call(f32[32,32]{1,0:T(8,128)S(1)} %fusion.59), custom_call_target="Cholesky" | custom-call | tf_op jit(solution)/shard_map/jit(cholesky)/cholesky | solution.py:34
  20.6 2.4 %custom-call.7 = f32[1,32,32]{1,2,0:T(8,128)S(1)} custom-call(f32[1,32,32]{2,1,0:T(8,128)S(1)} %fusion.51), custom_call_target="InvertDiagBlocksLowerTriangular" | custom-call | tf_op jit(solution)/shard_map/jit(_solve_triangular)/triangular_solve | solution.py:35
  25.7 3.7 %collective-permute-start.5 = (f32[32,512]{1,0:T(8,128)S(1)}, f32[32,512]{1,0:T(8,128)S(1)}, u32[]{:S(2)}, u32[]{:S(2)}) collective-permute-start(f32[32,512]{1,0:T(8,128)S(1)} %fusion.45), channel_id=1, source_target_pairs={{2,0},{3,1},{4,2},{5,3},{6,4},{7,5},{8,6},{9,7},{10,8},{11,9},{12,... | collective-permute-start | bytes 196616 | tf_op jit(solution)/shard_map/ppermute | solution.py:15
  30.2 5.6 %fusion.4 = f32[32,5,512]{2,0,1:T(8,128)S(1)} fusion(f32[1,5,512,512]{3,2,1,0:T(8,128)} %param.9, f32[32,512]{1,0:T(8,128)S(1)} %fusion.45), kind=kOutput, calls=%fused_computation.4 | convolution fusion | flops 503316480 | bytes 5636096 | tf_op jit(solution)/shard_map/pi,eij->epj/dot_general | solution.py:45
  36.7 3.7 %collective-permute-start.9 = (f32[32,512]{1,0:T(8,128)S(1)}, f32[32,512]{1,0:T(8,128)S(1)}, u32[]{:S(2)}, u32[]{:S(2)}) collective-permute-start(f32[32,512]{1,0:T(8,128)S(1)} %fusion.45), channel_id=1, source_target_pairs={{6,0},{7,1},{8,2},{9,3},{10,4},{11,5},{12,6},{13,7},{14,8},{15,9},... | collective-permute-start | bytes 196616 | tf_op jit(solution)/shard_map/ppermute | solution.py:15
  41.0 2.5 %collective-permute-start.12 = (f32[32,512]{1,0:T(8,128)S(1)}, f32[32,512]{1,0:T(8,128)S(1)}, u32[]{:S(2)}, u32[]{:S(2)}) collective-permute-start(f32[32,512]{1,0:T(8,128)S(1)} %bitcast.183), channel_id=1, source_target_pairs={{14,0},{15,1},{0,2},{1,3},{2,4},{3,5},{4,6},{5,7},{6,8},{7,9},{8,1... | collective-permute-start | bytes 196616 | tf_op jit(solution)/shard_map/ppermute | solution.py:15
  44.4 2.6 %collective-permute-start.14 = (f32[32,512]{1,0:T(8,128)S(1)}, f32[32,512]{1,0:T(8,128)S(1)}, u32[]{:S(2)}, u32[]{:S(2)}) collective-permute-start(f32[32,512]{1,0:T(8,128)S(1)} %bitcast.179), channel_id=1, source_target_pairs={{12,0},{13,1},{14,2},{15,3},{0,4},{1,5},{2,6},{3,7},{4,8},{5,9},{6... | collective-permute-start | bytes 196616 | tf_op jit(solution)/shard_map/ppermute | solution.py:15
  47.8 2.5 %collective-permute-start.16 = (f32[32,512]{1,0:T(8,128)S(1)}, f32[32,512]{1,0:T(8,128)S(1)}, u32[]{:S(2)}, u32[]{:S(2)}) collective-permute-start(f32[32,512]{1,0:T(8,128)S(1)} %bitcast.175), channel_id=1, source_target_pairs={{10,0},{11,1},{12,2},{13,3},{14,4},{15,5},{0,6},{1,7},{2,8},{3,9},... | collective-permute-start | bytes 196616 | tf_op jit(solution)/shard_map/ppermute | solution.py:15
  50.3 3.3 %collective-permute-start.17 = (f32[32,512]{1,0:T(8,128)S(1)}, f32[32,512]{1,0:T(8,128)S(1)}, u32[]{:S(2)}, u32[]{:S(2)}) collective-permute-start(f32[32,512]{1,0:T(8,128)S(1)} %bitcast.174), channel_id=1, source_target_pairs={{9,0},{10,1},{11,2},{12,3},{13,4},{14,5},{15,6},{0,7},{1,8},{2,9},... | collective-permute-start | bytes 196616 | tf_op jit(solution)/shard_map/ppermute | solution.py:15
  53.6 5.0 %fusion.8 = f32[32,512]{1,0:T(8,128)S(1)} fusion(f32[1,5,512,512]{3,2,1,0:T(8,128)S(1)} %bitcast.169, f32[32,512,5]{1,2,0:T(8,128)S(1)} %fusion.37), kind=kOutput, calls=%fused_computation.8 | convolution fusion | flops 503316480 | bytes 5636096 | tf_op jit(solution)/shard_map/pej,eij->pi/dot_general | solution.py:44
  65.6 3.6 %collective-permute-done.20 = f32[32,32]{1,0:T(8,128)S(1)} collective-permute-done((f32[32,32]{1,0:T(8,128)S(1)}, f32[32,32]{1,0:T(8,128)S(1)}, u32[]{:S(2)}, u32[]{:S(2)}) %collective-permute-start.20) | collective-permute-done | bytes 4128 | tf_op jit(solution)/shard_map/ppermute | solution.py:24
  69.6 4.3 %collective-permute-done.21 = f32[32,32]{1,0:T(8,128)S(1)} collective-permute-done((f32[32,32]{1,0:T(8,128)S(1)}, f32[32,32]{1,0:T(8,128)S(1)}, u32[]{:S(2)}, u32[]{:S(2)}) %collective-permute-start.21) | collective-permute-done | bytes 4128 | tf_op jit(solution)/shard_map/ppermute | solution.py:24
  79.4 3.6 %collective-permute-done.24 = f32[32,32]{0,1:T(8,128)S(1)} collective-permute-done((f32[32,32]{0,1:T(8,128)S(1)}, f32[32,32]{0,1:T(8,128)S(1)}, u32[]{:S(2)}, u32[]{:S(2)}) %collective-permute-start.24) | collective-permute-done | bytes 4128 | tf_op jit(solution)/shard_map/ppermute | solution.py:24
  83.4 4.2 %collective-permute-done.25 = f32[32,32]{0,1:T(8,128)S(1)} collective-permute-done((f32[32,32]{0,1:T(8,128)S(1)}, f32[32,32]{0,1:T(8,128)S(1)}, u32[]{:S(2)}, u32[]{:S(2)}) %collective-permute-start.25) | collective-permute-done | bytes 4128 | tf_op jit(solution)/shard_map/ppermute | solution.py:24
  87.8 2.9 %cholesky.70 = f32[32,32]{1,0:T(8,128)S(1)} custom-call(f32[32,32]{1,0:T(8,128)S(1)} %fusion.57), custom_call_target="Cholesky" | custom-call | tf_op jit(solution)/shard_map/jit(cholesky)/cholesky | solution.py:34
  92.0 2.4 %custom-call.8 = f32[1,32,32]{1,2,0:T(8,128)S(1)} custom-call(f32[1,32,32]{2,1,0:T(8,128)S(1)} %get-tuple-element.19), custom_call_target="InvertDiagBlocksLowerTriangular" | custom-call | tf_op jit(solution)/shard_map/jit(_solve_triangular)/triangular_solve | solution.py:35
  94.8 2.7 %collective-permute-start.27 = (f32[32,512]{1,0:T(8,128)S(1)}, f32[32,512]{1,0:T(8,128)S(1)}, u32[]{:S(2)}, u32[]{:S(2)}) collective-permute-start(f32[32,512]{1,0:T(8,128)S(1)} %fusion.55), channel_id=1, source_target_pairs={{2,0},{3,1},{4,2},{5,3},{6,4},{7,5},{8,6},{9,7},{10,8},{11,9},{12,... | collective-permute-start | bytes 196616 | tf_op jit(solution)/shard_map/ppermute | solution.py:15
  100.4 5.6 %fusion = f32[32,5,512]{2,0,1:T(8,128)S(1)} fusion(f32[1,5,512,512]{3,2,1,0:T(8,128)} %param.9, f32[32,512]{1,0:T(8,128)S(1)} %fusion.55), kind=kOutput, calls=%fused_computation | convolution fusion | flops 503316480 | bytes 5636096 | tf_op jit(solution)/shard_map/pi,eij->epj/dot_general | solution.py:45
  113.3 2.7 %collective-permute-start.36 = (f32[32,512]{1,0:T(8,128)S(1)}, f32[32,512]{1,0:T(8,128)S(1)}, u32[]{:S(2)}, u32[]{:S(2)}) collective-permute-start(f32[32,512]{1,0:T(8,128)S(1)} %bitcast.178), channel_id=1, source_target_pairs={{12,0},{13,1},{14,2},{15,3},{0,4},{1,5},{2,6},{3,7},{4,8},{5,9},{6... | collective-permute-start | bytes 196616 | tf_op jit(solution)/shard_map/ppermute | solution.py:15
  116.8 2.5 %collective-permute-start.38 = (f32[32,512]{1,0:T(8,128)S(1)}, f32[32,512]{1,0:T(8,128)S(1)}, u32[]{:S(2)}, u32[]{:S(2)}) collective-permute-start(f32[32,512]{1,0:T(8,128)S(1)} %bitcast.173), channel_id=1, source_target_pairs={{10,0},{11,1},{12,2},{13,3},{14,4},{15,5},{0,6},{1,7},{2,8},{3,9},... | collective-permute-start | bytes 196616 | tf_op jit(solution)/shard_map/ppermute | solution.py:15
  119.3 3.4 %collective-permute-start.39 = (f32[32,512]{1,0:T(8,128)S(1)}, f32[32,512]{1,0:T(8,128)S(1)}, u32[]{:S(2)}, u32[]{:S(2)}) collective-permute-start(f32[32,512]{1,0:T(8,128)S(1)} %bitcast.172), channel_id=1, source_target_pairs={{9,0},{10,1},{11,2},{12,3},{13,4},{14,5},{15,6},{0,7},{1,8},{2,9},... | collective-permute-start | bytes 196616 | tf_op jit(solution)/shard_map/ppermute | solution.py:15
  122.7 5.0 %fusion.11 = f32[32,512]{1,0:T(8,128)S(1)} fusion(f32[1,5,512,512]{3,2,1,0:T(8,128)S(1)} %bitcast.171, f32[32,512,5]{1,2,0:T(8,128)S(1)} %fusion.34), kind=kOutput, calls=%fused_computation.9 | convolution fusion | flops 503316480 | bytes 5636096 | tf_op jit(solution)/shard_map/pej,eij->pi/dot_general | solution.py:44
  132.4 2.0 %collective-permute-done.41 = f32[32,32]{1,0:T(8,128)S(1)} collective-permute-done((f32[32,32]{1,0:T(8,128)S(1)}, f32[32,32]{1,0:T(8,128)S(1)}, u32[]{:S(2)}, u32[]{:S(2)}) %collective-permute-start.41) | collective-permute-done | bytes 4128 | tf_op jit(solution)/shard_map/ppermute | solution.py:24
  134.6 3.6 %collective-permute-done.42 = f32[32,32]{1,0:T(8,128)S(1)} collective-permute-done((f32[32,32]{1,0:T(8,128)S(1)}, f32[32,32]{1,0:T(8,128)S(1)}, u32[]{:S(2)}, u32[]{:S(2)}) %collective-permute-start.42) | collective-permute-done | bytes 4128 | tf_op jit(solution)/shard_map/ppermute | solution.py:24
  138.4 4.4 %collective-permute-done.43 = f32[32,32]{1,0:T(8,128)S(1)} collective-permute-done((f32[32,32]{1,0:T(8,128)S(1)}, f32[32,32]{1,0:T(8,128)S(1)}, u32[]{:S(2)}, u32[]{:S(2)}) %collective-permute-start.43) | collective-permute-done | bytes 4128 | tf_op jit(solution)/shard_map/ppermute | solution.py:24
  148.4 3.6 %collective-permute-done.46 = f32[32,32]{0,1:T(8,128)S(1)} collective-permute-done((f32[32,32]{0,1:T(8,128)S(1)}, f32[32,32]{0,1:T(8,128)S(1)}, u32[]{:S(2)}, u32[]{:S(2)}) %collective-permute-start.46) | collective-permute-done | bytes 4128 | tf_op jit(solution)/shard_map/ppermute | solution.py:24
  152.2 4.4 %collective-permute-done.47 = f32[32,32]{0,1:T(8,128)S(1)} collective-permute-done((f32[32,32]{0,1:T(8,128)S(1)}, f32[32,32]{0,1:T(8,128)S(1)}, u32[]{:S(2)}, u32[]{:S(2)}) %collective-permute-start.47) | collective-permute-done | bytes 4128 | tf_op jit(solution)/shard_map/ppermute | solution.py:24
  156.7 2.9 %cholesky.81 = f32[32,32]{1,0:T(8,128)S(1)} custom-call(f32[32,32]{1,0:T(8,128)S(1)} %fusion.54), custom_call_target="Cholesky" | custom-call | tf_op jit(solution)/shard_map/jit(cholesky)/cholesky | solution.py:34
  160.9 2.4 %custom-call.9 = f32[1,32,32]{1,2,0:T(8,128)S(1)} custom-call(f32[1,32,32]{2,1,0:T(8,128)S(1)} %get-tuple-element.21), custom_call_target="InvertDiagBlocksLowerTriangular" | custom-call | tf_op jit(solution)/shard_map/jit(_solve_triangular)/triangular_solve | solution.py:35
  (171 shorter events, 55.2 us)
Async XLA Ops:
  11.6 4.8 %collective-permute-start.3 = (f32[32,32]{0,1:T(8,128)S(1)}, f32[32,32]{0,1:T(8,128)S(1)}, u32[]{:S(2)}, u32[]{:S(2)}) collective-permute-start(f32[32,32]{0,1:T(8,128)S(1)} %add.137), channel_id=1, source_target_pairs={{8,0},{9,1},{10,2},{11,3},{12,4},{13,5},{14,6},{15,7},{0,8},{1,9},... | collective-permute-start | bytes 12296 | tf_op jit(solution)/shard_map/ppermute | solution.py:24
  24.4 12.3 %collective-permute-start.4 = (f32[32,512]{1,0:T(8,128)S(1)}, f32[32,512]{1,0:T(8,128)S(1)}, u32[]{:S(2)}, u32[]{:S(2)}) collective-permute-start(f32[32,512]{1,0:T(8,128)S(1)} %fusion.45), channel_id=1, source_target_pairs={{1,0},{2,1},{3,2},{4,3},{5,4},{6,5},{7,6},{8,7},{9,8},{10,9},{11,1... | collective-permute-start | bytes 196616 | tf_op jit(solution)/shard_map/ppermute | solution.py:15
  25.7 14.7 %collective-permute-start.5 = (f32[32,512]{1,0:T(8,128)S(1)}, f32[32,512]{1,0:T(8,128)S(1)}, u32[]{:S(2)}, u32[]{:S(2)}) collective-permute-start(f32[32,512]{1,0:T(8,128)S(1)} %fusion.45), channel_id=1, source_target_pairs={{2,0},{3,1},{4,2},{5,3},{6,4},{7,5},{8,6},{9,7},{10,8},{11,9},{12,... | collective-permute-start | bytes 196616 | tf_op jit(solution)/shard_map/ppermute | solution.py:15
  29.4 11.0 %collective-permute-start.6 = (f32[32,512]{1,0:T(8,128)S(1)}, f32[32,512]{1,0:T(8,128)S(1)}, u32[]{:S(2)}, u32[]{:S(2)}) collective-permute-start(f32[32,512]{1,0:T(8,128)S(1)} %fusion.45), channel_id=1, source_target_pairs={{3,0},{4,1},{5,2},{6,3},{7,4},{8,5},{9,6},{10,7},{11,8},{12,9},{13... | collective-permute-start | bytes 196616 | tf_op jit(solution)/shard_map/ppermute | solution.py:15
  29.6 11.4 %collective-permute-start.7 = (f32[32,512]{1,0:T(8,128)S(1)}, f32[32,512]{1,0:T(8,128)S(1)}, u32[]{:S(2)}, u32[]{:S(2)}) collective-permute-start(f32[32,512]{1,0:T(8,128)S(1)} %fusion.45), channel_id=1, source_target_pairs={{4,0},{5,1},{6,2},{7,3},{8,4},{9,5},{10,6},{11,7},{12,8},{13,9},{1... | collective-permute-start | bytes 196616 | tf_op jit(solution)/shard_map/ppermute | solution.py:15
  30.1 13.4 %collective-permute-start.8 = (f32[32,512]{1,0:T(8,128)S(1)}, f32[32,512]{1,0:T(8,128)S(1)}, u32[]{:S(2)}, u32[]{:S(2)}) collective-permute-start(f32[32,512]{1,0:T(8,128)S(1)} %fusion.45), channel_id=1, source_target_pairs={{5,0},{6,1},{7,2},{8,3},{9,4},{10,5},{11,6},{12,7},{13,8},{14,9},{... | collective-permute-start | bytes 196616 | tf_op jit(solution)/shard_map/ppermute | solution.py:15
  36.7 7.7 %collective-permute-start.9 = (f32[32,512]{1,0:T(8,128)S(1)}, f32[32,512]{1,0:T(8,128)S(1)}, u32[]{:S(2)}, u32[]{:S(2)}) collective-permute-start(f32[32,512]{1,0:T(8,128)S(1)} %fusion.45), channel_id=1, source_target_pairs={{6,0},{7,1},{8,2},{9,3},{10,4},{11,5},{12,6},{13,7},{14,8},{15,9},... | collective-permute-start | bytes 196616 | tf_op jit(solution)/shard_map/ppermute | solution.py:15
  40.4 6.6 %collective-permute-start.10 = (f32[32,512]{1,0:T(8,128)S(1)}, f32[32,512]{1,0:T(8,128)S(1)}, u32[]{:S(2)}, u32[]{:S(2)}) collective-permute-start(f32[32,512]{1,0:T(8,128)S(1)} %fusion.45), channel_id=1, source_target_pairs={{7,0},{8,1},{9,2},{10,3},{11,4},{12,5},{13,6},{14,7},{15,8},{0,9},... | collective-permute-start | bytes 196616 | tf_op jit(solution)/shard_map/ppermute | solution.py:15
  40.5 7.3 %collective-permute-start.11 = (f32[32,512]{1,0:T(8,128)S(1)}, f32[32,512]{1,0:T(8,128)S(1)}, u32[]{:S(2)}, u32[]{:S(2)}) collective-permute-start(f32[32,512]{1,0:T(8,128)S(1)} %bitcast.185), channel_id=1, source_target_pairs={{15,0},{0,1},{1,2},{2,3},{3,4},{4,5},{5,6},{6,7},{7,8},{8,9},{9,10... | collective-permute-start | bytes 196616 | tf_op jit(solution)/shard_map/ppermute | solution.py:15
  41.0 9.3 %collective-permute-start.12 = (f32[32,512]{1,0:T(8,128)S(1)}, f32[32,512]{1,0:T(8,128)S(1)}, u32[]{:S(2)}, u32[]{:S(2)}) collective-permute-start(f32[32,512]{1,0:T(8,128)S(1)} %bitcast.183), channel_id=1, source_target_pairs={{14,0},{15,1},{0,2},{1,3},{2,4},{3,5},{4,6},{5,7},{6,8},{7,9},{8,1... | collective-permute-start | bytes 196616 | tf_op jit(solution)/shard_map/ppermute | solution.py:15
  43.5 15.1 %collective-permute-start.13 = (f32[32,512]{1,0:T(8,128)S(1)}, f32[32,512]{1,0:T(8,128)S(1)}, u32[]{:S(2)}, u32[]{:S(2)}) collective-permute-start(f32[32,512]{1,0:T(8,128)S(1)} %bitcast.181), channel_id=1, source_target_pairs={{13,0},{14,1},{15,2},{0,3},{1,4},{2,5},{3,6},{4,7},{5,8},{6,9},{7,... | collective-permute-start | bytes 196616 | tf_op jit(solution)/shard_map/ppermute | solution.py:15
  44.4 14.2 %collective-permute-start.14 = (f32[32,512]{1,0:T(8,128)S(1)}, f32[32,512]{1,0:T(8,128)S(1)}, u32[]{:S(2)}, u32[]{:S(2)}) collective-permute-start(f32[32,512]{1,0:T(8,128)S(1)} %bitcast.179), channel_id=1, source_target_pairs={{12,0},{13,1},{14,2},{15,3},{0,4},{1,5},{2,6},{3,7},{4,8},{5,9},{6... | collective-permute-start | bytes 196616 | tf_op jit(solution)/shard_map/ppermute | solution.py:15
  47.0 11.6 %collective-permute-start.15 = (f32[32,512]{1,0:T(8,128)S(1)}, f32[32,512]{1,0:T(8,128)S(1)}, u32[]{:S(2)}, u32[]{:S(2)}) collective-permute-start(f32[32,512]{1,0:T(8,128)S(1)} %bitcast.177), channel_id=1, source_target_pairs={{11,0},{12,1},{13,2},{14,3},{15,4},{0,5},{1,6},{2,7},{3,8},{4,9},{... | collective-permute-start | bytes 196616 | tf_op jit(solution)/shard_map/ppermute | solution.py:15
  47.8 10.9 %collective-permute-start.16 = (f32[32,512]{1,0:T(8,128)S(1)}, f32[32,512]{1,0:T(8,128)S(1)}, u32[]{:S(2)}, u32[]{:S(2)}) collective-permute-start(f32[32,512]{1,0:T(8,128)S(1)} %bitcast.175), channel_id=1, source_target_pairs={{10,0},{11,1},{12,2},{13,3},{14,4},{15,5},{0,6},{1,7},{2,8},{3,9},... | collective-permute-start | bytes 196616 | tf_op jit(solution)/shard_map/ppermute | solution.py:15
  50.3 8.4 %collective-permute-start.17 = (f32[32,512]{1,0:T(8,128)S(1)}, f32[32,512]{1,0:T(8,128)S(1)}, u32[]{:S(2)}, u32[]{:S(2)}) collective-permute-start(f32[32,512]{1,0:T(8,128)S(1)} %bitcast.174), channel_id=1, source_target_pairs={{9,0},{10,1},{11,2},{12,3},{13,4},{14,5},{15,6},{0,7},{1,8},{2,9},... | collective-permute-start | bytes 196616 | tf_op jit(solution)/shard_map/ppermute | solution.py:15
  69.3 4.6 %collective-permute-start.21 = (f32[32,32]{1,0:T(8,128)S(1)}, f32[32,32]{1,0:T(8,128)S(1)}, u32[]{:S(2)}, u32[]{:S(2)}) collective-permute-start(f32[32,32]{1,0:T(8,128)S(1)} %add.151), channel_id=1, source_target_pairs={{8,0},{9,1},{10,2},{11,3},{12,4},{13,5},{14,6},{15,7},{0,8},{1,9},... | collective-permute-start | bytes 12296 | tf_op jit(solution)/shard_map/ppermute | solution.py:24
  83.0 4.6 %collective-permute-start.25 = (f32[32,32]{0,1:T(8,128)S(1)}, f32[32,32]{0,1:T(8,128)S(1)}, u32[]{:S(2)}, u32[]{:S(2)}) collective-permute-start(f32[32,32]{0,1:T(8,128)S(1)} %add.155), channel_id=1, source_target_pairs={{8,0},{9,1},{10,2},{11,3},{12,4},{13,5},{14,6},{15,7},{0,8},{1,9},... | collective-permute-start | bytes 12296 | tf_op jit(solution)/shard_map/ppermute | solution.py:24
  94.8 13.1 %collective-permute-start.26 = (f32[32,512]{1,0:T(8,128)S(1)}, f32[32,512]{1,0:T(8,128)S(1)}, u32[]{:S(2)}, u32[]{:S(2)}) collective-permute-start(f32[32,512]{1,0:T(8,128)S(1)} %fusion.55), channel_id=1, source_target_pairs={{1,0},{2,1},{3,2},{4,3},{5,4},{6,5},{7,6},{8,7},{9,8},{10,9},{11,1... | collective-permute-start | bytes 196616 | tf_op jit(solution)/shard_map/ppermute | solution.py:15
  94.8 14.7 %collective-permute-start.27 = (f32[32,512]{1,0:T(8,128)S(1)}, f32[32,512]{1,0:T(8,128)S(1)}, u32[]{:S(2)}, u32[]{:S(2)}) collective-permute-start(f32[32,512]{1,0:T(8,128)S(1)} %fusion.55), channel_id=1, source_target_pairs={{2,0},{3,1},{4,2},{5,3},{6,4},{7,5},{8,6},{9,7},{10,8},{11,9},{12,... | collective-permute-start | bytes 196616 | tf_op jit(solution)/shard_map/ppermute | solution.py:15
  97.5 12.1 %collective-permute-start.28 = (f32[32,512]{1,0:T(8,128)S(1)}, f32[32,512]{1,0:T(8,128)S(1)}, u32[]{:S(2)}, u32[]{:S(2)}) collective-permute-start(f32[32,512]{1,0:T(8,128)S(1)} %fusion.55), channel_id=1, source_target_pairs={{3,0},{4,1},{5,2},{6,3},{7,4},{8,5},{9,6},{10,7},{11,8},{12,9},{13... | collective-permute-start | bytes 196616 | tf_op jit(solution)/shard_map/ppermute | solution.py:15
  97.5 13.4 %collective-permute-start.29 = (f32[32,512]{1,0:T(8,128)S(1)}, f32[32,512]{1,0:T(8,128)S(1)}, u32[]{:S(2)}, u32[]{:S(2)}) collective-permute-start(f32[32,512]{1,0:T(8,128)S(1)} %fusion.55), channel_id=1, source_target_pairs={{4,0},{5,1},{6,2},{7,3},{8,4},{9,5},{10,6},{11,7},{12,8},{13,9},{1... | collective-permute-start | bytes 196616 | tf_op jit(solution)/shard_map/ppermute | solution.py:15
  99.1 13.4 %collective-permute-start.30 = (f32[32,512]{1,0:T(8,128)S(1)}, f32[32,512]{1,0:T(8,128)S(1)}, u32[]{:S(2)}, u32[]{:S(2)}) collective-permute-start(f32[32,512]{1,0:T(8,128)S(1)} %fusion.55), channel_id=1, source_target_pairs={{5,0},{6,1},{7,2},{8,3},{9,4},{10,5},{11,6},{12,7},{13,8},{14,9},{... | collective-permute-start | bytes 196616 | tf_op jit(solution)/shard_map/ppermute | solution.py:15
  107.9 5.4 %collective-permute-start.31 = (f32[32,512]{1,0:T(8,128)S(1)}, f32[32,512]{1,0:T(8,128)S(1)}, u32[]{:S(2)}, u32[]{:S(2)}) collective-permute-start(f32[32,512]{1,0:T(8,128)S(1)} %fusion.55), channel_id=1, source_target_pairs={{6,0},{7,1},{8,2},{9,3},{10,4},{11,5},{12,6},{13,7},{14,8},{15,9},... | collective-permute-start | bytes 196616 | tf_op jit(solution)/shard_map/ppermute | solution.py:15
  109.5 6.5 %collective-permute-start.32 = (f32[32,512]{1,0:T(8,128)S(1)}, f32[32,512]{1,0:T(8,128)S(1)}, u32[]{:S(2)}, u32[]{:S(2)}) collective-permute-start(f32[32,512]{1,0:T(8,128)S(1)} %fusion.55), channel_id=1, source_target_pairs={{7,0},{8,1},{9,2},{10,3},{11,4},{12,5},{13,6},{14,7},{15,8},{0,9},... | collective-permute-start | bytes 196616 | tf_op jit(solution)/shard_map/ppermute | solution.py:15
  109.6 7.2 %collective-permute-start.33 = (f32[32,512]{1,0:T(8,128)S(1)}, f32[32,512]{1,0:T(8,128)S(1)}, u32[]{:S(2)}, u32[]{:S(2)}) collective-permute-start(f32[32,512]{1,0:T(8,128)S(1)} %bitcast.184), channel_id=1, source_target_pairs={{15,0},{0,1},{1,2},{2,3},{3,4},{4,5},{5,6},{6,7},{7,8},{8,9},{9,10... | collective-permute-start | bytes 196616 | tf_op jit(solution)/shard_map/ppermute | solution.py:15
  111.0 8.4 %collective-permute-start.34 = (f32[32,512]{1,0:T(8,128)S(1)}, f32[32,512]{1,0:T(8,128)S(1)}, u32[]{:S(2)}, u32[]{:S(2)}) collective-permute-start(f32[32,512]{1,0:T(8,128)S(1)} %bitcast.182), channel_id=1, source_target_pairs={{14,0},{15,1},{0,2},{1,3},{2,4},{3,5},{4,6},{5,7},{6,8},{7,9},{8,1... | collective-permute-start | bytes 196616 | tf_op jit(solution)/shard_map/ppermute | solution.py:15
  112.5 15.2 %collective-permute-start.35 = (f32[32,512]{1,0:T(8,128)S(1)}, f32[32,512]{1,0:T(8,128)S(1)}, u32[]{:S(2)}, u32[]{:S(2)}) collective-permute-start(f32[32,512]{1,0:T(8,128)S(1)} %bitcast.180), channel_id=1, source_target_pairs={{13,0},{14,1},{15,2},{0,3},{1,4},{2,5},{3,6},{4,7},{5,8},{6,9},{7,... | collective-permute-start | bytes 196616 | tf_op jit(solution)/shard_map/ppermute | solution.py:15
  113.3 14.4 %collective-permute-start.36 = (f32[32,512]{1,0:T(8,128)S(1)}, f32[32,512]{1,0:T(8,128)S(1)}, u32[]{:S(2)}, u32[]{:S(2)}) collective-permute-start(f32[32,512]{1,0:T(8,128)S(1)} %bitcast.178), channel_id=1, source_target_pairs={{12,0},{13,1},{14,2},{15,3},{0,4},{1,5},{2,6},{3,7},{4,8},{5,9},{6... | collective-permute-start | bytes 196616 | tf_op jit(solution)/shard_map/ppermute | solution.py:15
  116.0 11.7 %collective-permute-start.37 = (f32[32,512]{1,0:T(8,128)S(1)}, f32[32,512]{1,0:T(8,128)S(1)}, u32[]{:S(2)}, u32[]{:S(2)}) collective-permute-start(f32[32,512]{1,0:T(8,128)S(1)} %bitcast.176), channel_id=1, source_target_pairs={{11,0},{12,1},{13,2},{14,3},{15,4},{0,5},{1,6},{2,7},{3,8},{4,9},{... | collective-permute-start | bytes 196616 | tf_op jit(solution)/shard_map/ppermute | solution.py:15
  116.8 11.0 %collective-permute-start.38 = (f32[32,512]{1,0:T(8,128)S(1)}, f32[32,512]{1,0:T(8,128)S(1)}, u32[]{:S(2)}, u32[]{:S(2)}) collective-permute-start(f32[32,512]{1,0:T(8,128)S(1)} %bitcast.173), channel_id=1, source_target_pairs={{10,0},{11,1},{12,2},{13,3},{14,4},{15,5},{0,6},{1,7},{2,8},{3,9},... | collective-permute-start | bytes 196616 | tf_op jit(solution)/shard_map/ppermute | solution.py:15
  119.3 8.4 %collective-permute-start.39 = (f32[32,512]{1,0:T(8,128)S(1)}, f32[32,512]{1,0:T(8,128)S(1)}, u32[]{:S(2)}, u32[]{:S(2)}) collective-permute-start(f32[32,512]{1,0:T(8,128)S(1)} %bitcast.172), channel_id=1, source_target_pairs={{9,0},{10,1},{11,2},{12,3},{13,4},{14,5},{15,6},{0,7},{1,8},{2,9},... | collective-permute-start | bytes 196616 | tf_op jit(solution)/shard_map/ppermute | solution.py:15
  138.2 4.6 %collective-permute-start.43 = (f32[32,32]{1,0:T(8,128)S(1)}, f32[32,32]{1,0:T(8,128)S(1)}, u32[]{:S(2)}, u32[]{:S(2)}) collective-permute-start(f32[32,32]{1,0:T(8,128)S(1)} %add.167), channel_id=1, source_target_pairs={{8,0},{9,1},{10,2},{11,3},{12,4},{13,5},{14,6},{15,7},{0,8},{1,9},... | collective-permute-start | bytes 12296 | tf_op jit(solution)/shard_map/ppermute | solution.py:24
  (21 other events, 225.0 us)

commit v2 on v0

v2 whole, which is shorter than its diff:
```python
import functools

import jax
import jax.numpy as jnp
from jax import lax
from jax.experimental import pallas as pl
from jax.experimental.pallas import tpu as pltpu
from jax.sharding import PartitionSpec as P

REACH = 7
SCALE = 0.0078125
SIDE = 128

precise = lax.Precision.HIGHEST
roomy = pltpu.CompilerParams(vmem_limit_bytes=40 * 1024 * 1024)
in_vmem = pl.BlockSpec(memory_space=pltpu.VMEM)
in_smem = pl.BlockSpec(memory_space=pltpu.SMEM)


def struct(*shape):
    return jax.ShapeDtypeStruct(shape, jnp.float32)


def mm(left, right):
    return lax.dot_general(
        left, right, (((1,), (0,)), ((), ())), precision=precise, preferred_element_type=jnp.float32
    )


def mm_t(left, right):
    return lax.dot_general(
        left, right, (((1,), (1,)), ((), ())), precision=precise, preferred_element_type=jnp.float32
    )


def halves(block):
    high = block.astype(jnp.bfloat16)
    return high, (block - high.astype(jnp.float32)).astype(jnp.bfloat16)


def split_product(vectors, matrix, side):
    dims = (((1,), (side,)), ((), ()))
    dot = functools.partial(lax.dot_general, dimension_numbers=dims, preferred_element_type=jnp.float32)
    high, low = vectors
    matrix_high, matrix_low = halves(matrix)
    if low is None:
        return dot(high, matrix_high) + dot(high, matrix_low)
    rows = high.shape[0]
    both = dot(jnp.concatenate([high, low], axis=0), matrix_high)
    return both[:rows] + both[rows:] + dot(high, matrix_low)


def parts_of(block, exact):
    if exact:
        return block.astype(jnp.bfloat16), None
    return halves(block)


def factor(matrix):
    size = matrix.shape[0]
    step = 8
    strips = size // step
    lane = lax.broadcasted_iota(jnp.int32, (step, size), 1)
    rows = [lax.broadcasted_iota(jnp.int32, (step, size), 0) + step * s for s in range(strips)]
    columns = [
        [jnp.broadcast_to(matrix[step * s : step * s + step, j : j + 1], (step, size)) for s in range(strips)]
        for j in range(size)
    ]
    inverse = [jnp.where(lane == rows[s], 1.0, 0.0) for s in range(strips)]
    lower = [jnp.zeros((step, size), jnp.float32) for _ in range(strips)]
    for k in range(size):
        home, at = divmod(k, step)
        pivot = jnp.broadcast_to(columns[k][home][at : at + 1, :], (step, size))
        root = lax.rsqrt(pivot)
        root = root * (1.5 - 0.5 * (pivot * root) * root)
        scaled = [None] * strips
        for s in range(home, strips):
            scaled[s] = columns[k][s] * root
            if s == home:
                scaled[s] = jnp.where(rows[s] >= k, scaled[s], 0.0)
            lower[s] = jnp.where(lane == k, scaled[s], lower[s])
        for j in range(k + 1, size):
            place, inside = divmod(j, step)
            weight = jnp.broadcast_to(scaled[place][inside : inside + 1, :], (step, size))
            for s in range(place, strips):
                columns[j][s] = columns[j][s] - scaled[s] * weight
        done = jnp.broadcast_to(inverse[home][at : at + 1, :], (step, size)) * root
        for s in range(home, strips):
            if s == home:
                inverse[s] = jnp.where(rows[s] == k, done, inverse[s] - jnp.where(rows[s] > k, scaled[s], 0.0) * done)
            else:
                inverse[s] = inverse[s] - scaled[s] * done
    return jnp.concatenate(lower, axis=0), jnp.concatenate(inverse, axis=0)


def begin_kernel(probes_ref, diagonal_ref, message_ref):
    signs = (2 * probes_ref[...] - 1).astype(jnp.float32) * SCALE
    rows, order = signs.shape
    message_ref[:, :order] = signs
    message_ref[:, order : order + rows] = mm_t(signs, signs)
    square = lax.broadcasted_iota(jnp.int32, (SIDE, SIDE), 0) == lax.broadcasted_iota(jnp.int32, (SIDE, SIDE), 1)
    trace = jnp.zeros((1, SIDE), jnp.float32)
    for start in range(0, order, SIDE):
        tile = diagonal_ref[start : start + SIDE, start : start + SIDE]
        trace += jnp.sum(jnp.where(square, tile, 0.0) * (1.0 / order), axis=0, keepdims=True)
    trace = jnp.sum(trace, axis=1, keepdims=True)
    message_ref[:, order + rows :] = jnp.broadcast_to(trace, (rows, SIDE - rows))


def outgoing_kernel(exact, distance_ref, vectors_ref, forward_ref, own_ref, other_ref):
    order = forward_ref.shape[1]
    vectors = parts_of(vectors_ref[:, :order], exact)
    own_ref[...] = jnp.zeros_like(own_ref)
    other_ref[...] = jnp.zeros_like(other_ref)

    def step(e, _):
        product = split_product(vectors, forward_ref[e], 0)
        distance = distance_ref[e]
        half = distance >> 1

        @pl.when((distance & 1) == 0)
        def _():
            own_ref[half - 1] = product

        @pl.when((distance & 1) == 1)
        def _():
            other_ref[half] = product

        return 0

    lax.fori_loop(0, forward_ref.shape[0], step, 0)


def incoming_kernel(
    exact, distance_ref, vectors_ref, far_ref, middle_ref, odd_ref, forward_ref, diagonal_ref, trace_ref, image_ref, table
):
    order = forward_ref.shape[1]
    rows = vectors_ref.shape[0]
    table[0] = far_ref[:, :order]
    table[1] = middle_ref[:, :order]
    table[2] = far_ref[:, order : 2 * order]
    for j in range(4):
        table[3 + j] = odd_ref[j]
    vectors = vectors_ref[:, :order]
    trace = trace_ref[0:1, order + rows : order + rows + 1]
    line = lax.broadcasted_iota(jnp.int32, (order, order), 0) == lax.broadcasted_iota(jnp.int32, (order, order), 1)
    rest = diagonal_ref[...] - jnp.where(line, trace, 0.0)
    image_ref[...] = split_product(parts_of(vectors, exact), rest, 0)

    def step(e, _):
        distance = distance_ref[e]
        half = distance >> 1
        slot = jnp.where((distance & 1) == 0, half - 1, half + 3)
        image_ref[...] += split_product(parts_of(table[slot], exact), forward_ref[e], 1)
        return 0

    lax.fori_loop(0, forward_ref.shape[0], step, 0)


def first_kernel(devices, start_ref, image_ref, total_ref, sums_ref, message_ref):
    rows, order = image_ref.shape
    signs = start_ref[:, :order]
    shift = start_ref[0:1, order + rows : order + rows + 1] - sums_ref[0:1, rows : rows + 1] * (1.0 / devices)
    image = image_ref[...] + total_ref[...] + shift * signs
    message_ref[:, :order] = image
    both = mm_t(jnp.concatenate([signs, image], axis=0), image)
    message_ref[:, order : order + rows] = both[:rows]
    message_ref[:, order + rows : order + 2 * rows] = both[rows:]
    message_ref[:, order + 2 * rows :] = jnp.zeros((rows, SIDE - 2 * rows), jnp.float32)


def root_kernel(sums_ref, inverse_ref):
    rows = sums_ref.shape[0]
    inverse_ref[...] = factor(sums_ref[:, :rows])[1]


def coefficient_kernel(root_ref, sums_ref, out_ref):
    rows = root_ref.shape[0]
    root = root_ref[...]
    alpha = mm_t(mm(root, sums_ref[:, :rows]), root)
    gram = mm_t(mm(root, sums_ref[:, rows : 2 * rows]), root) - mm_t(alpha, alpha)
    beta, inverse = factor(gram)
    scaled = mm(inverse, root)
    back = mm(mm(inverse, alpha), root)
    link = lax.dot_general(
        beta, root, (((0,), (0,)), ((), ())), precision=precise, preferred_element_type=jnp.float32
    )
    out_ref[0] = scaled
    out_ref[1] = back
    out_ref[2] = link
    out_ref[3] = alpha
    out_ref[4] = beta


def second_kernel(
    devices, start_ref, message_ref, image_ref, total_ref, small_ref, sums_ref, basis_ref, result_ref, share_ref
):
    rows, order = image_ref.shape
    signs = start_ref[:, :order]
    first = message_ref[:, :order]
    mean = sums_ref[0:1, rows : rows + 1] * (1.0 / devices)
    shift = start_ref[0:1, order + rows : order + rows + 1] - mean
    image = image_ref[...] + total_ref[...] + shift * first
    scaled, back, link, alpha, beta = (small_ref[j] for j in range(5))
    basis = mm(scaled, first) - mm(back, signs)
    result = mm(scaled, image) - mm(back, first) - mm(link, signs)
    basis_ref[...] = basis
    result_ref[...] = result
    both = mm_t(jnp.concatenate([basis, result], axis=0), result)
    line = lax.broadcasted_iota(jnp.int32, (rows, rows), 0)
    lane = lax.broadcasted_iota(jnp.int32, (rows, rows), 1)
    part = 1.0 / devices
    share_ref[:, :rows] = both[:rows]
    share_ref[:, rows : 2 * rows] = both[rows:]
    share_ref[:, 2 * rows : 3 * rows] = (alpha + jnp.where(line == lane, mean, 0.0)) * part
    share_ref[:, 3 * rows :] = jnp.where(lane > line, mean, beta) * part


def last_kernel(share_ref, basis_ref, result_ref, next_ref, blocks_ref):
    rows = share_ref.shape[0]
    line = lax.broadcasted_iota(jnp.int32, (rows, rows), 0)
    lane = lax.broadcasted_iota(jnp.int32, (rows, rows), 1)
    alpha = share_ref[:, :rows]
    mean = share_ref[0:1, 4 * rows - 1 : 4 * rows]
    gram = share_ref[:, rows : 2 * rows] - mm_t(alpha, alpha)
    beta, inverse = factor(gram)
    next_ref[...] = mm(inverse, result_ref[...] - mm(alpha, basis_ref[...]))
    blocks_ref[0] = share_ref[:, 2 * rows : 3 * rows]
    blocks_ref[1] = jnp.where(lane > line, 0.0, share_ref[:, 3 * rows :])
    blocks_ref[2] = alpha + jnp.where(line == lane, mean, 0.0)
    blocks_ref[3] = beta


def call(kernel, out_shape, args, smem=0, scratch=(), flops=0):
    outs = in_vmem if not isinstance(out_shape, tuple) else (in_vmem,) * len(out_shape)
    return pl.pallas_call(
        kernel,
        out_shape=out_shape,
        in_specs=[in_smem] * smem + [in_vmem] * (len(args) - smem),
        out_specs=outs,
        scratch_shapes=list(scratch),
        compiler_params=roomy,
        cost_estimate=pl.CostEstimate(flops=flops, bytes_accessed=4 * sum(a.size for a in args), transcendentals=0),
    )(*args)


def body(probes, diagonal, forward_tiles, tile_columns):
    forward = forward_tiles[0]
    rows, order = probes.shape
    devices = lax.axis_size("col")
    position = lax.axis_index("col")
    core = position & 1
    distance = (tile_columns[0] - position) % devices

    def arriving(block, hops):
        return lax.ppermute(block, "col", [((i - hops) % devices, i) for i in range(devices)])

    def swapped(block, bits=1):
        return lax.ppermute(block, "col", [(i ^ bits, i) for i in range(devices)])

    def spread(message):
        block, sums = message[:, :order], message[:, order:]
        farthest = arriving(message, -8)
        middle = arriving(message, -4)
        sums = sums + farthest[:, order:]
        far = arriving(jnp.concatenate([block, middle[:, :order], sums], axis=1), -2)
        sums = sums + far[:, 2 * order :]
        near, third = far[:, :order], far[:, order : 2 * order]
        ahead = [block, near, middle[:, :order], third, farthest[:, :order]]
        odd = swapped(jnp.stack([jnp.where(core == 0, ahead[j + 1], ahead[j]) for j in range(4)]))
        sums = sums + arriving(sums, -4)
        hops = 16
        while hops < devices:
            sums = sums + arriving(sums, -hops)
            hops *= 2
        return far, middle, odd, sums + swapped(sums)

    def gathered(own, other):
        other = swapped(other)
        ahead = [jnp.where(core == 0, 0.0, other[0])]
        for j in range(1, 4):
            ahead.append(own[j - 1] + jnp.where(core == 0, other[j - 1], other[j]))
        ahead.append(jnp.where(core == 0, other[3], 0.0))
        near = arriving(jnp.stack([ahead[1], ahead[3]]), 2)
        farthest = arriving(ahead[4], 8)
        middle = arriving(ahead[2] + near[1], 4)
        return ahead[0] + near[0] + middle + farthest

    def products(message, exact):
        return call(
            functools.partial(outgoing_kernel, exact),
            (struct(3, rows, order), struct(4, rows, order)),
            (distance, message, forward),
            smem=1,
            flops=2 * rows * forward.size * 3,
        )

    def images(message, near, exact, start):
        far, middle, odd = near
        return call(
            functools.partial(incoming_kernel, exact),
            struct(rows, order),
            (distance, message, far, middle, odd, forward, diagonal, start),
            smem=1,
            scratch=(pltpu.VMEM((REACH, rows, order), jnp.float32),),
            flops=2 * rows * forward.size * 3,
        )

    start = call(begin_kernel, struct(rows, order + SIDE), (probes, diagonal))
    far, middle, odd, start_sums = spread(start)
    own, other = products(start, True)
    image = images(start, (far, middle, odd), True, start)
    total = gathered(own, other)
    message = call(functools.partial(first_kernel, devices), struct(rows, order + SIDE), (start, image, total, start_sums))

    root = call(root_kernel, struct(rows, rows), (start_sums,))
    far, middle, odd, sums = spread(message)
    own, other = products(message, False)
    image = images(message, (far, middle, odd), False, start)
    total = gathered(own, other)
    small = call(coefficient_kernel, struct(5, rows, rows), (root, sums))
    basis, result, share = call(
        functools.partial(second_kernel, devices),
        (struct(rows, order), struct(rows, order), struct(rows, SIDE)),
        (start, message, image, total, small, start_sums),
    )
    bits = 1
    while bits < devices:
        if bits >= 4 and 4 * bits <= devices:
            one, two, three = (swapped(share, bits * j) for j in (1, 2, 3))
            share = (share + one) + (two + three)
            bits *= 4
        else:
            share = share + swapped(share, bits)
            bits *= 2
    return call(last_kernel, (struct(rows, order), struct(4, rows, rows)), (share, basis, result))


def solution(mesh):
    placed = (
        P(None, ("groups", "col")),
        P(("groups", "col"), None),
        P(("groups", "col"), None, None, None),
        P(("groups", "col"), None),
    )
    return jax.shard_map(
        body,
        mesh=mesh,
        in_specs=placed,
        out_specs=(P(None, ("groups", "col")), P("groups", None, None)),
        check_vma=False,
    )
```

time: 390 us -> 93.4 us (0.24)
  blocking collectives: 299 us -> 0 us
  waiting for transfers between devices: 1.23 us -> 42.2 us
  matrix products: 30.9 us -> 0 us
  other arithmetic: 20.7 us -> 1.01 us
  Pallas kernels: 0 us -> 15.7 us
  starting transfers between devices: 35.6 us -> 26.1 us
  local copies, waits for them, and re-layouts: 1.05 us -> 7.05 us
    psum x5 -> x0, blocking collectives: 299 us -> none  [the longest x2 120 us: project(): lax.psum(jnp.einsum('pi,qi->pq', image, basis, precision=precise), 'col')]
    ppermute x28 -> x25, waiting for transfers between devices: 1.23 us -> 42.2 us  [the longest x14 31.4 us: arriving(): lax.ppermute(block, 'col', [((i - hops) % devices, i) for i in range(devi...]
    dot_general x18 -> x0, matrix products: 28.6 us -> none  [the longest x2 11.5 us: apply_kernel(): outgoing = jnp.einsum('pi,eij->epj', vectors, forward, precision=precise)]
    another operation x16 -> x6, other arithmetic: 20.7 us -> 0.11 us  [the longest x4 0.09 us: spread(): jnp.stack([jnp.where(core == 0, ahead[j + 1], ahead[j]) for j in range(4)])]
    pallas_call x0 -> x10, Pallas kernels: none -> 15.7 us  [call(): pl.pallas_call(kernel, out_shape=out_shape, in_specs=[in_smem] * smem + [...]
    ppermute x28 -> x25, starting transfers between devices: 35.6 us -> 26.1 us  [the longest x14 20.4 us: arriving(): lax.ppermute(block, 'col', [((i - hops) % devices, i) for i in range(devi...]
    unnamed x38 -> x12, local copies, waits for them, and re-layouts: 0.19 us -> 7.03 us
  transfers between devices with their start and end apart: 28 -> 25, of which waited for: 1 -> 16; matrix products, arithmetic and copies ran while one was open for 7% -> 1% of each run, Pallas kernels for 0% -> 7%
where the time goes in v2:
time: 93.4 us; the launch traced here: 93.1 us
  waiting for transfers between devices  42.2 us (45%)
  starting transfers between devices  26.1 us (28%)
  Pallas kernels  15.7 us (17%)
  local copies, waits for them, and re-layouts  7.05 us (8%)
  other arithmetic  1.01 us (1%)
  between operations  0.99 us (1%)
    ppermute x14, waiting for transfers between devices, arriving(): lax.ppermute(block, 'col', [((i - hops) % devices, i) for i in range(devi...  31.4 us
    ppermute x14, starting transfers between devices, arriving(): lax.ppermute(block, 'col', [((i - hops) % devices, i) for i in range(devi...  20.4 us
    pallas_call x10, Pallas kernels, call(): pl.pallas_call(kernel, out_shape=out_shape, in_specs=[in_smem] * smem + [...  15.7 us
    ppermute x11, waiting for transfers between devices, swapped(): return lax.ppermute(block, 'col', [(i ^ bits, i) for i in range(devices)])  10.8 us
    unnamed x12, local copies, waits for them, and re-layouts  7.03 us
    ppermute x11, starting transfers between devices, swapped(): return lax.ppermute(block, 'col', [(i ^ bits, i) for i in range(devices)])  5.68 us
  transfers between devices with their start and end apart: 25, of which 16 were waited for; matrix products, arithmetic and copies ran while one was open for 1% of the time, Pallas kernels for 7%

profile of v2, /device:TPU:0, one launch (start us, length us, event | category | flops | bytes accessed | tf_op | source)
XLA Modules:
  0.0 93.1 jit_solution(10498324355834017533)
XLA Ops:
  0.6 1.2 %copy-done.3 = f32[512,512]{1,0:T(8,128)S(1)} copy-done((f32[512,512]{1,0:T(8,128)S(1)}, f32[512,512]{1,0:T(8,128)}, u32[]{:S(2)}) %copy-start.3) | copy-done | bytes 1048600
  2.9 4.1 %collective-permute-start.1 = (f32[32,640]{1,0:T(8,128)S(1)}, f32[32,640]{1,0:T(8,128)S(1)}, u32[]{:S(2)}, u32[]{:S(2)}) collective-permute-start(f32[32,640]{1,0:T(8,128)S(1)} %shard_map.59.vectors_ref.trace_ref.start_ref), channel_id=1, source_target_pairs={{8,0},{9,1},{10,2},{11,3},{12,4},{13,5},{14,6},{15,7},{0,8},{1,9},... | collective-permute-start | bytes 245768 | tf_op jit(solution)/shard_map/ppermute | solution.py:256
  7.0 1.3 %collective-permute-start = (f32[32,640]{1,0:T(8,128)S(1)}, f32[32,640]{1,0:T(8,128)S(1)}, u32[]{:S(2)}, u32[]{:S(2)}) collective-permute-start(f32[32,640]{1,0:T(8,128)S(1)} %shard_map.59.vectors_ref.trace_ref.start_ref), channel_id=1, source_target_pairs={{4,0},{5,1},{6,2},{7,3},{8,4},{9,5},{10,6},{11,7},{12,8},{13,9},{1... | collective-permute-start | bytes 245768 | tf_op jit(solution)/shard_map/ppermute | solution.py:256
  8.4 3.1 %collective-permute-done.1 = f32[32,640]{1,0:T(8,128)S(1)} collective-permute-done((f32[32,640]{1,0:T(8,128)S(1)}, f32[32,640]{1,0:T(8,128)S(1)}, u32[]{:S(2)}, u32[]{:S(2)}) %collective-permute-start.1) | collective-permute-done | bytes 81952 | tf_op jit(solution)/shard_map/ppermute | solution.py:256
  11.6 5.9 %collective-permute-start.2 = (f32[32,1152]{1,0:T(8,128)S(1)}, f32[32,1152]{1,0:T(8,128)S(1)}, u32[]{:S(2)}, u32[]{:S(2)}) collective-permute-start(f32[32,1152]{1,0:T(8,128)S(1)} %pad_maximum_fusion.2), channel_id=1, source_target_pairs={{2,0},{3,1},{4,2},{5,3},{6,4},{7,5},{8,6},{9,7},{10,8},{11,9},{12,... | collective-permute-start | bytes 442376 | tf_op jit(solution)/shard_map/ppermute | solution.py:256
  18.2 2.5 %copy-done = f32[1,5,512,512]{3,2,1,0:T(8,128)S(1)} copy-done((f32[1,5,512,512]{3,2,1,0:T(8,128)S(1)}, f32[1,5,512,512]{3,2,1,0:T(8,128)}, u32[]{:S(2)}) %copy-start) | copy-done | bytes 5242904
  20.7 2.2 %shard_map.61 = (f32[3,32,512]{2,1,0:T(8,128)S(1)}, f32[4,32,512]{2,1,0:T(8,128)S(1)}) custom-call(s32[5]{0:T(128)S(1)} %and_select_fusion.distance_ref, f32[32,640]{1,0:T(8,128)S(1)} %shard_map.59.vectors_ref.trace_ref.start_ref, f32[5,512,512]{2,1,0:T(8,128)S(1)} %bitcast.39), custom_call_target="tpu_custom_call" | custom-call | flops 251658240 | bytes 5324820 | tf_op jit(solution)/shard_map/pallas_call | solution.py:236
  23.0 1.4 %collective-permute-done.4 = f32[4,32,512]{2,1,0:T(8,128)S(1)} collective-permute-done((f32[4,32,512]{2,1,0:T(8,128)S(1)}, f32[4,32,512]{2,1,0:T(8,128)S(1)}, u32[]{:S(2)}, u32[]{:S(2)}) %collective-permute-start.4) | collective-permute-done | bytes 262176 | tf_op jit(solution)/shard_map/ppermute | solution.py:259
  24.5 2.1 %collective-permute-start.5 = (f32[2,32,512]{2,1,0:T(8,128)S(1)}, f32[2,32,512]{2,1,0:T(8,128)S(1)}, u32[]{:S(2)}, u32[]{:S(2)}) collective-permute-start(f32[2,32,512]{2,1,0:T(8,128)S(1)} %pad_maximum_fusion.4), channel_id=1, source_target_pairs={{14,0},{15,1},{0,2},{1,3},{2,4},{3,5},{4,6},{5,7},{6,8},{7,9},{8,1... | collective-permute-start | bytes 393224 | tf_op jit(solution)/shard_map/ppermute | solution.py:256
  26.6 6.2 %collective-permute-done.5 = f32[2,32,512]{2,1,0:T(8,128)S(1)} collective-permute-done((f32[2,32,512]{2,1,0:T(8,128)S(1)}, f32[2,32,512]{2,1,0:T(8,128)S(1)}, u32[]{:S(2)}, u32[]{:S(2)}) %collective-permute-start.5) | collective-permute-done | bytes 131104 | tf_op jit(solution)/shard_map/ppermute | solution.py:256
  33.6 1.0 %collective-permute-done.9 = f32[32,128]{1,0:T(8,128)S(1)} collective-permute-done((f32[32,128]{1,0:T(8,128)S(1)}, f32[32,128]{1,0:T(8,128)S(1)}, u32[]{:S(2)}, u32[]{:S(2)}) %collective-permute-start.9) | collective-permute-done | bytes 16416 | tf_op jit(solution)/shard_map/ppermute | solution.py:259
  34.6 4.3 %collective-permute-done.6 = f32[32,512]{1,0:T(8,128)S(1)} collective-permute-done((f32[32,512]{1,0:T(8,128)S(1)}, f32[32,512]{1,0:T(8,128)S(1)}, u32[]{:S(2)}, u32[]{:S(2)}) %collective-permute-start.6) | collective-permute-done | bytes 65568 | tf_op jit(solution)/shard_map/ppermute | solution.py:256
  38.9 1.1 %collective-permute-done.7 = f32[32,512]{1,0:T(8,128)S(1)} collective-permute-done((f32[32,512]{1,0:T(8,128)S(1)}, f32[32,512]{1,0:T(8,128)S(1)}, u32[]{:S(2)}, u32[]{:S(2)}) %collective-permute-start.7) | collective-permute-done | bytes 65568 | tf_op jit(solution)/shard_map/ppermute | solution.py:256
  40.1 2.5 %copy-done.1 = f32[1,5,512,512]{3,2,1,0:T(8,128)S(1)} copy-done((f32[1,5,512,512]{3,2,1,0:T(8,128)S(1)}, f32[1,5,512,512]{3,2,1,0:T(8,128)}, u32[]{:S(2)}) %copy-start.1) | copy-done | bytes 5242904
  42.6 3.0 %shard_map.60.image_ref = f32[32,512]{1,0:T(8,128)S(1)} custom-call(s32[5]{0:T(128)S(1)} %and_select_fusion.distance_ref, f32[32,640]{1,0:T(8,128)S(1)} %shard_map.59.vectors_ref.trace_ref.start_ref, f32[32,1152]{1,0:T(8,128)S(1)} %collective-permute-done.2.far_ref, f32[32,640]{1,0:T(8,128)S(1)} %collective-permute-done.middle_ref, ...), custom_call_target="tpu_custom_call" | custom-call | flops 251658240 | bytes 6946836 | tf_op jit(solution)/shard_map/pallas_call | solution.py:236
  46.1 2.5 %collective-permute-start.10 = (f32[32,640]{1,0:T(8,128)S(1)}, f32[32,640]{1,0:T(8,128)S(1)}, u32[]{:S(2)}, u32[]{:S(2)}) collective-permute-start(f32[32,640]{1,0:T(8,128)S(1)} %shard_map.62.vectors_ref.message_ref), channel_id=1, source_target_pairs={{4,0},{5,1},{6,2},{7,3},{8,4},{9,5},{10,6},{11,7},{12,8},{13,9},{1... | collective-permute-start | bytes 245768 | tf_op jit(solution)/shard_map/ppermute | solution.py:256
  48.5 4.0 %collective-permute-done.11 = f32[32,640]{1,0:T(8,128)S(1)} collective-permute-done((f32[32,640]{1,0:T(8,128)S(1)}, f32[32,640]{1,0:T(8,128)S(1)}, u32[]{:S(2)}, u32[]{:S(2)}) %collective-permute-start.11) | collective-permute-done | bytes 81952 | tf_op jit(solution)/shard_map/ppermute | solution.py:256
  53.1 2.2 %shard_map.64 = (f32[3,32,512]{2,1,0:T(8,128)S(1)}, f32[4,32,512]{2,1,0:T(8,128)S(1)}) custom-call(s32[5]{0:T(128)S(1)} %and_select_fusion.distance_ref, f32[32,640]{1,0:T(8,128)S(1)} %shard_map.62.vectors_ref.message_ref, f32[5,512,512]{2,1,0:T(8,128)S(1)} %bitcast.41), custom_call_target="tpu_custom_call" | custom-call | flops 251658240 | bytes 5324820 | tf_op jit(solution)/shard_map/pallas_call | solution.py:236
  55.2 2.6 %collective-permute-done.12.far_ref = f32[32,1152]{1,0:T(8,128)S(1)} collective-permute-done((f32[32,1152]{1,0:T(8,128)S(1)}, f32[32,1152]{1,0:T(8,128)S(1)}, u32[]{:S(2)}, u32[]{:S(2)}) %collective-permute-start.12) | collective-permute-done | bytes 147488 | tf_op jit(solution)/shard_map/ppermute | solution.py:256
  57.8 2.4 %collective-permute-start.18 = (f32[32,128]{1,0:T(8,128)S(1)}, f32[32,128]{1,0:T(8,128)S(1)}, u32[]{:S(2)}, u32[]{:S(2)}) collective-permute-start(f32[32,128]{1,0:T(8,128)S(1)} %slice_add_fusion.4), channel_id=1, source_target_pairs={{4,0},{5,1},{6,2},{7,3},{8,4},{9,5},{10,6},{11,7},{12,8},{13,9},{1... | collective-permute-start | bytes 49160 | tf_op jit(solution)/shard_map/ppermute | solution.py:256
  60.2 1.3 %collective-permute-start.15 = (f32[2,32,512]{2,1,0:T(8,128)S(1)}, f32[2,32,512]{2,1,0:T(8,128)S(1)}, u32[]{:S(2)}, u32[]{:S(2)}) collective-permute-start(f32[2,32,512]{2,1,0:T(8,128)S(1)} %pad_maximum_fusion.5), channel_id=1, source_target_pairs={{14,0},{15,1},{0,2},{1,3},{2,4},{3,5},{4,6},{5,7},{6,8},{7,9},{8,1... | collective-permute-start | bytes 393224 | tf_op jit(solution)/shard_map/ppermute | solution.py:256
  61.6 7.1 %collective-permute-done.15 = f32[2,32,512]{2,1,0:T(8,128)S(1)} collective-permute-done((f32[2,32,512]{2,1,0:T(8,128)S(1)}, f32[2,32,512]{2,1,0:T(8,128)S(1)}, u32[]{:S(2)}, u32[]{:S(2)}) %collective-permute-start.15) | collective-permute-done | bytes 131104 | tf_op jit(solution)/shard_map/ppermute | solution.py:256
  70.5 1.5 %shard_map.66.small_ref = f32[5,32,32]{2,1,0:T(8,128)S(1)} custom-call(f32[32,32]{1,0:T(8,128)S(1)} %shard_map.65.root_ref, f32[32,128]{1,0:T(8,128)S(1)} %add.131.sums_ref), custom_call_target="tpu_custom_call" | custom-call | bytes 20480 | tf_op jit(solution)/shard_map/pallas_call | solution.py:236
  72.0 2.8 %collective-permute-done.16 = f32[32,512]{1,0:T(8,128)S(1)} collective-permute-done((f32[32,512]{1,0:T(8,128)S(1)}, f32[32,512]{1,0:T(8,128)S(1)}, u32[]{:S(2)}, u32[]{:S(2)}) %collective-permute-start.16) | collective-permute-done | bytes 65568 | tf_op jit(solution)/shard_map/ppermute | solution.py:256
  74.9 3.1 %shard_map.63.image_ref = f32[32,512]{1,0:T(8,128)S(1)} custom-call(s32[5]{0:T(128)S(1)} %and_select_fusion.distance_ref, f32[32,640]{1,0:T(8,128)S(1)} %shard_map.62.vectors_ref.message_ref, f32[32,1152]{1,0:T(8,128)S(1)} %collective-permute-done.12.far_ref, f32[32,640]{1,0:T(8,128)S(1)} %collective-permute-done.10.middle_ref, ...), custom_call_target="tpu_custom_call" | custom-call | flops 251658240 | bytes 6946836 | tf_op jit(solution)/shard_map/pallas_call | solution.py:236
  78.8 1.2 %collective-permute-done.20 = f32[32,128]{1,0:T(8,128)S(1)} collective-permute-done((f32[32,128]{1,0:T(8,128)S(1)}, f32[32,128]{1,0:T(8,128)S(1)}, u32[]{:S(2)}, u32[]{:S(2)}) %collective-permute-start.20) | collective-permute-done | bytes 16416 | tf_op jit(solution)/shard_map/ppermute | solution.py:259
  80.0 3.7 %collective-permute-done.21 = f32[32,128]{1,0:T(8,128)S(1)} collective-permute-done((f32[32,128]{1,0:T(8,128)S(1)}, f32[32,128]{1,0:T(8,128)S(1)}, u32[]{:S(2)}, u32[]{:S(2)}) %collective-permute-start.21) | collective-permute-done | bytes 16416 | tf_op jit(solution)/shard_map/ppermute | solution.py:259
  83.7 2.9 %collective-permute-start.24 = (f32[32,128]{1,0:T(8,128)S(1)}, f32[32,128]{1,0:T(8,128)S(1)}, u32[]{:S(2)}, u32[]{:S(2)}) collective-permute-start(f32[32,128]{1,0:T(8,128)S(1)} %add.133), channel_id=1, source_target_pairs={{12,0},{13,1},{14,2},{15,3},{8,4},{9,5},{10,6},{11,7},{4,8},{5,9},... | collective-permute-start | bytes 49160 | tf_op jit(solution)/shard_map/ppermute | solution.py:259
  86.6 1.5 %collective-permute-start.22 = (f32[32,128]{1,0:T(8,128)S(1)}, f32[32,128]{1,0:T(8,128)S(1)}, u32[]{:S(2)}, u32[]{:S(2)}) collective-permute-start(f32[32,128]{1,0:T(8,128)S(1)} %add.133), channel_id=1, source_target_pairs={{4,0},{5,1},{6,2},{7,3},{0,4},{1,5},{2,6},{3,7},{12,8},{13,9},{14,... | collective-permute-start | bytes 49160 | tf_op jit(solution)/shard_map/ppermute | solution.py:259
  88.1 1.1 %collective-permute-done.24 = f32[32,128]{1,0:T(8,128)S(1)} collective-permute-done((f32[32,128]{1,0:T(8,128)S(1)}, f32[32,128]{1,0:T(8,128)S(1)}, u32[]{:S(2)}, u32[]{:S(2)}) %collective-permute-start.24) | collective-permute-done | bytes 16416 | tf_op jit(solution)/shard_map/ppermute | solution.py:259
  89.2 2.0 %collective-permute-done.23 = f32[32,128]{1,0:T(8,128)S(1)} collective-permute-done((f32[32,128]{1,0:T(8,128)S(1)}, f32[32,128]{1,0:T(8,128)S(1)}, u32[]{:S(2)}, u32[]{:S(2)}) %collective-permute-start.23) | collective-permute-done | bytes 16416 | tf_op jit(solution)/shard_map/ppermute | solution.py:259
  91.3 1.8 %shard_map.68 = (f32[32,512]{1,0:T(8,128)}, f32[4,32,32]{2,1,0:T(8,128)}) custom-call(f32[32,128]{1,0:T(8,128)S(1)} %add_add_fusion.share_ref, f32[32,512]{1,0:T(8,128)S(1)} %get-tuple-element.14.basis_ref, f32[32,512]{1,0:T(8,128)S(1)} %get-tuple-element.15.result_ref), custom_call_target="tpu_custom_call" | custom-call | bytes 147456 | tf_op jit(solution)/shard_map/pallas_call | solution.py:236
  (70 shorter events, 6.5 us)
Async XLA Ops:
  0.6 1.2 %copy-start.3 = (f32[512,512]{1,0:T(8,128)S(1)}, f32[512,512]{1,0:T(8,128)}, u32[]{:S(2)}) copy-start(f32[512,512]{1,0:T(8,128)} %diagonal_ref.5) | copy-start | bytes 3145732
  1.9 0.8 copy-start.5
  2.7 37.4 %copy-start.4 = (f32[512,512]{1,0:T(8,128)S(1)}, f32[512,512]{1,0:T(8,128)}, u32[]{:S(2)}) copy-start(f32[512,512]{1,0:T(8,128)} %diagonal_ref.5) | copy-start | bytes 3145732
  2.9 8.5 %collective-permute-start.1 = (f32[32,640]{1,0:T(8,128)S(1)}, f32[32,640]{1,0:T(8,128)S(1)}, u32[]{:S(2)}, u32[]{:S(2)}) collective-permute-start(f32[32,640]{1,0:T(8,128)S(1)} %shard_map.59.vectors_ref.trace_ref.start_ref), channel_id=1, source_target_pairs={{8,0},{9,1},{10,2},{11,3},{12,4},{13,5},{14,6},{15,7},{0,8},{1,9},... | collective-permute-start | bytes 245768 | tf_op jit(solution)/shard_map/ppermute | solution.py:256
  7.0 4.6 %collective-permute-start = (f32[32,640]{1,0:T(8,128)S(1)}, f32[32,640]{1,0:T(8,128)S(1)}, u32[]{:S(2)}, u32[]{:S(2)}) collective-permute-start(f32[32,640]{1,0:T(8,128)S(1)} %shard_map.59.vectors_ref.trace_ref.start_ref), channel_id=1, source_target_pairs={{4,0},{5,1},{6,2},{7,3},{8,4},{9,5},{10,6},{11,7},{12,8},{13,9},{1... | collective-permute-start | bytes 245768 | tf_op jit(solution)/shard_map/ppermute | solution.py:256
  11.6 11.3 %collective-permute-start.2 = (f32[32,1152]{1,0:T(8,128)S(1)}, f32[32,1152]{1,0:T(8,128)S(1)}, u32[]{:S(2)}, u32[]{:S(2)}) collective-permute-start(f32[32,1152]{1,0:T(8,128)S(1)} %pad_maximum_fusion.2), channel_id=1, source_target_pairs={{2,0},{3,1},{4,2},{5,3},{6,4},{7,5},{8,6},{9,7},{10,8},{11,9},{12,... | collective-permute-start | bytes 442376 | tf_op jit(solution)/shard_map/ppermute | solution.py:256
  18.2 2.5 %copy-start = (f32[1,5,512,512]{3,2,1,0:T(8,128)S(1)}, f32[1,5,512,512]{3,2,1,0:T(8,128)}, u32[]{:S(2)}) copy-start(f32[1,5,512,512]{3,2,1,0:T(8,128)} %param.6) | copy-start | bytes 15728644
  22.9 1.5 %collective-permute-start.4 = (f32[4,32,512]{2,1,0:T(8,128)S(1)}, f32[4,32,512]{2,1,0:T(8,128)S(1)}, u32[]{:S(2)}, u32[]{:S(2)}) collective-permute-start(f32[4,32,512]{2,1,0:T(8,128)S(1)} %get-tuple-element.9), channel_id=1, source_target_pairs={{1,0},{0,1},{3,2},{2,3},{5,4},{4,5},{7,6},{6,7},{9,8},{8,9},{11,10... | collective-permute-start | bytes 786440 | tf_op jit(solution)/shard_map/ppermute | solution.py:259
  22.9 10.1 %collective-permute-start.8 = (f32[32,128]{1,0:T(8,128)S(1)}, f32[32,128]{1,0:T(8,128)S(1)}, u32[]{:S(2)}, u32[]{:S(2)}) collective-permute-start(f32[32,128]{1,0:T(8,128)S(1)} %slice_add_fusion.6), channel_id=1, source_target_pairs={{4,0},{5,1},{6,2},{7,3},{8,4},{9,5},{10,6},{11,7},{12,8},{13,9},{1... | collective-permute-start | bytes 49160 | tf_op jit(solution)/shard_map/ppermute | solution.py:256
  24.5 8.3 %collective-permute-start.5 = (f32[2,32,512]{2,1,0:T(8,128)S(1)}, f32[2,32,512]{2,1,0:T(8,128)S(1)}, u32[]{:S(2)}, u32[]{:S(2)}) collective-permute-start(f32[2,32,512]{2,1,0:T(8,128)S(1)} %pad_maximum_fusion.4), channel_id=1, source_target_pairs={{14,0},{15,1},{0,2},{1,3},{2,4},{3,5},{4,6},{5,7},{6,8},{7,9},{8,1... | collective-permute-start | bytes 393224 | tf_op jit(solution)/shard_map/ppermute | solution.py:256
  32.8 6.1 %collective-permute-start.6 = (f32[32,512]{1,0:T(8,128)S(1)}, f32[32,512]{1,0:T(8,128)S(1)}, u32[]{:S(2)}, u32[]{:S(2)}) collective-permute-start(f32[32,512]{1,0:T(8,128)S(1)} %get-tuple-element.22), channel_id=1, source_target_pairs={{12,0},{13,1},{14,2},{15,3},{0,4},{1,5},{2,6},{3,7},{4,8},{5,9},{6... | collective-permute-start | bytes 196616 | tf_op jit(solution)/shard_map/ppermute | solution.py:256
  32.9 7.2 %collective-permute-start.7 = (f32[32,512]{1,0:T(8,128)S(1)}, f32[32,512]{1,0:T(8,128)S(1)}, u32[]{:S(2)}, u32[]{:S(2)}) collective-permute-start(f32[32,512]{1,0:T(8,128)S(1)} %get-tuple-element.23), channel_id=1, source_target_pairs={{8,0},{9,1},{10,2},{11,3},{12,4},{13,5},{14,6},{15,7},{0,8},{1,9},... | collective-permute-start | bytes 196616 | tf_op jit(solution)/shard_map/ppermute | solution.py:256
  33.0 7.1 %collective-permute-start.3 = (f32[4,32,512]{2,1,0:T(8,128)S(1)}, f32[4,32,512]{2,1,0:T(8,128)S(1)}, u32[]{:S(2)}, u32[]{:S(2)}) collective-permute-start(f32[4,32,512]{2,1,0:T(8,128)S(1)} %pad_maximum_fusion), channel_id=1, source_target_pairs={{1,0},{0,1},{3,2},{2,3},{5,4},{4,5},{7,6},{6,7},{9,8},{8,9},{11,10... | collective-permute-start | bytes 786440 | tf_op jit(solution)/shard_map/ppermute | solution.py:259
  33.1 1.5 %collective-permute-start.9 = (f32[32,128]{1,0:T(8,128)S(1)}, f32[32,128]{1,0:T(8,128)S(1)}, u32[]{:S(2)}, u32[]{:S(2)}) collective-permute-start(f32[32,128]{1,0:T(8,128)S(1)} %add.117), channel_id=1, source_target_pairs={{1,0},{0,1},{3,2},{2,3},{5,4},{4,5},{7,6},{6,7},{9,8},{8,9},{11,10... | collective-permute-start | bytes 49160 | tf_op jit(solution)/shard_map/ppermute | solution.py:259
  40.1 2.5 %copy-start.1 = (f32[1,5,512,512]{3,2,1,0:T(8,128)S(1)}, f32[1,5,512,512]{3,2,1,0:T(8,128)}, u32[]{:S(2)}) copy-start(f32[1,5,512,512]{3,2,1,0:T(8,128)} %param.6) | copy-start | bytes 15728644
  42.6 10.4 %copy-start.2 = (f32[1,5,512,512]{3,2,1,0:T(8,128)S(1)}, f32[1,5,512,512]{3,2,1,0:T(8,128)}, u32[]{:S(2)}) copy-start(f32[1,5,512,512]{3,2,1,0:T(8,128)} %param.6) | copy-start | bytes 15728644
  46.0 6.5 %collective-permute-start.11 = (f32[32,640]{1,0:T(8,128)S(1)}, f32[32,640]{1,0:T(8,128)S(1)}, u32[]{:S(2)}, u32[]{:S(2)}) collective-permute-start(f32[32,640]{1,0:T(8,128)S(1)} %shard_map.62.vectors_ref.message_ref), channel_id=1, source_target_pairs={{8,0},{9,1},{10,2},{11,3},{12,4},{13,5},{14,6},{15,7},{0,8},{1,9},... | collective-permute-start | bytes 245768 | tf_op jit(solution)/shard_map/ppermute | solution.py:256
  46.1 6.5 %collective-permute-start.10 = (f32[32,640]{1,0:T(8,128)S(1)}, f32[32,640]{1,0:T(8,128)S(1)}, u32[]{:S(2)}, u32[]{:S(2)}) collective-permute-start(f32[32,640]{1,0:T(8,128)S(1)} %shard_map.62.vectors_ref.message_ref), channel_id=1, source_target_pairs={{4,0},{5,1},{6,2},{7,3},{8,4},{9,5},{10,6},{11,7},{12,8},{13,9},{1... | collective-permute-start | bytes 245768 | tf_op jit(solution)/shard_map/ppermute | solution.py:256
  52.6 5.2 %collective-permute-start.12 = (f32[32,1152]{1,0:T(8,128)S(1)}, f32[32,1152]{1,0:T(8,128)S(1)}, u32[]{:S(2)}, u32[]{:S(2)}) collective-permute-start(f32[32,1152]{1,0:T(8,128)S(1)} %pad_maximum_fusion.3), channel_id=1, source_target_pairs={{2,0},{3,1},{4,2},{5,3},{6,4},{7,5},{8,6},{9,7},{10,8},{11,9},{12,... | collective-permute-start | bytes 442376 | tf_op jit(solution)/shard_map/ppermute | solution.py:256
  55.2 5.0 %collective-permute-start.14 = (f32[4,32,512]{2,1,0:T(8,128)S(1)}, f32[4,32,512]{2,1,0:T(8,128)S(1)}, u32[]{:S(2)}, u32[]{:S(2)}) collective-permute-start(f32[4,32,512]{2,1,0:T(8,128)S(1)} %get-tuple-element.11), channel_id=1, source_target_pairs={{1,0},{0,1},{3,2},{2,3},{5,4},{4,5},{7,6},{6,7},{9,8},{8,9},{11,10... | collective-permute-start | bytes 786440 | tf_op jit(solution)/shard_map/ppermute | solution.py:259
  57.8 11.2 %collective-permute-start.18 = (f32[32,128]{1,0:T(8,128)S(1)}, f32[32,128]{1,0:T(8,128)S(1)}, u32[]{:S(2)}, u32[]{:S(2)}) collective-permute-start(f32[32,128]{1,0:T(8,128)S(1)} %slice_add_fusion.4), channel_id=1, source_target_pairs={{4,0},{5,1},{6,2},{7,3},{8,4},{9,5},{10,6},{11,7},{12,8},{13,9},{1... | collective-permute-start | bytes 49160 | tf_op jit(solution)/shard_map/ppermute | solution.py:256
  60.2 8.4 %collective-permute-start.15 = (f32[2,32,512]{2,1,0:T(8,128)S(1)}, f32[2,32,512]{2,1,0:T(8,128)S(1)}, u32[]{:S(2)}, u32[]{:S(2)}) collective-permute-start(f32[2,32,512]{2,1,0:T(8,128)S(1)} %pad_maximum_fusion.5), channel_id=1, source_target_pairs={{14,0},{15,1},{0,2},{1,3},{2,4},{3,5},{4,6},{5,7},{6,8},{7,9},{8,1... | collective-permute-start | bytes 393224 | tf_op jit(solution)/shard_map/ppermute | solution.py:256
  68.7 6.1 %collective-permute-start.16 = (f32[32,512]{1,0:T(8,128)S(1)}, f32[32,512]{1,0:T(8,128)S(1)}, u32[]{:S(2)}, u32[]{:S(2)}) collective-permute-start(f32[32,512]{1,0:T(8,128)S(1)} %get-tuple-element.20), channel_id=1, source_target_pairs={{12,0},{13,1},{14,2},{15,3},{0,4},{1,5},{2,6},{3,7},{4,8},{5,9},{6... | collective-permute-start | bytes 196616 | tf_op jit(solution)/shard_map/ppermute | solution.py:256
  68.8 6.1 %collective-permute-start.17 = (f32[32,512]{1,0:T(8,128)S(1)}, f32[32,512]{1,0:T(8,128)S(1)}, u32[]{:S(2)}, u32[]{:S(2)}) collective-permute-start(f32[32,512]{1,0:T(8,128)S(1)} %get-tuple-element.21), channel_id=1, source_target_pairs={{8,0},{9,1},{10,2},{11,3},{12,4},{13,5},{14,6},{15,7},{0,8},{1,9},... | collective-permute-start | bytes 196616 | tf_op jit(solution)/shard_map/ppermute | solution.py:256
  68.9 6.0 %collective-permute-start.13 = (f32[4,32,512]{2,1,0:T(8,128)S(1)}, f32[4,32,512]{2,1,0:T(8,128)S(1)}, u32[]{:S(2)}, u32[]{:S(2)}) collective-permute-start(f32[4,32,512]{2,1,0:T(8,128)S(1)} %pad_maximum_fusion.1), channel_id=1, source_target_pairs={{1,0},{0,1},{3,2},{2,3},{5,4},{4,5},{7,6},{6,7},{9,8},{8,9},{11,10... | collective-permute-start | bytes 786440 | tf_op jit(solution)/shard_map/ppermute | solution.py:259
  69.0 1.5 %collective-permute-start.19 = (f32[32,128]{1,0:T(8,128)S(1)}, f32[32,128]{1,0:T(8,128)S(1)}, u32[]{:S(2)}, u32[]{:S(2)}) collective-permute-start(f32[32,128]{1,0:T(8,128)S(1)} %add.130), channel_id=1, source_target_pairs={{1,0},{0,1},{3,2},{2,3},{5,4},{4,5},{7,6},{6,7},{9,8},{8,9},{11,10... | collective-permute-start | bytes 49160 | tf_op jit(solution)/shard_map/ppermute | solution.py:259
  78.7 1.2 %collective-permute-start.20 = (f32[32,128]{1,0:T(8,128)S(1)}, f32[32,128]{1,0:T(8,128)S(1)}, u32[]{:S(2)}, u32[]{:S(2)}) collective-permute-start(f32[32,128]{1,0:T(8,128)S(1)} %get-tuple-element.13), channel_id=1, source_target_pairs={{1,0},{0,1},{3,2},{2,3},{5,4},{4,5},{7,6},{6,7},{9,8},{8,9},{11,10... | collective-permute-start | bytes 49160 | tf_op jit(solution)/shard_map/ppermute | solution.py:259
  80.0 3.7 %collective-permute-start.21 = (f32[32,128]{1,0:T(8,128)S(1)}, f32[32,128]{1,0:T(8,128)S(1)}, u32[]{:S(2)}, u32[]{:S(2)}) collective-permute-start(f32[32,128]{1,0:T(8,128)S(1)} %add.132), channel_id=1, source_target_pairs={{2,0},{3,1},{0,2},{1,3},{6,4},{7,5},{4,6},{5,7},{10,8},{11,9},{8,1... | collective-permute-start | bytes 49160 | tf_op jit(solution)/shard_map/ppermute | solution.py:259
  83.7 5.5 %collective-permute-start.24 = (f32[32,128]{1,0:T(8,128)S(1)}, f32[32,128]{1,0:T(8,128)S(1)}, u32[]{:S(2)}, u32[]{:S(2)}) collective-permute-start(f32[32,128]{1,0:T(8,128)S(1)} %add.133), channel_id=1, source_target_pairs={{12,0},{13,1},{14,2},{15,3},{8,4},{9,5},{10,6},{11,7},{4,8},{5,9},... | collective-permute-start | bytes 49160 | tf_op jit(solution)/shard_map/ppermute | solution.py:259
  86.6 4.6 %collective-permute-start.23 = (f32[32,128]{1,0:T(8,128)S(1)}, f32[32,128]{1,0:T(8,128)S(1)}, u32[]{:S(2)}, u32[]{:S(2)}) collective-permute-start(f32[32,128]{1,0:T(8,128)S(1)} %add.133), channel_id=1, source_target_pairs={{8,0},{9,1},{10,2},{11,3},{12,4},{13,5},{14,6},{15,7},{0,8},{1,9},... | collective-permute-start | bytes 49160 | tf_op jit(solution)/shard_map/ppermute | solution.py:259
  86.6 4.6 %collective-permute-start.22 = (f32[32,128]{1,0:T(8,128)S(1)}, f32[32,128]{1,0:T(8,128)S(1)}, u32[]{:S(2)}, u32[]{:S(2)}) collective-permute-start(f32[32,128]{1,0:T(8,128)S(1)} %add.133), channel_id=1, source_target_pairs={{4,0},{5,1},{6,2},{7,3},{0,4},{1,5},{2,6},{3,7},{12,8},{13,9},{14,... | collective-permute-start | bytes 49160 | tf_op jit(solution)/shard_map/ppermute | solution.py:259

commit v3 on v2

v3 whole, which is shorter than its diff:
```python
import functools

import jax
import jax.numpy as jnp
from jax import lax
from jax.experimental import pallas as pl
from jax.experimental.pallas import tpu as pltpu
from jax.sharding import PartitionSpec as P

SCALE = 0.0078125
SIDE = 128
PAD = 8

precise = lax.Precision.HIGHEST
in_vmem = pl.BlockSpec(memory_space=pltpu.VMEM)
in_hbm = pl.BlockSpec(memory_space=pltpu.HBM)
in_smem = pl.BlockSpec(memory_space=pltpu.SMEM)


def struct(*shape):
    return pltpu.VMEM(shape, jnp.float32)


def mm(left, right):
    return lax.dot_general(
        left, right, (((1,), (0,)), ((), ())), precision=precise, preferred_element_type=jnp.float32
    )


def mm_t(left, right):
    return lax.dot_general(
        left, right, (((1,), (1,)), ((), ())), precision=precise, preferred_element_type=jnp.float32
    )


def halves(block):
    high = block.astype(jnp.bfloat16)
    return high, (block - high.astype(jnp.float32)).astype(jnp.bfloat16)


def split_product(vectors, matrix_high, matrix_low, side):
    dims = (((1,), (side,)), ((), ()))
    dot = functools.partial(lax.dot_general, dimension_numbers=dims, preferred_element_type=jnp.float32)
    high, low = vectors
    if low is None:
        return dot(high, matrix_high) + dot(high, matrix_low)
    rows = high.shape[0]
    both = dot(jnp.concatenate([high, low], axis=0), matrix_high)
    return both[:rows] + both[rows:] + dot(high, matrix_low)


def parts_of(block, exact):
    if exact:
        return block.astype(jnp.bfloat16), None
    return halves(block)


def factor(matrix):
    size = matrix.shape[0]
    step = 8
    strips = size // step
    lane = lax.broadcasted_iota(jnp.int32, (step, size), 1)
    rows = [lax.broadcasted_iota(jnp.int32, (step, size), 0) + step * s for s in range(strips)]
    columns = [
        [jnp.broadcast_to(matrix[step * s : step * s + step, j : j + 1], (step, size)) for s in range(strips)]
        for j in range(size)
    ]
    inverse = [jnp.where(lane == rows[s], 1.0, 0.0) for s in range(strips)]
    lower = [jnp.zeros((step, size), jnp.float32) for _ in range(strips)]
    for k in range(size):
        home, at = divmod(k, step)
        pivot = jnp.broadcast_to(columns[k][home][at : at + 1, :], (step, size))
        root = lax.rsqrt(pivot)
        root = root * (1.5 - 0.5 * (pivot * root) * root)
        scaled = [None] * strips
        for s in range(home, strips):
            scaled[s] = columns[k][s] * root
            if s == home:
                scaled[s] = jnp.where(rows[s] >= k, scaled[s], 0.0)
            lower[s] = jnp.where(lane == k, scaled[s], lower[s])
        for j in range(k + 1, size):
            place, inside = divmod(j, step)
            weight = jnp.broadcast_to(scaled[place][inside : inside + 1, :], (step, size))
            for s in range(place, strips):
                columns[j][s] = columns[j][s] - scaled[s] * weight
        done = jnp.broadcast_to(inverse[home][at : at + 1, :], (step, size)) * root
        for s in range(home, strips):
            if s == home:
                inverse[s] = jnp.where(rows[s] == k, done, inverse[s] - jnp.where(rows[s] > k, scaled[s], 0.0) * done)
            else:
                inverse[s] = inverse[s] - scaled[s] * done
    return jnp.concatenate(lower, axis=0), jnp.concatenate(inverse, axis=0)


def pack(ref, place, matrix):
    side = matrix.shape[0]
    for q in range(side // PAD):
        start = SIDE * place + side * q
        ref[ref.shape[0] - PAD :, start : start + side] = matrix[PAD * q : PAD * q + PAD]


def unpack(ref, place, side):
    starts = [SIDE * place + side * q for q in range(side // PAD)]
    return jnp.concatenate([ref[ref.shape[0] - PAD :, s : s + side] for s in starts], axis=0)


def place_of(columns_ref, e):
    devices = lax.axis_size("col")
    position = lax.axis_index("col")
    core = position & 1
    ahead = core + lax.rem(columns_ref[0, e] - position + devices, devices)
    chip = ahead >> 1
    return core, (chip + 1) & 1, (chip - 1) >> 1, ahead & 1, chip == 0


def put_product(columns_ref, e, product, keep_ref, send_ref):
    core, speaker, part, block, here = place_of(columns_ref, e)
    slot = jnp.where(here, 1, part) * 2 + block

    @pl.when(speaker == core)
    def _():
        keep_ref[slot] = product

    @pl.when(speaker != core)
    def _():
        send_ref[slot] = product


def begin_kernel(
    columns_ref, probes_hbm, diagonal_hbm, forward_hbm,
    message_ref, core_ref, keep_ref, send_ref, high_ref, low_ref, diagonal_high_ref, diagonal_low_ref,
    probes_ref, diagonal_ref, forward_ref, sems,
):
    tiles = forward_ref.shape[0]
    copies = [pltpu.make_async_copy(probes_hbm, probes_ref, sems.at[0])]
    copies += [pltpu.make_async_copy(forward_hbm.at[e], forward_ref.at[e], sems.at[e + 1]) for e in range(tiles)]
    copies += [pltpu.make_async_copy(diagonal_hbm, diagonal_ref, sems.at[tiles + 1])]
    for copy in copies:
        copy.start()
    keep_ref[...] = jnp.zeros_like(keep_ref)
    send_ref[...] = jnp.zeros_like(send_ref)
    core_ref[...] = jnp.full(core_ref.shape, lax.axis_index("col") & 1, jnp.int32)
    copies[0].wait()
    signs = (2 * probes_ref[...] - 1).astype(jnp.float32) * SCALE
    rows, order = signs.shape
    message_ref[:rows] = signs
    gram = mm_t(signs, signs)
    exact = (signs.astype(jnp.bfloat16), None)
    for e in range(tiles):
        copies[e + 1].wait()
        high, low = halves(forward_ref[e])
        high_ref[e] = high
        low_ref[e] = low
        put_product(columns_ref, e, split_product(exact, high, low, 0), keep_ref, send_ref)
    copies[tiles + 1].wait()
    square = lax.broadcasted_iota(jnp.int32, (SIDE, SIDE), 0) == lax.broadcasted_iota(jnp.int32, (SIDE, SIDE), 1)
    trace = jnp.zeros((1, SIDE), jnp.float32)
    for start in range(0, order, SIDE):
        tile = diagonal_ref[start : start + SIDE, start : start + SIDE]
        trace += jnp.sum(jnp.where(square, tile, 0.0) * (1.0 / order), axis=0, keepdims=True)
    trace = jnp.sum(trace, axis=1, keepdims=True)
    message_ref[rows:] = jnp.broadcast_to(trace, (PAD, order))
    pack(message_ref, 0, gram)
    line = lax.broadcasted_iota(jnp.int32, (order, order), 0) == lax.broadcasted_iota(jnp.int32, (order, order), 1)
    high, low = halves(diagonal_ref[...] - jnp.where(line, trace, 0.0))
    diagonal_high_ref[...] = high
    diagonal_low_ref[...] = low


def outgoing_kernel(columns_ref, message_ref, high_ref, low_ref, keep_ref, send_ref):
    rows = keep_ref.shape[1]
    vectors = halves(message_ref[:rows])
    keep_ref[...] = jnp.zeros_like(keep_ref)
    send_ref[...] = jnp.zeros_like(send_ref)
    for e in range(high_ref.shape[0]):
        put_product(columns_ref, e, split_product(vectors, high_ref[e], low_ref[e], 0), keep_ref, send_ref)


def incoming_kernel(
    exact, columns_ref, message_ref, pair_ref, mine_ref, theirs_ref, high_ref, low_ref, diagonal_high_ref, diagonal_low_ref, image_ref
):
    rows = image_ref.shape[0]
    image = split_product(parts_of(message_ref[:rows], exact), diagonal_high_ref[...], diagonal_low_ref[...], 0)
    for e in range(high_ref.shape[0]):
        core, speaker, part, block, here = place_of(columns_ref, e)
        start = pl.multiple_of(jnp.where(here, 0, part) * 2 * rows + block * rows, rows)
        inside = pl.multiple_of(block * rows, rows)
        met = jnp.where(speaker == core, mine_ref[pl.ds(start, rows)], theirs_ref[pl.ds(start, rows)])
        met = jnp.where(here, pair_ref[pl.ds(inside, rows)], met)
        image += split_product(parts_of(met, exact), high_ref[e], low_ref[e], 1)
    image_ref[...] = image


def shift_of(devices, start_ref, sums_ref):
    mean = sums_ref[0:1, SIDE : SIDE + 1] * (1.0 / devices)
    return mean, start_ref[start_ref.shape[0] - PAD :][0:1, SIDE : SIDE + 1] - mean


def first_kernel(devices, start_ref, image_ref, total_ref, sums_ref, message_ref):
    rows, order = image_ref.shape
    signs = start_ref[:rows]
    image = image_ref[...] + total_ref[...] + shift_of(devices, start_ref, sums_ref)[1] * signs
    message_ref[:rows] = image
    both = mm_t(jnp.concatenate([signs, image], axis=0), image)
    message_ref[rows:] = jnp.zeros((PAD, order), jnp.float32)
    pack(message_ref, 0, both[:rows])
    pack(message_ref, 1, both[rows:])


def root_kernel(sums_ref, inverse_ref):
    inverse_ref[...] = factor(unpack(sums_ref, 0, inverse_ref.shape[0]))[1]


def second_kernel(
    devices, start_ref, message_ref, image_ref, total_ref, root_ref, first_sums_ref, sums_ref, basis_ref, result_ref, share_ref
):
    rows, order = image_ref.shape
    signs = start_ref[:rows]
    first = message_ref[:rows]
    mean, shift = shift_of(devices, start_ref, first_sums_ref)
    image = image_ref[...] + total_ref[...] + shift * first
    root = root_ref[...]
    alpha = mm_t(mm(root, unpack(sums_ref, 0, rows)), root)
    gram = mm_t(mm(root, unpack(sums_ref, 1, rows)), root) - mm_t(alpha, alpha)
    beta, inverse = factor(gram)
    scaled = mm(inverse, root)
    back = mm(mm(inverse, alpha), root)
    link = lax.dot_general(
        beta, root, (((0,), (0,)), ((), ())), precision=precise, preferred_element_type=jnp.float32
    )
    basis = mm(scaled, first) - mm(back, signs)
    result = mm(scaled, image) - mm(back, first) - mm(link, signs)
    basis_ref[...] = basis
    result_ref[...] = result
    both = mm_t(jnp.concatenate([basis, result], axis=0), result)
    line = lax.broadcasted_iota(jnp.int32, (rows, rows), 0)
    lane = lax.broadcasted_iota(jnp.int32, (rows, rows), 1)
    part = 1.0 / devices
    share_ref[:, :rows] = both[:rows]
    share_ref[:, rows : 2 * rows] = both[rows:]
    share_ref[:, 2 * rows : 3 * rows] = (alpha + jnp.where(line == lane, mean, 0.0)) * part
    share_ref[:, 3 * rows :] = jnp.where(lane > line, mean, beta) * part


def last_kernel(share_ref, basis_ref, result_ref, next_ref, blocks_ref):
    rows = share_ref.shape[0]
    line = lax.broadcasted_iota(jnp.int32, (rows, rows), 0)
    lane = lax.broadcasted_iota(jnp.int32, (rows, rows), 1)
    alpha = share_ref[:, :rows]
    mean = share_ref[0:1, 4 * rows - 1 : 4 * rows]
    gram = share_ref[:, rows : 2 * rows] - mm_t(alpha, alpha)
    beta, inverse = factor(gram)
    next_ref[...] = mm(inverse, result_ref[...] - mm(alpha, basis_ref[...]))
    blocks_ref[0] = share_ref[:, 2 * rows : 3 * rows]
    blocks_ref[1] = jnp.where(lane > line, 0.0, share_ref[:, 3 * rows :])
    blocks_ref[2] = alpha + jnp.where(line == lane, mean, 0.0)
    blocks_ref[3] = beta


def call(kernel, out_shape, args, smem=0, hbm=0, scratch=(), room=8):
    args = [pltpu.with_memory_space_constraint(a, pltpu.HBM) if j < smem + hbm else a for j, a in enumerate(args)]
    outs = in_vmem if not isinstance(out_shape, tuple) else (in_vmem,) * len(out_shape)
    return pl.pallas_call(
        kernel,
        out_shape=out_shape,
        in_specs=[in_smem] * smem + [in_hbm] * hbm + [in_vmem] * (len(args) - smem - hbm),
        out_specs=outs,
        scratch_shapes=list(scratch),
        compiler_params=pltpu.CompilerParams(vmem_limit_bytes=room * 1024 * 1024),
        cost_estimate=pl.CostEstimate(flops=1, bytes_accessed=1, transcendentals=0),
    )(*args)


def body(probes, diagonal, forward_tiles, tile_columns):
    forward = forward_tiles[0]
    rows, order = probes.shape
    devices = lax.axis_size("col")

    def swapped(block, bits=1):
        return lax.ppermute(block, "col", [(i ^ bits, i) for i in range(devices)])

    def from_chips(block, *chips):
        hops = [chips[i & 1] for i in range(devices)]
        route = [((i + 2 * hops[i]) % devices, i) for i in range(devices) if hops[i] is not None]
        return lax.ppermute(block, "col", route)

    def whole(sums):
        bits = 2
        while bits < devices:
            sums = sums + swapped(sums, bits)
            bits *= 2
        return sums

    def apply(message, products, exact):
        partner = swapped(message)
        pair = jnp.concatenate(
            [
                jnp.where(lower, message[:rows], partner[:rows]),
                jnp.where(lower, partner[:rows], message[:rows]),
                message[rows:] + partner[rows:],
            ]
        )
        payload = pair[2 * rows :]
        near, far = from_chips(pair, 1, 2), from_chips(pair, 3, None)
        last = from_chips(jnp.concatenate([pair[:rows], payload]), None, 4)
        if products is None:
            message, pair = lax.optimization_barrier((message, pair))
            products = call(
                outgoing_kernel,
                (struct(4, rows, order), struct(4, rows, order)),
                (tile_columns, message, high, low),
                smem=1,
            )
        keep, send = products
        ahead = keep + swapped(send)
        near_ahead = jnp.concatenate([ahead[0], ahead[1], payload])
        far_ahead = jnp.concatenate([ahead[2], ahead[3], payload])
        near_back, far_back = from_chips(near_ahead, -1, -2), from_chips(far_ahead, -3, None)
        last_back = from_chips(ahead[2], None, -4)
        near, far, last, near_back, far_back, last_back = lax.optimization_barrier(
            (near, far, last, near_back, far_back, last_back)
        )
        mine = jnp.concatenate([near[: 2 * rows], far[:rows] + last[:rows], far[rows : 2 * rows]])
        theirs = swapped(mine)
        image = call(
            functools.partial(incoming_kernel, exact),
            struct(rows, order),
            (tile_columns, message, pair, mine, theirs, high, low, diagonal_high, diagonal_low),
            smem=1,
        )
        if devices == 16:
            sums = jnp.where(lower_pad, payload, 0.0) + near[2 * rows :] + far[2 * rows :] + last[rows:]
            sums = sums + near_back[2 * rows :] + far_back[2 * rows :]
        else:
            sums = jnp.where(lower_pad, whole(payload), 0.0)
        first = near_back[:rows] + far_back[:rows] + last_back
        second = near_back[rows : 2 * rows] + jnp.where(lower, far_back[rows : 2 * rows], far_ahead[rows : 2 * rows])
        other = swapped(jnp.concatenate([jnp.where(lower, second, first), sums]))
        return image, jnp.where(lower, first, second) + other[:rows], sums + other[rows:]

    tiles = forward.shape[0]
    split = pltpu.VMEM(forward.shape, jnp.bfloat16)
    split_diagonal = pltpu.VMEM(diagonal.shape, jnp.bfloat16)
    start, core, keep, send, high, low, diagonal_high, diagonal_low = call(
        begin_kernel,
        (
            struct(rows + PAD, order), pltpu.VMEM((rows, order), jnp.int32),
            struct(4, rows, order), struct(4, rows, order),
            split, split, split_diagonal, split_diagonal,
        ),
        (tile_columns, probes, diagonal, forward),
        smem=1,
        hbm=3,
        room=12,
        scratch=(
            pltpu.VMEM(probes.shape, jnp.int32),
            pltpu.VMEM(diagonal.shape, jnp.float32),
            pltpu.VMEM(forward.shape, jnp.float32),
            pltpu.SemaphoreType.DMA((tiles + 2,)),
        ),
    )
    lower = core == 0
    lower_pad = lower[:PAD]
    image, total, start_sums = apply(start, (keep, send), True)
    message = call(
        functools.partial(first_kernel, devices), struct(rows + PAD, order), (start, image, total, start_sums)
    )
    image, total, sums = apply(message, None, False)
    root = call(root_kernel, struct(rows, rows), (start_sums,))
    basis, result, share = call(
        functools.partial(second_kernel, devices),
        (struct(rows, order), struct(rows, order), struct(rows, SIDE)),
        (start, message, image, total, root, start_sums, sums),
    )
    bits = 1
    while bits < devices:
        if 4 * bits <= devices:
            one, two, three = (swapped(share, bits * j) for j in (1, 2, 3))
            share = (share + one) + (two + three)
            bits *= 4
        else:
            share = share + swapped(share, bits)
            bits *= 2
    outs = (jax.ShapeDtypeStruct((rows, order), jnp.float32), jax.ShapeDtypeStruct((4, rows, rows), jnp.float32))
    return call(last_kernel, outs, (share, basis, result))


def solution(mesh):
    placed = (
        P(None, ("groups", "col")),
        P(("groups", "col"), None),
        P(("groups", "col"), None, None, None),
        P(("groups", "col"), None),
    )
    return jax.shard_map(
        body,
        mesh=mesh,
        in_specs=placed,
        out_specs=(P(None, ("groups", "col")), P("groups", None, None)),
        check_vma=False,
    )
```

time: 93.4 us -> 75.6 us (0.81)
  waiting for transfers between devices: 42.2 us -> 22.1 us
  starting transfers between devices: 26.1 us -> 35.2 us
  local copies, waits for them, and re-layouts: 7.05 us -> 0.06 us
    ppermute x14 -> x12, waiting for transfers between devices: 31.4 us -> 12.5 us  [from_chips(): return lax.ppermute(block, 'col', route)]
    unnamed x12 -> x0, local copies, waits for them, and re-layouts: 7.03 us -> none
    ppermute x14 -> x12, starting transfers between devices: 20.4 us -> 25.1 us  [from_chips(): return lax.ppermute(block, 'col', route)]
    ppermute x11 -> x14, starting transfers between devices: 5.68 us -> 10.1 us  [swapped(): return lax.ppermute(block, 'col', [(i ^ bits, i) for i in range(devices)])]
    ppermute x11 -> x14, waiting for transfers between devices: 10.8 us -> 9.56 us  [swapped(): return lax.ppermute(block, 'col', [(i ^ bits, i) for i in range(devices)])]
    pallas_call x10 -> x8, Pallas kernels: 15.7 us -> 16.5 us  [call(): pl.pallas_call(kernel, out_shape=out_shape, in_specs=[in_smem] * smem + [...]
  transfers between devices with their start and end apart: 25 -> 26, of which waited for: 16 -> 14; matrix products, arithmetic and copies ran while one was open for 1% -> 0% of each run, Pallas kernels for 7% -> 1%
where the time goes in v3:
time: 75.6 us; the launch traced here: 75.3 us
  starting transfers between devices  35.2 us (47%)
  waiting for transfers between devices  22.1 us (29%)
  Pallas kernels  16.5 us (22%)
  between operations  0.98 us (1%)
    ppermute x12, starting transfers between devices, from_chips(): return lax.ppermute(block, 'col', route)  25.1 us
    pallas_call x8, Pallas kernels, call(): pl.pallas_call(kernel, out_shape=out_shape, in_specs=[in_smem] * smem + [...  16.5 us
    ppermute x12, waiting for transfers between devices, from_chips(): return lax.ppermute(block, 'col', route)  12.5 us
    ppermute x14, starting transfers between devices, swapped(): return lax.ppermute(block, 'col', [(i ^ bits, i) for i in range(devices)])  10.1 us
    ppermute x14, waiting for transfers between devices, swapped(): return lax.ppermute(block, 'col', [(i ^ bits, i) for i in range(devices)])  9.56 us
  transfers between devices with their start and end apart: 26, of which 14 were waited for; matrix products, arithmetic and copies ran while one was open for 0% of the time, Pallas kernels for 1%

profile of v3, /device:TPU:0, one launch (start us, length us, event | category | flops | bytes accessed | tf_op | source)
XLA Modules:
  0.0 75.3 jit_solution(4540215772717501784)
XLA Ops:
  0.6 4.3 %shard_map.59 = (f32[40,512]{1,0:T(8,128)S(1)}, s32[32,512]{1,0:T(8,128)S(1)}, f32[4,32,512]{2,1,0:T(8,128)S(1)}, f32[4,32,512]{2,1,0:T(8,128)S(1)}, bf16[5,512,...) custom-call(s32[1,5]{1,0:T(1,128)} %columns_ref.7, ...), custom_call_target="tpu_custom_call" | custom-call | flops 1 | bytes 1 | tf_op jit(solution)/shard_map/pallas_call | solution.py:263
  5.6 0.8 %collective-permute-done = f32[40,512]{1,0:T(8,128)S(1)} collective-permute-done((f32[40,512]{1,0:T(8,128)S(1)}, f32[40,512]{1,0:T(8,128)S(1)}, u32[]{:S(2)}, u32[]{:S(2)}) %collective-permute-start) | collective-permute-done | bytes 81952 | tf_op jit(solution)/shard_map/ppermute | solution.py:280
  6.5 0.7 collective-permute-start.3
  7.3 6.0 %collective-permute-start.1 = (f32[72,512]{1,0:T(8,128)S(1)}, f32[72,512]{1,0:T(8,128)S(1)}, u32[]{:S(2)}, u32[]{:S(2)}) collective-permute-start(f32[72,512]{1,0:T(8,128)S(1)} %get-tuple-element.76.pair_ref), channel_id=1, source_target_pairs={{2,0},{5,1},{4,2},{7,3},{6,4},{9,5},{8,6},{11,7},{10,8},{13,9},{12... | collective-permute-start | bytes 442376 | tf_op jit(solution)/shard_map/ppermute | solution.py:285
  13.2 1.9 %collective-permute-start.2 = (f32[72,512]{1,0:T(8,128)S(1)}, f32[72,512]{1,0:T(8,128)S(1)}, u32[]{:S(2)}, u32[]{:S(2)}) collective-permute-start(f32[72,512]{1,0:T(8,128)S(1)} %get-tuple-element.76.pair_ref), channel_id=1, source_target_pairs={{6,0},{8,2},{10,4},{12,6},{14,8},{0,10},{2,12},{4,14},{22,16},{24,... | collective-permute-start | bytes 442376 | tf_op jit(solution)/shard_map/ppermute | solution.py:285
  15.2 2.0 %collective-permute-start.5 = (f32[72,512]{1,0:T(8,128)S(1)}, f32[72,512]{1,0:T(8,128)S(1)}, u32[]{:S(2)}, u32[]{:S(2)}) collective-permute-start(f32[72,512]{1,0:T(8,128)S(1)} %get-tuple-element.75), channel_id=1, source_target_pairs={{14,0},{13,1},{0,2},{15,3},{2,4},{1,5},{4,6},{3,7},{6,8},{5,9},{8,... | collective-permute-start | bytes 442376 | tf_op jit(solution)/shard_map/ppermute | solution.py:285
  17.1 2.9 %collective-permute-start.6 = (f32[72,512]{1,0:T(8,128)S(1)}, f32[72,512]{1,0:T(8,128)S(1)}, u32[]{:S(2)}, u32[]{:S(2)}) collective-permute-start(f32[72,512]{1,0:T(8,128)S(1)} %get-tuple-element.74), channel_id=1, source_target_pairs={{10,0},{12,2},{14,4},{0,6},{2,8},{4,10},{6,12},{8,14},{26,16},{28,... | collective-permute-start | bytes 442376 | tf_op jit(solution)/shard_map/ppermute | solution.py:285
  20.8 5.0 %collective-permute-done.2 = f32[72,512]{1,0:T(8,128)S(1)} collective-permute-done((f32[72,512]{1,0:T(8,128)S(1)}, f32[72,512]{1,0:T(8,128)S(1)}, u32[]{:S(2)}, u32[]{:S(2)}) %collective-permute-start.2) | collective-permute-done | bytes 147488 | tf_op jit(solution)/shard_map/ppermute | solution.py:285
  25.7 2.2 %collective-permute-done.6 = f32[72,512]{1,0:T(8,128)S(1)} collective-permute-done((f32[72,512]{1,0:T(8,128)S(1)}, f32[72,512]{1,0:T(8,128)S(1)}, u32[]{:S(2)}, u32[]{:S(2)}) %collective-permute-start.6) | collective-permute-done | bytes 147488 | tf_op jit(solution)/shard_map/ppermute | solution.py:285
  28.7 0.7 collective-permute-done.9
  29.8 2.4 %shard_map.60.image_ref = f32[32,512]{1,0:T(8,128)S(1)} custom-call(s32[1,5]{1,0:T(1,128)} %columns_ref.7, f32[40,512]{1,0:T(8,128)S(1)} %get-tuple-element.29.message_ref.start_ref, f32[72,512]{1,0:T(8,128)S(1)} %get-tuple-element.76.pair_ref, f32[128,512]{1,0:T(8,128)S(1)} %pad_maximum_fusion.mine_ref, f32[128,512]{1,0:T(8,128)S(1)} %collective-permute-done.8.theirs_ref, ...), custom_call_target="tpu_custom_call" | custom-call | flops 1 | bytes 1 | tf_op jit(solution)/shard_map/pallas_call | solution.py:263
  33.0 0.9 %collective-permute-done.10 = f32[40,512]{1,0:T(8,128)S(1)} collective-permute-done((f32[40,512]{1,0:T(8,128)S(1)}, f32[40,512]{1,0:T(8,128)S(1)}, u32[]{:S(2)}, u32[]{:S(2)}) %collective-permute-start.10) | collective-permute-done | bytes 81952 | tf_op jit(solution)/shard_map/ppermute | solution.py:280
  34.0 2.1 %shard_map.62 = (f32[4,32,512]{2,1,0:T(8,128)S(1)}, f32[4,32,512]{2,1,0:T(8,128)S(1)}) custom-call(s32[1,5]{1,0:T(1,128)} %columns_ref.7, f32[40,512]{1,0:T(8,128)S(1)} %shard_map.61.message_ref, bf16[5,512,512]{2,1,0:T(8,128)(2,1)S(1)} %get-tuple-element.36.high_ref, bf16[5,512,512]{2,1,0:T(8,128)(2,1)S(1)} %get-tuple-element.37.low_ref), custom_call_target="tpu_custom_call" | custom-call | flops 1 | bytes 1 | tf_op jit(solution)/shard_map/pallas_call | solution.py:263
  36.5 0.9 %collective-permute-start.11 = (f32[72,512]{1,0:T(8,128)S(1)}, f32[72,512]{1,0:T(8,128)S(1)}, u32[]{:S(2)}, u32[]{:S(2)}) collective-permute-start(f32[72,512]{1,0:T(8,128)S(1)} %pad_maximum_fusion.7.pair_ref), channel_id=1, source_target_pairs={{2,0},{5,1},{4,2},{7,3},{6,4},{9,5},{8,6},{11,7},{10,8},{13,9},{12... | collective-permute-start | bytes 442376 | tf_op jit(solution)/shard_map/ppermute | solution.py:285
  37.4 2.4 %collective-permute-start.12 = (f32[72,512]{1,0:T(8,128)S(1)}, f32[72,512]{1,0:T(8,128)S(1)}, u32[]{:S(2)}, u32[]{:S(2)}) collective-permute-start(f32[72,512]{1,0:T(8,128)S(1)} %pad_maximum_fusion.7.pair_ref), channel_id=1, source_target_pairs={{6,0},{8,2},{10,4},{12,6},{14,8},{0,10},{2,12},{4,14},{22,16},{24,... | collective-permute-start | bytes 442376 | tf_op jit(solution)/shard_map/ppermute | solution.py:285
  39.9 0.7 collective-permute-start.13
  40.7 3.0 %collective-permute-start.15 = (f32[72,512]{1,0:T(8,128)S(1)}, f32[72,512]{1,0:T(8,128)S(1)}, u32[]{:S(2)}, u32[]{:S(2)}) collective-permute-start(f32[72,512]{1,0:T(8,128)S(1)} %get-tuple-element.73), channel_id=1, source_target_pairs={{14,0},{13,1},{0,2},{15,3},{2,4},{1,5},{4,6},{3,7},{6,8},{5,9},{8,... | collective-permute-start | bytes 442376 | tf_op jit(solution)/shard_map/ppermute | solution.py:285
  43.6 3.4 %collective-permute-start.16 = (f32[72,512]{1,0:T(8,128)S(1)}, f32[72,512]{1,0:T(8,128)S(1)}, u32[]{:S(2)}, u32[]{:S(2)}) collective-permute-start(f32[72,512]{1,0:T(8,128)S(1)} %get-tuple-element.72), channel_id=1, source_target_pairs={{10,0},{12,2},{14,4},{0,6},{2,8},{4,10},{6,12},{8,14},{26,16},{28,... | collective-permute-start | bytes 442376 | tf_op jit(solution)/shard_map/ppermute | solution.py:285
  47.0 0.7 collective-permute-start.17
  48.4 1.0 %collective-permute-done.12 = f32[72,512]{1,0:T(8,128)S(1)} collective-permute-done((f32[72,512]{1,0:T(8,128)S(1)}, f32[72,512]{1,0:T(8,128)S(1)}, u32[]{:S(2)}, u32[]{:S(2)}) %collective-permute-start.12) | collective-permute-done | bytes 147488 | tf_op jit(solution)/shard_map/ppermute | solution.py:285
  49.4 4.4 %collective-permute-done.16 = f32[72,512]{1,0:T(8,128)S(1)} collective-permute-done((f32[72,512]{1,0:T(8,128)S(1)}, f32[72,512]{1,0:T(8,128)S(1)}, u32[]{:S(2)}, u32[]{:S(2)}) %collective-permute-start.16) | collective-permute-done | bytes 147488 | tf_op jit(solution)/shard_map/ppermute | solution.py:285
  53.8 1.7 %collective-permute-start.19 = (f32[40,512]{1,0:T(8,128)S(1)}, f32[40,512]{1,0:T(8,128)S(1)}, u32[]{:S(2)}, u32[]{:S(2)}) collective-permute-start(f32[40,512]{1,0:T(8,128)S(1)} %pad_maximum_fusion.11), channel_id=1, source_target_pairs={{1,0},{0,1},{3,2},{2,3},{5,4},{4,5},{7,6},{6,7},{9,8},{8,9},{11,10... | collective-permute-start | bytes 245768 | tf_op jit(solution)/shard_map/ppermute | solution.py:280
  55.6 0.8 %collective-permute-done.19 = f32[40,512]{1,0:T(8,128)S(1)} collective-permute-done((f32[40,512]{1,0:T(8,128)S(1)}, f32[40,512]{1,0:T(8,128)S(1)}, u32[]{:S(2)}, u32[]{:S(2)}) %collective-permute-start.19) | collective-permute-done | bytes 81952 | tf_op jit(solution)/shard_map/ppermute | solution.py:280
  57.1 2.5 %shard_map.63.image_ref = f32[32,512]{1,0:T(8,128)S(1)} custom-call(s32[1,5]{1,0:T(1,128)} %columns_ref.7, f32[40,512]{1,0:T(8,128)S(1)} %shard_map.61.message_ref, f32[72,512]{1,0:T(8,128)S(1)} %pad_maximum_fusion.7.pair_ref, f32[128,512]{1,0:T(8,128)S(1)} %pad_maximum_fusion.1.mine_ref, f32[128,512]{1,0:T(8,128)S(1)} %collective-permute-done.18.theirs_ref, ...), custom_call_target="tpu_custom_call" | custom-call | flops 1 | bytes 1 | tf_op jit(solution)/shard_map/pallas_call | solution.py:263
  59.6 2.3 %shard_map.65 = (f32[32,512]{1,0:T(8,128)S(1)}, f32[32,512]{1,0:T(8,128)S(1)}, f32[32,128]{1,0:T(8,128)S(1)}) custom-call(f32[40,512]{1,0:T(8,128)S(1)} %get-tuple-element.29.message_ref.start_ref, f32[40,512]{1,0:T(8,128)S(1)} %shard_map.61.message_ref, f32[32,512]{1,0:T(8,128)S(1)} %shard_map.63.image_ref, f32[32,512]{1,0:T(8,128)S(1)} %slice_add_fusion.total_ref, ...), custom_call_target="tpu_custom_call" | custom-call | flops 1 | bytes 1 | tf_op jit(solution)/shard_map/pallas_call | solution.py:263
  62.1 0.8 %collective-permute-start.21 = (f32[32,128]{1,0:T(8,128)S(1)}, f32[32,128]{1,0:T(8,128)S(1)}, u32[]{:S(2)}, u32[]{:S(2)}) collective-permute-start(f32[32,128]{1,0:T(8,128)S(1)} %get-tuple-element.53), channel_id=1, source_target_pairs={{2,0},{3,1},{0,2},{1,3},{6,4},{7,5},{4,6},{5,7},{10,8},{11,9},{8,1... | collective-permute-start | bytes 49160 | tf_op jit(solution)/shard_map/ppermute | solution.py:280
  62.9 0.9 %collective-permute-start.22 = (f32[32,128]{1,0:T(8,128)S(1)}, f32[32,128]{1,0:T(8,128)S(1)}, u32[]{:S(2)}, u32[]{:S(2)}) collective-permute-start(f32[32,128]{1,0:T(8,128)S(1)} %get-tuple-element.53), channel_id=1, source_target_pairs={{3,0},{2,1},{1,2},{0,3},{7,4},{6,5},{5,6},{4,7},{11,8},{10,9},{9,1... | collective-permute-start | bytes 49160 | tf_op jit(solution)/shard_map/ppermute | solution.py:280
  63.8 2.0 %collective-permute-done.21 = f32[32,128]{1,0:T(8,128)S(1)} collective-permute-done((f32[32,128]{1,0:T(8,128)S(1)}, f32[32,128]{1,0:T(8,128)S(1)}, u32[]{:S(2)}, u32[]{:S(2)}) %collective-permute-start.21) | collective-permute-done | bytes 16416 | tf_op jit(solution)/shard_map/ppermute | solution.py:280
  66.2 1.7 %collective-permute-start.24 = (f32[32,128]{1,0:T(8,128)S(1)}, f32[32,128]{1,0:T(8,128)S(1)}, u32[]{:S(2)}, u32[]{:S(2)}) collective-permute-start(f32[32,128]{1,0:T(8,128)S(1)} %add_add_fusion.3), channel_id=1, source_target_pairs={{8,0},{9,1},{10,2},{11,3},{12,4},{13,5},{14,6},{15,7},{0,8},{1,9},... | collective-permute-start | bytes 49160 | tf_op jit(solution)/shard_map/ppermute | solution.py:280
  67.9 2.7 %collective-permute-start.25 = (f32[32,128]{1,0:T(8,128)S(1)}, f32[32,128]{1,0:T(8,128)S(1)}, u32[]{:S(2)}, u32[]{:S(2)}) collective-permute-start(f32[32,128]{1,0:T(8,128)S(1)} %add_add_fusion.3), channel_id=1, source_target_pairs={{12,0},{13,1},{14,2},{15,3},{8,4},{9,5},{10,6},{11,7},{4,8},{5,9},... | collective-permute-start | bytes 49160 | tf_op jit(solution)/shard_map/ppermute | solution.py:280
  70.9 2.5 %collective-permute-done.25 = f32[32,128]{1,0:T(8,128)S(1)} collective-permute-done((f32[32,128]{1,0:T(8,128)S(1)}, f32[32,128]{1,0:T(8,128)S(1)}, u32[]{:S(2)}, u32[]{:S(2)}) %collective-permute-start.25) | collective-permute-done | bytes 16416 | tf_op jit(solution)/shard_map/ppermute | solution.py:280
  73.4 1.8 %shard_map.66 = (f32[32,512]{1,0:T(8,128)}, f32[4,32,32]{2,1,0:T(8,128)}) custom-call(f32[32,128]{1,0:T(8,128)S(1)} %add_add_fusion.2.share_ref, f32[32,512]{1,0:T(8,128)S(1)} %get-tuple-element.54.basis_ref, f32[32,512]{1,0:T(8,128)S(1)} %get-tuple-element.55.result_ref), custom_call_target="tpu_custom_call" | custom-call | flops 1 | bytes 1 | tf_op jit(solution)/shard_map/pallas_call | solution.py:263
  (60 shorter events, 6.4 us)
Async XLA Ops:
  5.0 1.4 %collective-permute-start = (f32[40,512]{1,0:T(8,128)S(1)}, f32[40,512]{1,0:T(8,128)S(1)}, u32[]{:S(2)}, u32[]{:S(2)}) collective-permute-start(f32[40,512]{1,0:T(8,128)S(1)} %get-tuple-element.29.message_ref.start_ref), channel_id=1, source_target_pairs={{1,0},{0,1},{3,2},{2,3},{5,4},{4,5},{7,6},{6,7},{9,8},{8,9},{11,10... | collective-permute-start | bytes 245768 | tf_op jit(solution)/shard_map/ppermute | solution.py:280
  5.5 1.7 %collective-permute-start.4 = (f32[4,32,512]{2,1,0:T(8,128)S(1)}, f32[4,32,512]{2,1,0:T(8,128)S(1)}, u32[]{:S(2)}, u32[]{:S(2)}) collective-permute-start(f32[4,32,512]{2,1,0:T(8,128)S(1)} %get-tuple-element.32), channel_id=1, source_target_pairs={{1,0},{0,1},{3,2},{2,3},{5,4},{4,5},{7,6},{6,7},{9,8},{8,9},{11,10... | collective-permute-start | bytes 786440 | tf_op jit(solution)/shard_map/ppermute | solution.py:280
  6.5 13.6 %collective-permute-start.3 = (f32[40,512]{1,0:T(8,128)S(1)}, f32[40,512]{1,0:T(8,128)S(1)}, u32[]{:S(2)}, u32[]{:S(2)}) collective-permute-start(f32[40,512]{1,0:T(8,128)S(1)} %pad_maximum_fusion.8), channel_id=1, source_target_pairs={{9,1},{11,3},{13,5},{15,7},{1,9},{3,11},{5,13},{7,15},{25,17},{27,... | collective-permute-start | bytes 245768 | tf_op jit(solution)/shard_map/ppermute | solution.py:285
  7.3 13.5 %collective-permute-start.1 = (f32[72,512]{1,0:T(8,128)S(1)}, f32[72,512]{1,0:T(8,128)S(1)}, u32[]{:S(2)}, u32[]{:S(2)}) collective-permute-start(f32[72,512]{1,0:T(8,128)S(1)} %get-tuple-element.76.pair_ref), channel_id=1, source_target_pairs={{2,0},{5,1},{4,2},{7,3},{6,4},{9,5},{8,6},{11,7},{10,8},{13,9},{12... | collective-permute-start | bytes 442376 | tf_op jit(solution)/shard_map/ppermute | solution.py:285
  13.2 12.5 %collective-permute-start.2 = (f32[72,512]{1,0:T(8,128)S(1)}, f32[72,512]{1,0:T(8,128)S(1)}, u32[]{:S(2)}, u32[]{:S(2)}) collective-permute-start(f32[72,512]{1,0:T(8,128)S(1)} %get-tuple-element.76.pair_ref), channel_id=1, source_target_pairs={{6,0},{8,2},{10,4},{12,6},{14,8},{0,10},{2,12},{4,14},{22,16},{24,... | collective-permute-start | bytes 442376 | tf_op jit(solution)/shard_map/ppermute | solution.py:285
  15.2 10.6 %collective-permute-start.5 = (f32[72,512]{1,0:T(8,128)S(1)}, f32[72,512]{1,0:T(8,128)S(1)}, u32[]{:S(2)}, u32[]{:S(2)}) collective-permute-start(f32[72,512]{1,0:T(8,128)S(1)} %get-tuple-element.75), channel_id=1, source_target_pairs={{14,0},{13,1},{0,2},{15,3},{2,4},{1,5},{4,6},{3,7},{6,8},{5,9},{8,... | collective-permute-start | bytes 442376 | tf_op jit(solution)/shard_map/ppermute | solution.py:285
  17.1 10.8 %collective-permute-start.6 = (f32[72,512]{1,0:T(8,128)S(1)}, f32[72,512]{1,0:T(8,128)S(1)}, u32[]{:S(2)}, u32[]{:S(2)}) collective-permute-start(f32[72,512]{1,0:T(8,128)S(1)} %get-tuple-element.74), channel_id=1, source_target_pairs={{10,0},{12,2},{14,4},{0,6},{2,8},{4,10},{6,12},{8,14},{26,16},{28,... | collective-permute-start | bytes 442376 | tf_op jit(solution)/shard_map/ppermute | solution.py:285
  20.1 0.7 collective-permute-start.7
  28.0 1.3 %collective-permute-start.9 = (f32[40,512]{1,0:T(8,128)S(1)}, f32[40,512]{1,0:T(8,128)S(1)}, u32[]{:S(2)}, u32[]{:S(2)}) collective-permute-start(f32[40,512]{1,0:T(8,128)S(1)} %pad_maximum_fusion.9), channel_id=1, source_target_pairs={{1,0},{0,1},{3,2},{2,3},{5,4},{4,5},{7,6},{6,7},{9,8},{8,9},{11,10... | collective-permute-start | bytes 245768 | tf_op jit(solution)/shard_map/ppermute | solution.py:280
  28.1 1.7 %collective-permute-start.8 = (f32[128,512]{1,0:T(8,128)S(1)}, f32[128,512]{1,0:T(8,128)S(1)}, u32[]{:S(2)}, u32[]{:S(2)}) collective-permute-start(f32[128,512]{1,0:T(8,128)S(1)} %pad_maximum_fusion.mine_ref), channel_id=1, source_target_pairs={{1,0},{0,1},{3,2},{2,3},{5,4},{4,5},{7,6},{6,7},{9,8},{8,9},{11,10... | collective-permute-start | bytes 786440 | tf_op jit(solution)/shard_map/ppermute | solution.py:280
  32.6 1.3 %collective-permute-start.10 = (f32[40,512]{1,0:T(8,128)S(1)}, f32[40,512]{1,0:T(8,128)S(1)}, u32[]{:S(2)}, u32[]{:S(2)}) collective-permute-start(f32[40,512]{1,0:T(8,128)S(1)} %shard_map.61.message_ref), channel_id=1, source_target_pairs={{1,0},{0,1},{3,2},{2,3},{5,4},{4,5},{7,6},{6,7},{9,8},{8,9},{11,10... | collective-permute-start | bytes 245768 | tf_op jit(solution)/shard_map/ppermute | solution.py:280
  36.1 4.5 %collective-permute-start.14 = (f32[4,32,512]{2,1,0:T(8,128)S(1)}, f32[4,32,512]{2,1,0:T(8,128)S(1)}, u32[]{:S(2)}, u32[]{:S(2)}) collective-permute-start(f32[4,32,512]{2,1,0:T(8,128)S(1)} %get-tuple-element.46), channel_id=1, source_target_pairs={{1,0},{0,1},{3,2},{2,3},{5,4},{4,5},{7,6},{6,7},{9,8},{8,9},{11,10... | collective-permute-start | bytes 786440 | tf_op jit(solution)/shard_map/ppermute | solution.py:280
  36.5 11.9 %collective-permute-start.11 = (f32[72,512]{1,0:T(8,128)S(1)}, f32[72,512]{1,0:T(8,128)S(1)}, u32[]{:S(2)}, u32[]{:S(2)}) collective-permute-start(f32[72,512]{1,0:T(8,128)S(1)} %pad_maximum_fusion.7.pair_ref), channel_id=1, source_target_pairs={{2,0},{5,1},{4,2},{7,3},{6,4},{9,5},{8,6},{11,7},{10,8},{13,9},{12... | collective-permute-start | bytes 442376 | tf_op jit(solution)/shard_map/ppermute | solution.py:285
  37.4 11.9 %collective-permute-start.12 = (f32[72,512]{1,0:T(8,128)S(1)}, f32[72,512]{1,0:T(8,128)S(1)}, u32[]{:S(2)}, u32[]{:S(2)}) collective-permute-start(f32[72,512]{1,0:T(8,128)S(1)} %pad_maximum_fusion.7.pair_ref), channel_id=1, source_target_pairs={{6,0},{8,2},{10,4},{12,6},{14,8},{0,10},{2,12},{4,14},{22,16},{24,... | collective-permute-start | bytes 442376 | tf_op jit(solution)/shard_map/ppermute | solution.py:285
  39.9 7.1 %collective-permute-start.13 = (f32[40,512]{1,0:T(8,128)S(1)}, f32[40,512]{1,0:T(8,128)S(1)}, u32[]{:S(2)}, u32[]{:S(2)}) collective-permute-start(f32[40,512]{1,0:T(8,128)S(1)} %pad_maximum_fusion.10), channel_id=1, source_target_pairs={{9,1},{11,3},{13,5},{15,7},{1,9},{3,11},{5,13},{7,15},{25,17},{27,... | collective-permute-start | bytes 245768 | tf_op jit(solution)/shard_map/ppermute | solution.py:285
  40.7 8.7 %collective-permute-start.15 = (f32[72,512]{1,0:T(8,128)S(1)}, f32[72,512]{1,0:T(8,128)S(1)}, u32[]{:S(2)}, u32[]{:S(2)}) collective-permute-start(f32[72,512]{1,0:T(8,128)S(1)} %get-tuple-element.73), channel_id=1, source_target_pairs={{14,0},{13,1},{0,2},{15,3},{2,4},{1,5},{4,6},{3,7},{6,8},{5,9},{8,... | collective-permute-start | bytes 442376 | tf_op jit(solution)/shard_map/ppermute | solution.py:285
  43.6 10.1 %collective-permute-start.16 = (f32[72,512]{1,0:T(8,128)S(1)}, f32[72,512]{1,0:T(8,128)S(1)}, u32[]{:S(2)}, u32[]{:S(2)}) collective-permute-start(f32[72,512]{1,0:T(8,128)S(1)} %get-tuple-element.72), channel_id=1, source_target_pairs={{10,0},{12,2},{14,4},{0,6},{2,8},{4,10},{6,12},{8,14},{26,16},{28,... | collective-permute-start | bytes 442376 | tf_op jit(solution)/shard_map/ppermute | solution.py:285
  47.0 2.3 %collective-permute-start.17 = (f32[32,512]{1,0:T(8,128)S(1)}, f32[32,512]{1,0:T(8,128)S(1)}, u32[]{:S(2)}, u32[]{:S(2)}) collective-permute-start(f32[32,512]{1,0:T(8,128)S(1)} %get-tuple-element.58), channel_id=1, source_target_pairs={{9,1},{11,3},{13,5},{15,7},{1,9},{3,11},{5,13},{7,15},{25,17},{27,... | collective-permute-start | bytes 196616 | tf_op jit(solution)/shard_map/ppermute | solution.py:285
  53.8 2.6 %collective-permute-start.19 = (f32[40,512]{1,0:T(8,128)S(1)}, f32[40,512]{1,0:T(8,128)S(1)}, u32[]{:S(2)}, u32[]{:S(2)}) collective-permute-start(f32[40,512]{1,0:T(8,128)S(1)} %pad_maximum_fusion.11), channel_id=1, source_target_pairs={{1,0},{0,1},{3,2},{2,3},{5,4},{4,5},{7,6},{6,7},{9,8},{8,9},{11,10... | collective-permute-start | bytes 245768 | tf_op jit(solution)/shard_map/ppermute | solution.py:280
  55.5 1.6 %collective-permute-start.18 = (f32[128,512]{1,0:T(8,128)S(1)}, f32[128,512]{1,0:T(8,128)S(1)}, u32[]{:S(2)}, u32[]{:S(2)}) collective-permute-start(f32[128,512]{1,0:T(8,128)S(1)} %pad_maximum_fusion.1.mine_ref), channel_id=1, source_target_pairs={{1,0},{0,1},{3,2},{2,3},{5,4},{4,5},{7,6},{6,7},{9,8},{8,9},{11,10... | collective-permute-start | bytes 786440 | tf_op jit(solution)/shard_map/ppermute | solution.py:280
  61.9 1.9 %collective-permute-start.20 = (f32[32,128]{1,0:T(8,128)S(1)}, f32[32,128]{1,0:T(8,128)S(1)}, u32[]{:S(2)}, u32[]{:S(2)}) collective-permute-start(f32[32,128]{1,0:T(8,128)S(1)} %get-tuple-element.53), channel_id=1, source_target_pairs={{1,0},{0,1},{3,2},{2,3},{5,4},{4,5},{7,6},{6,7},{9,8},{8,9},{11,10... | collective-permute-start | bytes 49160 | tf_op jit(solution)/shard_map/ppermute | solution.py:280
  62.1 3.8 %collective-permute-start.21 = (f32[32,128]{1,0:T(8,128)S(1)}, f32[32,128]{1,0:T(8,128)S(1)}, u32[]{:S(2)}, u32[]{:S(2)}) collective-permute-start(f32[32,128]{1,0:T(8,128)S(1)} %get-tuple-element.53), channel_id=1, source_target_pairs={{2,0},{3,1},{0,2},{1,3},{6,4},{7,5},{4,6},{5,7},{10,8},{11,9},{8,1... | collective-permute-start | bytes 49160 | tf_op jit(solution)/shard_map/ppermute | solution.py:280
  62.9 3.3 %collective-permute-start.22 = (f32[32,128]{1,0:T(8,128)S(1)}, f32[32,128]{1,0:T(8,128)S(1)}, u32[]{:S(2)}, u32[]{:S(2)}) collective-permute-start(f32[32,128]{1,0:T(8,128)S(1)} %get-tuple-element.53), channel_id=1, source_target_pairs={{3,0},{2,1},{1,2},{0,3},{7,4},{6,5},{5,6},{4,7},{11,8},{10,9},{9,1... | collective-permute-start | bytes 49160 | tf_op jit(solution)/shard_map/ppermute | solution.py:280
  66.2 4.5 %collective-permute-start.23 = (f32[32,128]{1,0:T(8,128)S(1)}, f32[32,128]{1,0:T(8,128)S(1)}, u32[]{:S(2)}, u32[]{:S(2)}) collective-permute-start(f32[32,128]{1,0:T(8,128)S(1)} %add_add_fusion.3), channel_id=1, source_target_pairs={{4,0},{5,1},{6,2},{7,3},{0,4},{1,5},{2,6},{3,7},{12,8},{13,9},{14,... | collective-permute-start | bytes 49160 | tf_op jit(solution)/shard_map/ppermute | solution.py:280
  66.2 4.7 %collective-permute-start.24 = (f32[32,128]{1,0:T(8,128)S(1)}, f32[32,128]{1,0:T(8,128)S(1)}, u32[]{:S(2)}, u32[]{:S(2)}) collective-permute-start(f32[32,128]{1,0:T(8,128)S(1)} %add_add_fusion.3), channel_id=1, source_target_pairs={{8,0},{9,1},{10,2},{11,3},{12,4},{13,5},{14,6},{15,7},{0,8},{1,9},... | collective-permute-start | bytes 49160 | tf_op jit(solution)/shard_map/ppermute | solution.py:280
  67.9 5.5 %collective-permute-start.25 = (f32[32,128]{1,0:T(8,128)S(1)}, f32[32,128]{1,0:T(8,128)S(1)}, u32[]{:S(2)}, u32[]{:S(2)}) collective-permute-start(f32[32,128]{1,0:T(8,128)S(1)} %add_add_fusion.3), channel_id=1, source_target_pairs={{12,0},{13,1},{14,2},{15,3},{8,4},{9,5},{10,6},{11,7},{4,8},{5,9},... | collective-permute-start | bytes 49160 | tf_op jit(solution)/shard_map/ppermute | solution.py:280

commit v4 on v3

v4 whole, which is shorter than its diff:
```python
import functools

import jax
import jax.numpy as jnp
from jax import lax
from jax.experimental import pallas as pl
from jax.experimental.pallas import tpu as pltpu
from jax.sharding import PartitionSpec as P

SCALE = 0.0078125
SIDE = 128
PAD = 8
SLOTS = 6

precise = lax.Precision.HIGHEST
in_vmem = pl.BlockSpec(memory_space=pltpu.VMEM)
in_hbm = pl.BlockSpec(memory_space=pltpu.HBM)
in_smem = pl.BlockSpec(memory_space=pltpu.SMEM)


def struct(*shape):
    return pltpu.VMEM(shape, jnp.float32)


def mm(left, right):
    return lax.dot_general(
        left, right, (((1,), (0,)), ((), ())), precision=precise, preferred_element_type=jnp.float32
    )


def mm_t(left, right):
    return lax.dot_general(
        left, right, (((1,), (1,)), ((), ())), precision=precise, preferred_element_type=jnp.float32
    )


def halves(block):
    high = block.astype(jnp.bfloat16)
    return high, (block - high.astype(jnp.float32)).astype(jnp.bfloat16)


def split_product(vectors, matrix_high, matrix_low, side):
    dims = (((1,), (side,)), ((), ()))
    dot = functools.partial(lax.dot_general, dimension_numbers=dims, preferred_element_type=jnp.float32)
    high, low = vectors
    if low is None:
        return dot(high, matrix_high) + dot(high, matrix_low)
    rows = high.shape[0]
    both = dot(jnp.concatenate([high, low], axis=0), matrix_high)
    return both[:rows] + both[rows:] + dot(high, matrix_low)


def parts_of(block, exact):
    if exact:
        return block.astype(jnp.bfloat16), None
    return halves(block)


def factor(matrix):
    size = matrix.shape[0]
    step = 8
    strips = size // step
    lane = lax.broadcasted_iota(jnp.int32, (step, size), 1)
    rows = [lax.broadcasted_iota(jnp.int32, (step, size), 0) + step * s for s in range(strips)]
    columns = [
        [jnp.broadcast_to(matrix[step * s : step * s + step, j : j + 1], (step, size)) for s in range(strips)]
        for j in range(size)
    ]
    inverse = [jnp.where(lane == rows[s], 1.0, 0.0) for s in range(strips)]
    lower = [jnp.zeros((step, size), jnp.float32) for _ in range(strips)]
    for k in range(size):
        home, at = divmod(k, step)
        pivot = jnp.broadcast_to(columns[k][home][at : at + 1, :], (step, size))
        root = lax.rsqrt(pivot)
        root = root * (1.5 - 0.5 * (pivot * root) * root)
        scaled = [None] * strips
        for s in range(home, strips):
            scaled[s] = columns[k][s] * root
            if s == home:
                scaled[s] = jnp.where(rows[s] >= k, scaled[s], 0.0)
            lower[s] = jnp.where(lane == k, scaled[s], lower[s])
        for j in range(k + 1, size):
            place, inside = divmod(j, step)
            weight = jnp.broadcast_to(scaled[place][inside : inside + 1, :], (step, size))
            for s in range(place, strips):
                columns[j][s] = columns[j][s] - scaled[s] * weight
        done = jnp.broadcast_to(inverse[home][at : at + 1, :], (step, size)) * root
        for s in range(home, strips):
            if s == home:
                inverse[s] = jnp.where(rows[s] == k, done, inverse[s] - jnp.where(rows[s] > k, scaled[s], 0.0) * done)
            else:
                inverse[s] = inverse[s] - scaled[s] * done
    return jnp.concatenate(lower, axis=0), jnp.concatenate(inverse, axis=0)


def pack(ref, base, place, matrix):
    side = matrix.shape[0]
    for q in range(side // PAD):
        start = SIDE * place + side * q
        ref[base : base + PAD, start : start + side] = matrix[PAD * q : PAD * q + PAD]


def unpack(ref, place, side):
    starts = [SIDE * place + side * q for q in range(side // PAD)]
    return jnp.concatenate([ref[:, s : s + side] for s in starts], axis=0)


def place_of(columns_ref, e):
    devices = lax.axis_size("col")
    position = lax.axis_index("col")
    core = position & 1
    ahead = core + lax.rem(columns_ref[0, e] - position + devices, devices)
    return core, ahead >> 1, ahead & 1


def place_products(columns_ref, products_ref, bundle_ref, keep_ref):
    rows = products_ref.shape[1]
    start = rows + PAD
    keep_ref[...] = jnp.zeros_like(keep_ref)
    bundle_ref[start:] = jnp.zeros((bundle_ref.shape[0] - start, bundle_ref.shape[1]), jnp.float32)
    for e in range(products_ref.shape[0]):
        core, chip, block = place_of(columns_ref, e)
        speaker = jnp.where(chip == 1, 0, 1)
        slot = jnp.where(chip == 0, SLOTS - 1, jnp.where(chip < 3, 0, 2 * chip - 4) + block)

        @pl.when(speaker == core)
        def _():
            keep_ref[slot] = products_ref[e]

        @pl.when(speaker != core)
        def _():
            bundle_ref[pl.ds(pl.multiple_of(start + slot * rows, PAD), rows)] = products_ref[e]


def begin_kernel(
    columns_ref, probes_hbm, diagonal_hbm, forward_hbm,
    bundle_ref, core_ref, keep_ref, high_ref, low_ref,
    probes_ref, diagonal_ref, forward_ref, products_ref, sems,
):
    tiles = forward_ref.shape[0]
    squares = diagonal_ref.shape[0]
    copies = [pltpu.make_async_copy(probes_hbm, probes_ref, sems.at[0])]
    for q in range(squares):
        ends = pl.ds(SIDE * q, SIDE)
        copies += [pltpu.make_async_copy(diagonal_hbm.at[ends, ends], diagonal_ref.at[q], sems.at[1 + q])]
    for e in range(tiles):
        copies += [pltpu.make_async_copy(forward_hbm.at[e], forward_ref.at[e], sems.at[1 + squares + e])]
    for copy in copies:
        copy.start()
    core_ref[...] = jnp.full(core_ref.shape, lax.axis_index("col") & 1, jnp.int32)
    copies[0].wait()
    signs = (2 * probes_ref[...] - 1).astype(jnp.float32) * SCALE
    rows, order = signs.shape
    bundle_ref[:rows] = signs
    square = lax.broadcasted_iota(jnp.int32, (SIDE, SIDE), 0) == lax.broadcasted_iota(jnp.int32, (SIDE, SIDE), 1)
    trace = jnp.zeros((SIDE, SIDE), jnp.float32)
    for q in range(squares):
        copies[1 + q].wait()
        trace += jnp.where(square, diagonal_ref[q], 0.0) * (1.0 / order)
    trace = jnp.sum(jnp.sum(trace, axis=0, keepdims=True), axis=1, keepdims=True)
    bundle_ref[rows : rows + PAD] = jnp.broadcast_to(trace, (PAD, order))
    pack(bundle_ref, rows, 0, mm_t(signs, signs))
    exact = (signs.astype(jnp.bfloat16), None)
    for e in range(tiles):
        copies[1 + squares + e].wait()
        high, low = halves(forward_ref[e])
        high_ref[e] = high
        low_ref[e] = low
        products_ref[e] = split_product(exact, high, low, 0)
    place_products(columns_ref, products_ref, bundle_ref, keep_ref)


def first_near_kernel(
    bundle_ref, diagonal_ref, tile_high_ref, tile_low_ref, image_ref, high_ref, low_ref, turned_high_ref, turned_low_ref
):
    rows, order = image_ref.shape
    trace = bundle_ref[rows : rows + 1, SIDE : SIDE + 1]
    line = lax.broadcasted_iota(jnp.int32, (order, order), 0) == lax.broadcasted_iota(jnp.int32, (order, order), 1)
    high, low = halves(diagonal_ref[...] - jnp.where(line, trace, 0.0))
    high_ref[...] = high
    low_ref[...] = low
    image_ref[...] = split_product(parts_of(bundle_ref[:rows], True), high, low, 0)
    for e in range(tile_high_ref.shape[0]):
        turned_high_ref[e] = tile_high_ref[e].T
        turned_low_ref[e] = tile_low_ref[e].T


def second_near_kernel(bundle_ref, high_ref, low_ref, image_ref):
    rows = image_ref.shape[0]
    image_ref[...] = split_product(parts_of(bundle_ref[:rows], False), high_ref[...], low_ref[...], 0)


def incoming_kernel(exact, columns_ref, pair_ref, mine_ref, theirs_ref, high_ref, low_ref, image_ref, ready_ref):
    rows = image_ref.shape[0]
    tiles = high_ref.shape[0]
    for e in range(tiles):
        core, chip, block = place_of(columns_ref, e)
        speaker = jnp.where(chip == 2, 1, 0)
        part = jnp.where(chip < 3, 0, 2 * chip - 4)
        start = pl.multiple_of((part + block) * rows, rows)
        inside = pl.multiple_of(block * rows, rows)
        met = jnp.where(speaker == core, mine_ref[pl.ds(start, rows)], theirs_ref[pl.ds(start, rows)])
        met = jnp.where(chip == 0, pair_ref[pl.ds(inside, rows)], met)
        high, low = parts_of(met, exact)
        ready_ref[e, :rows] = high
        if not exact:
            ready_ref[e, rows:] = low
    image = jnp.zeros(image_ref.shape, jnp.float32)
    for e in range(tiles):
        vectors = ready_ref[e, :rows], None if exact else ready_ref[e, rows:]
        image += split_product(vectors, high_ref[e], low_ref[e], 0)
    image_ref[...] = image


def shift_of(devices, start_ref, sums_ref, rows):
    mean = sums_ref[0:1, SIDE : SIDE + 1] * (1.0 / devices)
    return mean, start_ref[rows : rows + 1, SIDE : SIDE + 1] - mean


def first_kernel(
    devices, columns_ref, start_ref, near_ref, image_ref, total_ref, sums_ref, high_ref, low_ref,
    bundle_ref, keep_ref, products_ref,
):
    rows, order = image_ref.shape
    signs = start_ref[:rows]
    image = near_ref[...] + image_ref[...] + total_ref[...]
    image += shift_of(devices, start_ref, sums_ref, rows)[1] * signs
    bundle_ref[:rows] = image
    vectors = halves(image)
    for e in range(high_ref.shape[0]):
        products_ref[e] = split_product(vectors, high_ref[e], low_ref[e], 0)
    both = mm_t(jnp.concatenate([signs, image], axis=0), image)
    bundle_ref[rows : rows + PAD] = jnp.zeros((PAD, order), jnp.float32)
    pack(bundle_ref, rows, 0, both[:rows])
    pack(bundle_ref, rows, 1, both[rows:])
    place_products(columns_ref, products_ref, bundle_ref, keep_ref)


def root_kernel(sums_ref, start_ref, message_ref, root_ref, lines_ref):
    rows = root_ref.shape[0]
    root = factor(unpack(sums_ref, 0, rows))[1]
    root_ref[...] = root
    lines_ref[...] = mm(root, jnp.concatenate([start_ref[:rows], message_ref[:rows]], axis=1))


def second_kernel(
    devices, start_ref, message_ref, near_ref, image_ref, total_ref, root_ref, lines_ref, first_sums_ref, sums_ref,
    basis_ref, result_ref, share_ref,
):
    rows, order = image_ref.shape
    mean, shift = shift_of(devices, start_ref, first_sums_ref, rows)
    root = root_ref[...]
    alpha = mm_t(mm(root, unpack(sums_ref, 0, rows)), root)
    gram = mm_t(mm(root, unpack(sums_ref, 1, rows)), root) - mm_t(alpha, alpha)
    image = mm(root, near_ref[...] + image_ref[...] + total_ref[...] + shift * message_ref[:rows])
    first_basis, first = lines_ref[:, :order], lines_ref[:, order:]
    bent = mm(alpha, lines_ref[...])
    beta, inverse = factor(gram)
    both = mm(inverse, jnp.concatenate([first - bent[:, :order], image - bent[:, order:]], axis=1))
    link = lax.dot_general(
        beta, first_basis, (((0,), (0,)), ((), ())), precision=precise, preferred_element_type=jnp.float32
    )
    basis = both[:, :order]
    result = both[:, order:] - link
    basis_ref[...] = basis
    result_ref[...] = result
    both = mm_t(jnp.concatenate([basis, result], axis=0), result)
    line = lax.broadcasted_iota(jnp.int32, (rows, rows), 0)
    lane = lax.broadcasted_iota(jnp.int32, (rows, rows), 1)
    part = 1.0 / devices
    share_ref[:, :rows] = both[:rows]
    share_ref[:, rows : 2 * rows] = both[rows:]
    share_ref[:, 2 * rows : 3 * rows] = (alpha + jnp.where(line == lane, mean, 0.0)) * part
    share_ref[:, 3 * rows :] = jnp.where(lane > line, mean, beta) * part


def last_kernel(share_ref, basis_ref, result_ref, next_ref, blocks_ref):
    rows = share_ref.shape[0]
    line = lax.broadcasted_iota(jnp.int32, (rows, rows), 0)
    lane = lax.broadcasted_iota(jnp.int32, (rows, rows), 1)
    alpha = share_ref[:, :rows]
    mean = share_ref[0:1, 4 * rows - 1 : 4 * rows]
    gram = share_ref[:, rows : 2 * rows] - mm_t(alpha, alpha)
    beta, inverse = factor(gram)
    next_ref[...] = mm(inverse, result_ref[...] - mm(alpha, basis_ref[...]))
    blocks_ref[0] = share_ref[:, 2 * rows : 3 * rows]
    blocks_ref[1] = jnp.where(lane > line, 0.0, share_ref[:, 3 * rows :])
    blocks_ref[2] = alpha + jnp.where(line == lane, mean, 0.0)
    blocks_ref[3] = beta


def call(kernel, out_shape, args, smem=0, hbm=0, scratch=(), room=8):
    args = [pltpu.with_memory_space_constraint(a, pltpu.HBM) if j < smem + hbm else a for j, a in enumerate(args)]
    outs = in_vmem if not isinstance(out_shape, tuple) else (in_vmem,) * len(out_shape)
    return pl.pallas_call(
        kernel,
        out_shape=out_shape,
        in_specs=[in_smem] * smem + [in_hbm] * hbm + [in_vmem] * (len(args) - smem - hbm),
        out_specs=outs,
        scratch_shapes=list(scratch),
        compiler_params=pltpu.CompilerParams(vmem_limit_bytes=room * 1024 * 1024),
        cost_estimate=pl.CostEstimate(flops=1, bytes_accessed=1, transcendentals=0),
    )(*args)


def body(probes, diagonal, forward_tiles, tile_columns):
    forward = forward_tiles[0]
    rows, order = probes.shape
    devices = lax.axis_size("col")

    def swapped(block, bits=1):
        return lax.ppermute(block, "col", [(i ^ bits, i) for i in range(devices)])

    def from_chips(block, *chips):
        hops = [chips[i & 1] for i in range(devices)]
        route = [((i + 2 * hops[i]) % devices, i) for i in range(devices) if hops[i] is not None]
        return lax.ppermute(block, "col", route)

    def whole(sums):
        bits = 2
        while bits < devices:
            sums = sums + swapped(sums, bits)
            bits *= 2
        return sums

    def apply(bundle, keep, near_call, exact):
        partner = swapped(bundle)
        own, its = bundle[:rows], partner[:rows]
        payload = bundle[rows:top] + partner[rows:top]
        pair = jnp.concatenate([jnp.where(lower, own, its), jnp.where(lower, its, own), payload])
        ahead = keep + partner[top:].reshape(keep.shape)
        near_ahead = jnp.concatenate([ahead[0], ahead[1], payload])
        third_ahead = jnp.concatenate([ahead[2], ahead[3]])
        third_ahead = jnp.concatenate([jnp.where(both_lower, pair[: 2 * rows], third_ahead), payload])
        fourth_ahead = jnp.concatenate([jnp.where(lower, pair[:rows], ahead[4]), payload])
        near = from_chips(pair, 1, 2)
        near_back = from_chips(near_ahead, -1, -2)
        third = from_chips(third_ahead, 3, -3)
        fourth = from_chips(fourth_ahead, 4, -4)
        bundle, _, _ = lax.optimization_barrier((bundle, near_ahead, third_ahead))
        inner, turned = near_call(bundle)
        near, near_back, third, fourth, inner, turned = lax.optimization_barrier(
            (near, near_back, third, fourth, inner, turned)
        )
        mine = jnp.concatenate([near[: 2 * rows], third[: 2 * rows], fourth[:rows]])
        if devices == 16:
            sums = near[2 * rows :] + near_back[2 * rows :] + third[2 * rows :]
            sums = sums + jnp.where(lower_pad, payload + fourth[rows:], 0.0)
        else:
            sums = jnp.where(lower_pad, whole(payload), 0.0)
        first = near_back[:rows] + jnp.where(lower, 0.0, third[:rows] + fourth[:rows])
        second = near_back[rows : 2 * rows] + jnp.where(lower, 0.0, third[rows : 2 * rows] + ahead[SLOTS - 1])
        other = jnp.concatenate([jnp.where(lower, second, first), sums])
        mine, other = lax.optimization_barrier((mine, other))
        theirs, other = swapped(mine), swapped(other)
        image = call(
            functools.partial(incoming_kernel, exact),
            struct(rows, order),
            (tile_columns, pair, mine, theirs, *turned[-2:]),
            smem=1,
            scratch=(pltpu.VMEM((tiles, 2 * rows, order), jnp.bfloat16),),
        )
        return inner, image, jnp.where(lower, first, second) + other[:rows], sums + other[rows:], turned

    tiles = forward.shape[0]
    top = rows + PAD
    bundles = (struct(top + SLOTS * rows, order), struct(SLOTS, rows, order))
    products = pltpu.VMEM((tiles, rows, order), jnp.float32)
    split = pltpu.VMEM(forward.shape, jnp.bfloat16)
    split_diagonal = pltpu.VMEM(diagonal.shape, jnp.bfloat16)
    start, core, keep, high, low = call(
        begin_kernel,
        (bundles[0], pltpu.VMEM((rows, order), jnp.int32), bundles[1], split, split),
        (tile_columns, probes, diagonal, forward),
        smem=1,
        hbm=3,
        room=12,
        scratch=(
            pltpu.VMEM(probes.shape, jnp.int32),
            pltpu.VMEM((order // SIDE, SIDE, SIDE), jnp.float32),
            pltpu.VMEM(forward.shape, jnp.float32),
            products,
            pltpu.SemaphoreType.DMA((tiles + 1 + order // SIDE,)),
        ),
    )
    lower = core == 0
    lower_pad = lower[:PAD]
    both_lower = jnp.concatenate([lower, lower])

    def first_near(bundle):
        made = call(
            first_near_kernel,
            (struct(rows, order), split_diagonal, split_diagonal, split, split),
            (bundle, diagonal, high, low),
        )
        return made[0], made[1:]

    inner, image, total, start_sums, turned = apply(start, keep, first_near, True)
    diagonal_high, diagonal_low, *turned = turned
    message, keep = call(
        functools.partial(first_kernel, devices),
        bundles,
        (tile_columns, start, inner, image, total, start_sums, high, low),
        smem=1,
        scratch=(products,),
    )
    def second_near(bundle):
        inner = call(second_near_kernel, struct(rows, order), (bundle, diagonal_high, diagonal_low))
        ahead = call(root_kernel, (struct(rows, rows), struct(rows, 2 * order)), (start_sums, start, bundle))
        return inner, (*ahead, *turned)

    inner, image, total, sums, (root, lines, *_) = apply(message, keep, second_near, False)
    basis, result, share = call(
        functools.partial(second_kernel, devices),
        (struct(rows, order), struct(rows, order), struct(rows, SIDE)),
        (start, message, inner, image, total, root, lines, start_sums, sums),
    )
    bits = 1
    while bits < devices:
        if 4 * bits <= devices:
            one, two, three = (swapped(share, bits * j) for j in (1, 2, 3))
            share = (share + one) + (two + three)
            bits *= 4
        else:
            share = share + swapped(share, bits)
            bits *= 2
    outs = (jax.ShapeDtypeStruct((rows, order), jnp.float32), jax.ShapeDtypeStruct((4, rows, rows), jnp.float32))
    return call(last_kernel, outs, (share, basis, result))


def solution(mesh):
    placed = (
        P(None, ("groups", "col")),
        P(("groups", "col"), None),
        P(("groups", "col"), None, None, None),
        P(("groups", "col"), None),
    )
    return jax.shard_map(
        body,
        mesh=mesh,
        in_specs=placed,
        out_specs=(P(None, ("groups", "col")), P("groups", None, None)),
        check_vma=False,
    )
```

time: 75.6 us -> 69.2 us (0.915)
  starting transfers between devices: 35.2 us -> 23.7 us
  waiting for transfers between devices: 22.1 us -> 27.5 us
    ppermute x12 -> x8, starting transfers between devices: 25.1 us -> 15.1 us  [from_chips(): return lax.ppermute(block, 'col', route)]
    ppermute x12 -> x8, waiting for transfers between devices: 12.5 us -> 18.2 us  [from_chips(): return lax.ppermute(block, 'col', route)]
    ppermute x14 -> x12, starting transfers between devices: 10.1 us -> 8.56 us  [swapped(): return lax.ppermute(block, 'col', [(i ^ bits, i) for i in range(devices)])]
    pallas_call x8 -> x9, Pallas kernels: 16.5 us -> 16.2 us  [call(): pl.pallas_call(kernel, out_shape=out_shape, in_specs=[in_smem] * smem + [...]
    ppermute x14 -> x12, waiting for transfers between devices: 9.56 us -> 9.31 us  [swapped(): return lax.ppermute(block, 'col', [(i ^ bits, i) for i in range(devices)])]
  transfers between devices with their start and end apart: 26 -> 20, of which waited for: 14 -> 12; matrix products, arithmetic and copies ran while one was open for 0% -> 0% of each run, Pallas kernels for 1% -> 4%
where the time goes in v4:
time: 69.2 us; the launch traced here: 69 us
  waiting for transfers between devices  27.5 us (40%)
  starting transfers between devices  23.7 us (34%)
  Pallas kernels  16.2 us (23%)
  between operations  0.93 us (1%)
    ppermute x8, waiting for transfers between devices, from_chips(): return lax.ppermute(block, 'col', route)  18.2 us
    pallas_call x9, Pallas kernels, call(): pl.pallas_call(kernel, out_shape=out_shape, in_specs=[in_smem] * smem + [...  16.2 us
    ppermute x8, starting transfers between devices, from_chips(): return lax.ppermute(block, 'col', route)  15.1 us
    ppermute x12, waiting for transfers between devices, swapped(): return lax.ppermute(block, 'col', [(i ^ bits, i) for i in range(devices)])  9.31 us
    ppermute x12, starting transfers between devices, swapped(): return lax.ppermute(block, 'col', [(i ^ bits, i) for i in range(devices)])  8.56 us
  transfers between devices with their start and end apart: 20, of which 12 were waited for; matrix products, arithmetic and copies ran while one was open for 0% of the time, Pallas kernels for 4%

profile of v4, /device:TPU:0, one launch (start us, length us, event | category | flops | bytes accessed | tf_op | source)
XLA Modules:
  0.0 69.0 jit_solution(6489462499482308752)
XLA Ops:
  0.6 4.3 %shard_map.59 = (f32[232,512]{1,0:T(8,128)S(1)}, s32[32,512]{1,0:T(8,128)S(1)}, f32[6,32,512]{2,1,0:T(8,128)S(1)}, bf16[5,512,512]{2,1,0:T(8,128)(2,1)S(1)}, bf16[5,512,512]{2,1,0:T(8,128)(2,1)S(1)}) custom-call(s32[1,5]{1,0:T(1,128)} %columns_ref.7, s32[32,512]{1,0:T(8,128)} %probes_hbm.1, f32[512,512]{1,0:T(8,128)} %diagonal_ref.1, f32[5,512,512]{2,1,0:T(8,128)} %bitcast.51), custom_call_target="tpu_custom_call" | custom-call | flops 1 | bytes 1 | tf_op jit(solution)/shard_map/pallas_call | solution.py:295
  4.9 0.5 collective-permute-start
  5.4 1.5 %collective-permute-done = f32[232,512]{1,0:T(8,128)S(1)} collective-permute-done((f32[232,512]{1,0:T(8,128)S(1)}, f32[232,512]{1,0:T(8,128)S(1)}, u32[]{:S(2)}, u32[]{:S(2)}) %collective-permute-start) | collective-permute-done | bytes 475168 | tf_op jit(solution)/shard_map/ppermute | solution.py:312
  7.1 5.0 %collective-permute-start.3 = (f32[72,512]{1,0:T(8,128)S(1)}, f32[72,512]{1,0:T(8,128)S(1)}, u32[]{:S(2)}, u32[]{:S(2)}) collective-permute-start(f32[72,512]{1,0:T(8,128)S(1)} %get-tuple-element.105), channel_id=1, source_target_pairs={{6,0},{11,1},{8,2},{13,3},{10,4},{15,5},{12,6},{1,7},{14,8},{3,9},... | collective-permute-start | bytes 442376 | tf_op jit(solution)/shard_map/ppermute | solution.py:317
  12.1 1.5 %collective-permute-start.2 = (f32[72,512]{1,0:T(8,128)S(1)}, f32[72,512]{1,0:T(8,128)S(1)}, u32[]{:S(2)}, u32[]{:S(2)}) collective-permute-start(f32[72,512]{1,0:T(8,128)S(1)} %get-tuple-element.106), channel_id=1, source_target_pairs={{14,0},{13,1},{0,2},{15,3},{2,4},{1,5},{4,6},{3,7},{6,8},{5,9},{8,... | collective-permute-start | bytes 442376 | tf_op jit(solution)/shard_map/ppermute | solution.py:317
  13.6 3.2 %collective-permute-start.1 = (f32[72,512]{1,0:T(8,128)S(1)}, f32[72,512]{1,0:T(8,128)S(1)}, u32[]{:S(2)}, u32[]{:S(2)}) collective-permute-start(f32[72,512]{1,0:T(8,128)S(1)} %get-tuple-element.107.pair_ref), channel_id=1, source_target_pairs={{2,0},{5,1},{4,2},{7,3},{6,4},{9,5},{8,6},{11,7},{10,8},{13,9},{12... | collective-permute-start | bytes 442376 | tf_op jit(solution)/shard_map/ppermute | solution.py:317
  16.9 1.5 %shard_map.60 = (f32[32,512]{1,0:T(8,128)S(1)}, bf16[512,512]{1,0:T(8,128)(2,1)S(1)}, bf16[512,512]{1,0:T(8,128)(2,1)S(1)}, bf16[5,512,512]{2,1,0:T(8,128)(2,1)S(1)}, bf16[5,512,512]{2,1,0:T(8,128)(2,1)S(1)}) custom-call(f32[232,512]{1,0:T(8,128)S(1)} %get-tuple-element.46.bundle_ref.start_ref, f32[512,512]{1,0:T(8,128)S(1)} %copy-done, ...), custom_call_target="tpu_custom_call" | custom-call | flops 1 | bytes 1 | tf_op jit(solution)/shard_map/pallas_call | solution.py:295
  18.4 8.6 %collective-permute-done.4 = f32[40,512]{1,0:T(8,128)S(1)} collective-permute-done((f32[40,512]{1,0:T(8,128)S(1)}, f32[40,512]{1,0:T(8,128)S(1)}, u32[]{:S(2)}, u32[]{:S(2)}) %collective-permute-start.4) | collective-permute-done | bytes 81952 | tf_op jit(solution)/shard_map/ppermute | solution.py:317
  27.2 0.5 collective-permute-start.5
  27.7 0.8 %collective-permute-done.6 = f32[40,512]{1,0:T(8,128)S(1)} collective-permute-done((f32[40,512]{1,0:T(8,128)S(1)}, f32[40,512]{1,0:T(8,128)S(1)}, u32[]{:S(2)}, u32[]{:S(2)}) %collective-permute-start.6) | collective-permute-done | bytes 81952 | tf_op jit(solution)/shard_map/ppermute | solution.py:312
  28.5 0.4 collective-permute-done.5.theirs_ref
  29.0 1.7 %shard_map.61.image_ref = f32[32,512]{1,0:T(8,128)S(1)} custom-call(s32[1,5]{1,0:T(1,128)} %columns_ref.7, f32[72,512]{1,0:T(8,128)S(1)} %get-tuple-element.107.pair_ref, f32[160,512]{1,0:T(8,128)S(1)} %pad_maximum_fusion.mine_ref, f32[160,512]{1,0:T(8,128)S(1)} %collective-permute-done.5.theirs_ref, bf16[5,512,512]{2,1,0:T(8,128)(2,1)S(1)} %get-tuple-element.76.high_ref, ...), custom_call_target="tpu_custom_call" | custom-call | flops 1 | bytes 1 | tf_op jit(solution)/shard_map/pallas_call | solution.py:295
  30.6 2.0 %shard_map.62 = (f32[232,512]{1,0:T(8,128)S(1)}, f32[6,32,512]{2,1,0:T(8,128)S(1)}) custom-call(s32[1,5]{1,0:T(1,128)} %columns_ref.7, f32[232,512]{1,0:T(8,128)S(1)} %get-tuple-element.46.bundle_ref.start_ref, f32[32,512]{1,0:T(8,128)S(1)} %get-tuple-element.54.near_ref, f32[32,512]{1,0:T(8,128)S(1)} %shard_map.61.image_ref, ...), custom_call_target="tpu_custom_call" | custom-call | flops 1 | bytes 1 | tf_op jit(solution)/shard_map/pallas_call | solution.py:295
  33.0 1.5 %collective-permute-done.7 = f32[232,512]{1,0:T(8,128)S(1)} collective-permute-done((f32[232,512]{1,0:T(8,128)S(1)}, f32[232,512]{1,0:T(8,128)S(1)}, u32[]{:S(2)}, u32[]{:S(2)}) %collective-permute-start.7) | collective-permute-done | bytes 475168 | tf_op jit(solution)/shard_map/ppermute | solution.py:312
  34.7 0.7 %collective-permute-start.10 = (f32[72,512]{1,0:T(8,128)S(1)}, f32[72,512]{1,0:T(8,128)S(1)}, u32[]{:S(2)}, u32[]{:S(2)}) collective-permute-start(f32[72,512]{1,0:T(8,128)S(1)} %get-tuple-element.102), channel_id=1, source_target_pairs={{6,0},{11,1},{8,2},{13,3},{10,4},{15,5},{12,6},{1,7},{14,8},{3,9},... | collective-permute-start | bytes 442376 | tf_op jit(solution)/shard_map/ppermute | solution.py:317
  35.4 2.6 %collective-permute-start.9 = (f32[72,512]{1,0:T(8,128)S(1)}, f32[72,512]{1,0:T(8,128)S(1)}, u32[]{:S(2)}, u32[]{:S(2)}) collective-permute-start(f32[72,512]{1,0:T(8,128)S(1)} %get-tuple-element.103), channel_id=1, source_target_pairs={{14,0},{13,1},{0,2},{15,3},{2,4},{1,5},{4,6},{3,7},{6,8},{5,9},{8,... | collective-permute-start | bytes 442376 | tf_op jit(solution)/shard_map/ppermute | solution.py:317
  38.0 2.2 %collective-permute-start.8 = (f32[72,512]{1,0:T(8,128)S(1)}, f32[72,512]{1,0:T(8,128)S(1)}, u32[]{:S(2)}, u32[]{:S(2)}) collective-permute-start(f32[72,512]{1,0:T(8,128)S(1)} %get-tuple-element.104.pair_ref), channel_id=1, source_target_pairs={{2,0},{5,1},{4,2},{7,3},{6,4},{9,5},{8,6},{11,7},{10,8},{13,9},{12... | collective-permute-start | bytes 442376 | tf_op jit(solution)/shard_map/ppermute | solution.py:317
  40.2 1.0 %shard_map.64 = (f32[32,32]{1,0:T(8,128)S(1)}, f32[32,1024]{1,0:T(8,128)S(1)}) custom-call(f32[8,512]{1,0:T(8,128)S(1)} %slice_add_fusion.4.sums_ref.first_sums_ref, f32[232,512]{1,0:T(8,128)S(1)} %get-tuple-element.46.bundle_ref.start_ref, f32[232,512]{1,0:T(8,128)S(1)} %get-tuple-element.65.bundle_ref.message_ref), custom_call_target="tpu_custom_call" | custom-call | flops 1 | bytes 1 | tf_op jit(solution)/shard_map/pallas_call | solution.py:295
  41.5 9.6 %collective-permute-done.11 = f32[40,512]{1,0:T(8,128)S(1)} collective-permute-done((f32[40,512]{1,0:T(8,128)S(1)}, f32[40,512]{1,0:T(8,128)S(1)}, u32[]{:S(2)}, u32[]{:S(2)}) %collective-permute-start.11) | collective-permute-done | bytes 81952 | tf_op jit(solution)/shard_map/ppermute | solution.py:317
  51.3 0.5 collective-permute-start.12
  51.8 0.8 %collective-permute-done.13 = f32[40,512]{1,0:T(8,128)S(1)} collective-permute-done((f32[40,512]{1,0:T(8,128)S(1)}, f32[40,512]{1,0:T(8,128)S(1)}, u32[]{:S(2)}, u32[]{:S(2)}) %collective-permute-start.13) | collective-permute-done | bytes 81952 | tf_op jit(solution)/shard_map/ppermute | solution.py:312
  53.0 1.7 %shard_map.65.image_ref = f32[32,512]{1,0:T(8,128)S(1)} custom-call(s32[1,5]{1,0:T(1,128)} %columns_ref.7, f32[72,512]{1,0:T(8,128)S(1)} %get-tuple-element.104.pair_ref, f32[160,512]{1,0:T(8,128)S(1)} %pad_maximum_fusion.1.mine_ref, f32[160,512]{1,0:T(8,128)S(1)} %collective-permute-done.12.theirs_ref, bf16[5,512,512]{2,1,0:T(8,128)(2,1)S(1)} %get-tuple-element.76.high_ref, ...), custom_call_target="tpu_custom_call" | custom-call | flops 1 | bytes 1 | tf_op jit(solution)/shard_map/pallas_call | solution.py:295
  54.7 2.1 %shard_map.66 = (f32[32,512]{1,0:T(8,128)S(1)}, f32[32,512]{1,0:T(8,128)S(1)}, f32[32,128]{1,0:T(8,128)S(1)}) custom-call(f32[232,512]{1,0:T(8,128)S(1)} %get-tuple-element.46.bundle_ref.start_ref, f32[232,512]{1,0:T(8,128)S(1)} %get-tuple-element.65.bundle_ref.message_ref, f32[32,512]{1,0:T(8,128)S(1)} %shard_map.63.near_ref, ...), custom_call_target="tpu_custom_call" | custom-call | flops 1 | bytes 1 | tf_op jit(solution)/shard_map/pallas_call | solution.py:295
  56.8 2.0 %collective-permute-start.15 = (f32[32,128]{1,0:T(8,128)S(1)}, f32[32,128]{1,0:T(8,128)S(1)}, u32[]{:S(2)}, u32[]{:S(2)}) collective-permute-start(f32[32,128]{1,0:T(8,128)S(1)} %get-tuple-element.81), channel_id=1, source_target_pairs={{2,0},{3,1},{0,2},{1,3},{6,4},{7,5},{4,6},{5,7},{10,8},{11,9},{8,1... | collective-permute-start | bytes 49160 | tf_op jit(solution)/shard_map/ppermute | solution.py:312
  58.8 1.2 %collective-permute-done.16 = f32[32,128]{1,0:T(8,128)S(1)} collective-permute-done((f32[32,128]{1,0:T(8,128)S(1)}, f32[32,128]{1,0:T(8,128)S(1)}, u32[]{:S(2)}, u32[]{:S(2)}) %collective-permute-start.16) | collective-permute-done | bytes 16416 | tf_op jit(solution)/shard_map/ppermute | solution.py:312
  60.0 0.7 %collective-permute-done.15 = f32[32,128]{1,0:T(8,128)S(1)} collective-permute-done((f32[32,128]{1,0:T(8,128)S(1)}, f32[32,128]{1,0:T(8,128)S(1)}, u32[]{:S(2)}, u32[]{:S(2)}) %collective-permute-start.15) | collective-permute-done | bytes 16416 | tf_op jit(solution)/shard_map/ppermute | solution.py:312
  60.7 1.8 %collective-permute-start.19 = (f32[32,128]{1,0:T(8,128)S(1)}, f32[32,128]{1,0:T(8,128)S(1)}, u32[]{:S(2)}, u32[]{:S(2)}) collective-permute-start(f32[32,128]{1,0:T(8,128)S(1)} %add_add_fusion.1), channel_id=1, source_target_pairs={{12,0},{13,1},{14,2},{15,3},{8,4},{9,5},{10,6},{11,7},{4,8},{5,9},... | collective-permute-start | bytes 49160 | tf_op jit(solution)/shard_map/ppermute | solution.py:312
  62.6 0.6 collective-permute-start.18
  63.2 2.0 %collective-permute-start.17 = (f32[32,128]{1,0:T(8,128)S(1)}, f32[32,128]{1,0:T(8,128)S(1)}, u32[]{:S(2)}, u32[]{:S(2)}) collective-permute-start(f32[32,128]{1,0:T(8,128)S(1)} %add_add_fusion.1), channel_id=1, source_target_pairs={{4,0},{5,1},{6,2},{7,3},{0,4},{1,5},{2,6},{3,7},{12,8},{13,9},{14,... | collective-permute-start | bytes 49160 | tf_op jit(solution)/shard_map/ppermute | solution.py:312
  65.2 1.1 %collective-permute-done.19 = f32[32,128]{1,0:T(8,128)S(1)} collective-permute-done((f32[32,128]{1,0:T(8,128)S(1)}, f32[32,128]{1,0:T(8,128)S(1)}, u32[]{:S(2)}, u32[]{:S(2)}) %collective-permute-start.19) | collective-permute-done | bytes 16416 | tf_op jit(solution)/shard_map/ppermute | solution.py:312
  66.3 0.9 %collective-permute-done.18 = f32[32,128]{1,0:T(8,128)S(1)} collective-permute-done((f32[32,128]{1,0:T(8,128)S(1)}, f32[32,128]{1,0:T(8,128)S(1)}, u32[]{:S(2)}, u32[]{:S(2)}) %collective-permute-start.18) | collective-permute-done | bytes 16416 | tf_op jit(solution)/shard_map/ppermute | solution.py:312
  67.2 1.8 %shard_map.67 = (f32[32,512]{1,0:T(8,128)}, f32[4,32,32]{2,1,0:T(8,128)}) custom-call(f32[32,128]{1,0:T(8,128)S(1)} %add_add_fusion.share_ref, f32[32,512]{1,0:T(8,128)S(1)} %get-tuple-element.82.basis_ref, f32[32,512]{1,0:T(8,128)S(1)} %get-tuple-element.83.result_ref), custom_call_target="tpu_custom_call" | custom-call | flops 1 | bytes 1 | tf_op jit(solution)/shard_map/pallas_call | solution.py:295
  (54 shorter events, 2.1 us)
Async XLA Ops:
  4.9 12.0 %copy-start = (f32[512,512]{1,0:T(8,128)S(1)}, f32[512,512]{1,0:T(8,128)}, u32[]{:S(2)}) copy-start(f32[512,512]{1,0:T(8,128)} %diagonal_ref.1) | copy-start | bytes 3145732
  4.9 2.0 %collective-permute-start = (f32[232,512]{1,0:T(8,128)S(1)}, f32[232,512]{1,0:T(8,128)S(1)}, u32[]{:S(2)}, u32[]{:S(2)}) collective-permute-start(f32[232,512]{1,0:T(8,128)S(1)} %get-tuple-element.46.bundle_ref.start_ref), channel_id=1, source_target_pairs={{1,0},{0,1},{3,2},{2,3},{5,4},{4,5},{7,6},{6,7},{9,8},{8,9},{11,10... | collective-permute-start | bytes 1425416 | tf_op jit(solution)/shard_map/ppermute | solution.py:312
  7.1 19.9 %collective-permute-start.3 = (f32[72,512]{1,0:T(8,128)S(1)}, f32[72,512]{1,0:T(8,128)S(1)}, u32[]{:S(2)}, u32[]{:S(2)}) collective-permute-start(f32[72,512]{1,0:T(8,128)S(1)} %get-tuple-element.105), channel_id=1, source_target_pairs={{6,0},{11,1},{8,2},{13,3},{10,4},{15,5},{12,6},{1,7},{14,8},{3,9},... | collective-permute-start | bytes 442376 | tf_op jit(solution)/shard_map/ppermute | solution.py:317
  12.1 14.9 %collective-permute-start.2 = (f32[72,512]{1,0:T(8,128)S(1)}, f32[72,512]{1,0:T(8,128)S(1)}, u32[]{:S(2)}, u32[]{:S(2)}) collective-permute-start(f32[72,512]{1,0:T(8,128)S(1)} %get-tuple-element.106), channel_id=1, source_target_pairs={{14,0},{13,1},{0,2},{15,3},{2,4},{1,5},{4,6},{3,7},{6,8},{5,9},{8,... | collective-permute-start | bytes 442376 | tf_op jit(solution)/shard_map/ppermute | solution.py:317
  13.6 13.4 %collective-permute-start.1 = (f32[72,512]{1,0:T(8,128)S(1)}, f32[72,512]{1,0:T(8,128)S(1)}, u32[]{:S(2)}, u32[]{:S(2)}) collective-permute-start(f32[72,512]{1,0:T(8,128)S(1)} %get-tuple-element.107.pair_ref), channel_id=1, source_target_pairs={{2,0},{5,1},{4,2},{7,3},{6,4},{9,5},{8,6},{11,7},{10,8},{13,9},{12... | collective-permute-start | bytes 442376 | tf_op jit(solution)/shard_map/ppermute | solution.py:317
  16.8 10.1 %collective-permute-start.4 = (f32[40,512]{1,0:T(8,128)S(1)}, f32[40,512]{1,0:T(8,128)S(1)}, u32[]{:S(2)}, u32[]{:S(2)}) collective-permute-start(f32[40,512]{1,0:T(8,128)S(1)} %pad_maximum_fusion.8), channel_id=1, source_target_pairs={{8,0},{9,1},{10,2},{11,3},{12,4},{13,5},{14,6},{15,7},{0,8},{1,9},... | collective-permute-start | bytes 245768 | tf_op jit(solution)/shard_map/ppermute | solution.py:317
  27.1 1.3 %collective-permute-start.6 = (f32[40,512]{1,0:T(8,128)S(1)}, f32[40,512]{1,0:T(8,128)S(1)}, u32[]{:S(2)}, u32[]{:S(2)}) collective-permute-start(f32[40,512]{1,0:T(8,128)S(1)} %pad_maximum_fusion.9), channel_id=1, source_target_pairs={{1,0},{0,1},{3,2},{2,3},{5,4},{4,5},{7,6},{6,7},{9,8},{8,9},{11,10... | collective-permute-start | bytes 245768 | tf_op jit(solution)/shard_map/ppermute | solution.py:312
  27.2 1.8 %collective-permute-start.5 = (f32[160,512]{1,0:T(8,128)S(1)}, f32[160,512]{1,0:T(8,128)S(1)}, u32[]{:S(2)}, u32[]{:S(2)}) collective-permute-start(f32[160,512]{1,0:T(8,128)S(1)} %pad_maximum_fusion.mine_ref), channel_id=1, source_target_pairs={{1,0},{0,1},{3,2},{2,3},{5,4},{4,5},{7,6},{6,7},{9,8},{8,9},{11,10... | collective-permute-start | bytes 983048 | tf_op jit(solution)/shard_map/ppermute | solution.py:312
  32.6 1.9 %collective-permute-start.7 = (f32[232,512]{1,0:T(8,128)S(1)}, f32[232,512]{1,0:T(8,128)S(1)}, u32[]{:S(2)}, u32[]{:S(2)}) collective-permute-start(f32[232,512]{1,0:T(8,128)S(1)} %get-tuple-element.65.bundle_ref.message_ref), channel_id=1, source_target_pairs={{1,0},{0,1},{3,2},{2,3},{5,4},{4,5},{7,6},{6,7},{9,8},{8,9},{11,10... | collective-permute-start | bytes 1425416 | tf_op jit(solution)/shard_map/ppermute | solution.py:312
  34.7 16.3 %collective-permute-start.10 = (f32[72,512]{1,0:T(8,128)S(1)}, f32[72,512]{1,0:T(8,128)S(1)}, u32[]{:S(2)}, u32[]{:S(2)}) collective-permute-start(f32[72,512]{1,0:T(8,128)S(1)} %get-tuple-element.102), channel_id=1, source_target_pairs={{6,0},{11,1},{8,2},{13,3},{10,4},{15,5},{12,6},{1,7},{14,8},{3,9},... | collective-permute-start | bytes 442376 | tf_op jit(solution)/shard_map/ppermute | solution.py:317
  35.4 15.6 %collective-permute-start.9 = (f32[72,512]{1,0:T(8,128)S(1)}, f32[72,512]{1,0:T(8,128)S(1)}, u32[]{:S(2)}, u32[]{:S(2)}) collective-permute-start(f32[72,512]{1,0:T(8,128)S(1)} %get-tuple-element.103), channel_id=1, source_target_pairs={{14,0},{13,1},{0,2},{15,3},{2,4},{1,5},{4,6},{3,7},{6,8},{5,9},{8,... | collective-permute-start | bytes 442376 | tf_op jit(solution)/shard_map/ppermute | solution.py:317
  38.0 13.0 %collective-permute-start.8 = (f32[72,512]{1,0:T(8,128)S(1)}, f32[72,512]{1,0:T(8,128)S(1)}, u32[]{:S(2)}, u32[]{:S(2)}) collective-permute-start(f32[72,512]{1,0:T(8,128)S(1)} %get-tuple-element.104.pair_ref), channel_id=1, source_target_pairs={{2,0},{5,1},{4,2},{7,3},{6,4},{9,5},{8,6},{11,7},{10,8},{13,9},{12... | collective-permute-start | bytes 442376 | tf_op jit(solution)/shard_map/ppermute | solution.py:317
  40.2 10.9 %collective-permute-start.11 = (f32[40,512]{1,0:T(8,128)S(1)}, f32[40,512]{1,0:T(8,128)S(1)}, u32[]{:S(2)}, u32[]{:S(2)}) collective-permute-start(f32[40,512]{1,0:T(8,128)S(1)} %pad_maximum_fusion.10), channel_id=1, source_target_pairs={{8,0},{9,1},{10,2},{11,3},{12,4},{13,5},{14,6},{15,7},{0,8},{1,9},... | collective-permute-start | bytes 245768 | tf_op jit(solution)/shard_map/ppermute | solution.py:317
  51.2 1.3 %collective-permute-start.13 = (f32[40,512]{1,0:T(8,128)S(1)}, f32[40,512]{1,0:T(8,128)S(1)}, u32[]{:S(2)}, u32[]{:S(2)}) collective-permute-start(f32[40,512]{1,0:T(8,128)S(1)} %pad_maximum_fusion.11), channel_id=1, source_target_pairs={{1,0},{0,1},{3,2},{2,3},{5,4},{4,5},{7,6},{6,7},{9,8},{8,9},{11,10... | collective-permute-start | bytes 245768 | tf_op jit(solution)/shard_map/ppermute | solution.py:312
  51.3 1.8 %collective-permute-start.12 = (f32[160,512]{1,0:T(8,128)S(1)}, f32[160,512]{1,0:T(8,128)S(1)}, u32[]{:S(2)}, u32[]{:S(2)}) collective-permute-start(f32[160,512]{1,0:T(8,128)S(1)} %pad_maximum_fusion.1.mine_ref), channel_id=1, source_target_pairs={{1,0},{0,1},{3,2},{2,3},{5,4},{4,5},{7,6},{6,7},{9,8},{8,9},{11,10... | collective-permute-start | bytes 983048 | tf_op jit(solution)/shard_map/ppermute | solution.py:312
  56.8 3.2 %collective-permute-start.16 = (f32[32,128]{1,0:T(8,128)S(1)}, f32[32,128]{1,0:T(8,128)S(1)}, u32[]{:S(2)}, u32[]{:S(2)}) collective-permute-start(f32[32,128]{1,0:T(8,128)S(1)} %get-tuple-element.81), channel_id=1, source_target_pairs={{3,0},{2,1},{1,2},{0,3},{7,4},{6,5},{5,6},{4,7},{11,8},{10,9},{9,1... | collective-permute-start | bytes 49160 | tf_op jit(solution)/shard_map/ppermute | solution.py:312
  56.8 3.9 %collective-permute-start.15 = (f32[32,128]{1,0:T(8,128)S(1)}, f32[32,128]{1,0:T(8,128)S(1)}, u32[]{:S(2)}, u32[]{:S(2)}) collective-permute-start(f32[32,128]{1,0:T(8,128)S(1)} %get-tuple-element.81), channel_id=1, source_target_pairs={{2,0},{3,1},{0,2},{1,3},{6,4},{7,5},{4,6},{5,7},{10,8},{11,9},{8,1... | collective-permute-start | bytes 49160 | tf_op jit(solution)/shard_map/ppermute | solution.py:312
  58.8 1.9 %collective-permute-start.14 = (f32[32,128]{1,0:T(8,128)S(1)}, f32[32,128]{1,0:T(8,128)S(1)}, u32[]{:S(2)}, u32[]{:S(2)}) collective-permute-start(f32[32,128]{1,0:T(8,128)S(1)} %get-tuple-element.81), channel_id=1, source_target_pairs={{1,0},{0,1},{3,2},{2,3},{5,4},{4,5},{7,6},{6,7},{9,8},{8,9},{11,10... | collective-permute-start | bytes 49160 | tf_op jit(solution)/shard_map/ppermute | solution.py:312
  60.7 5.6 %collective-permute-start.19 = (f32[32,128]{1,0:T(8,128)S(1)}, f32[32,128]{1,0:T(8,128)S(1)}, u32[]{:S(2)}, u32[]{:S(2)}) collective-permute-start(f32[32,128]{1,0:T(8,128)S(1)} %add_add_fusion.1), channel_id=1, source_target_pairs={{12,0},{13,1},{14,2},{15,3},{8,4},{9,5},{10,6},{11,7},{4,8},{5,9},... | collective-permute-start | bytes 49160 | tf_op jit(solution)/shard_map/ppermute | solution.py:312
  62.6 4.6 %collective-permute-start.18 = (f32[32,128]{1,0:T(8,128)S(1)}, f32[32,128]{1,0:T(8,128)S(1)}, u32[]{:S(2)}, u32[]{:S(2)}) collective-permute-start(f32[32,128]{1,0:T(8,128)S(1)} %add_add_fusion.1), channel_id=1, source_target_pairs={{8,0},{9,1},{10,2},{11,3},{12,4},{13,5},{14,6},{15,7},{0,8},{1,9},... | collective-permute-start | bytes 49160 | tf_op jit(solution)/shard_map/ppermute | solution.py:312
  63.2 4.0 %collective-permute-start.17 = (f32[32,128]{1,0:T(8,128)S(1)}, f32[32,128]{1,0:T(8,128)S(1)}, u32[]{:S(2)}, u32[]{:S(2)}) collective-permute-start(f32[32,128]{1,0:T(8,128)S(1)} %add_add_fusion.1), channel_id=1, source_target_pairs={{4,0},{5,1},{6,2},{7,3},{0,4},{1,5},{2,6},{3,7},{12,8},{13,9},{14,... | collective-permute-start | bytes 49160 | tf_op jit(solution)/shard_map/ppermute | solution.py:312

commit v5 on v4

--- a/solution.py
+++ b/solution.py
@@ -11,6 +11,7 @@
 SIDE = 128
 PAD = 8
 SLOTS = 6
+NOTES = 2
 
 precise = lax.Precision.HIGHEST
 in_vmem = pl.BlockSpec(memory_space=pltpu.VMEM)
@@ -93,16 +94,29 @@
     return jnp.concatenate(lower, axis=0), jnp.concatenate(inverse, axis=0)
 
 
-def pack(ref, base, place, matrix):
-    side = matrix.shape[0]
-    for q in range(side // PAD):
-        start = SIDE * place + side * q
-        ref[base : base + PAD, start : start + side] = matrix[PAD * q : PAD * q + PAD]
-
-
-def unpack(ref, place, side):
-    starts = [SIDE * place + side * q for q in range(side // PAD)]
-    return jnp.concatenate([ref[:, s : s + side] for s in starts], axis=0)
+def pack(matrix):
+    return jnp.concatenate([matrix[q : q + PAD] for q in range(0, matrix.shape[0], PAD)], axis=1)
+
+
+def unpack(tile, side):
+    return jnp.concatenate([tile[:, q : q + side] for q in range(0, SIDE, side)], axis=0)
+
+
+def join(tiles, wide):
+    rows = [jnp.concatenate([tiles[q + j] for j in range(wide)], axis=1) for q in range(0, tiles.shape[0], wide)]
+    return jnp.concatenate(rows, axis=0)
+
+
+def put(ref, base, block):
+    wide = block.shape[1] // SIDE
+    for i in range(block.shape[0] // PAD):
+        for j in range(wide):
+            ref[base + wide * i + j] = block[PAD * i : PAD * i + PAD, SIDE * j : SIDE * j + SIDE]
+
+
+def block_of(ref, shape):
+    rows, order = shape
+    return join(ref[: rows * order // (PAD * SIDE)], order // SIDE)
 
 
 def place_of(columns_ref, e):
@@ -114,10 +128,10 @@
 
 
 def place_products(columns_ref, products_ref, bundle_ref, keep_ref):
-    rows = products_ref.shape[1]
-    start = rows + PAD
+    size = keep_ref.shape[0] // SLOTS
+    start = size + NOTES
     keep_ref[...] = jnp.zeros_like(keep_ref)
-    bundle_ref[start:] = jnp.zeros((bundle_ref.shape[0] - start, bundle_ref.shape[1]), jnp.float32)
+    bundle_ref[start:] = jnp.zeros_like(keep_ref)
     for e in range(products_ref.shape[0]):
         core, chip, block = place_of(columns_ref, e)
         speaker = jnp.where(chip == 1, 0, 1)
@@ -125,11 +139,11 @@
 
         @pl.when(speaker == core)
         def _():
-            keep_ref[slot] = products_ref[e]
+            put(keep_ref, slot * size, products_ref[e])
 
         @pl.when(speaker != core)
         def _():
-            bundle_ref[pl.ds(pl.multiple_of(start + slot * rows, PAD), rows)] = products_ref[e]
+            put(bundle_ref, start + slot * size, products_ref[e])
 
 
 def begin_kernel(
@@ -151,15 +165,16 @@
     copies[0].wait()
     signs = (2 * probes_ref[...] - 1).astype(jnp.float32) * SCALE
     rows, order = signs.shape
-    bundle_ref[:rows] = signs
+    size = rows * order // (PAD * SIDE)
+    put(bundle_ref, 0, signs)
     square = lax.broadcasted_iota(jnp.int32, (SIDE, SIDE), 0) == lax.broadcasted_iota(jnp.int32, (SIDE, SIDE), 1)
     trace = jnp.zeros((SIDE, SIDE), jnp.float32)
     for q in range(squares):
         copies[1 + q].wait()
         trace += jnp.where(square, diagonal_ref[q], 0.0) * (1.0 / order)
     trace = jnp.sum(jnp.sum(trace, axis=0, keepdims=True), axis=1, keepdims=True)
-    bundle_ref[rows : rows + PAD] = jnp.broadcast_to(trace, (PAD, order))
-    pack(bundle_ref, rows, 0, mm_t(signs, signs))
+    bundle_ref[size] = pack(mm_t(signs, signs))
+    bundle_ref[size + 1] = jnp.broadcast_to(trace, (PAD, SIDE))
     exact = (signs.astype(jnp.bfloat16), None)
     for e in range(tiles):
         copies[1 + squares + e].wait()
@@ -174,33 +189,33 @@
     bundle_ref, diagonal_ref, tile_high_ref, tile_low_ref, image_ref, high_ref, low_ref, turned_high_ref, turned_low_ref
 ):
     rows, order = image_ref.shape
-    trace = bundle_ref[rows : rows + 1, SIDE : SIDE + 1]
+    trace = bundle_ref[rows * order // (PAD * SIDE) + 1, 0:1, 0:1]
     line = lax.broadcasted_iota(jnp.int32, (order, order), 0) == lax.broadcasted_iota(jnp.int32, (order, order), 1)
     high, low = halves(diagonal_ref[...] - jnp.where(line, trace, 0.0))
     high_ref[...] = high
     low_ref[...] = low
-    image_ref[...] = split_product(parts_of(bundle_ref[:rows], True), high, low, 0)
+    image_ref[...] = split_product(parts_of(block_of(bundle_ref, image_ref.shape), True), high, low, 0)
     for e in range(tile_high_ref.shape[0]):
         turned_high_ref[e] = tile_high_ref[e].T
         turned_low_ref[e] = tile_low_ref[e].T
 
 
 def second_near_kernel(bundle_ref, high_ref, low_ref, image_ref):
-    rows = image_ref.shape[0]
-    image_ref[...] = split_product(parts_of(bundle_ref[:rows], False), high_ref[...], low_ref[...], 0)
+    image_ref[...] = split_product(parts_of(block_of(bundle_ref, image_ref.shape), False), high_ref[...], low_ref[...], 0)
 
 
 def incoming_kernel(exact, columns_ref, pair_ref, mine_ref, theirs_ref, high_ref, low_ref, image_ref, ready_ref):
-    rows = image_ref.shape[0]
+    rows, order = image_ref.shape
+    size = rows * order // (PAD * SIDE)
     tiles = high_ref.shape[0]
     for e in range(tiles):
         core, chip, block = place_of(columns_ref, e)
         speaker = jnp.where(chip == 2, 1, 0)
         part = jnp.where(chip < 3, 0, 2 * chip - 4)
-        start = pl.multiple_of((part + block) * rows, rows)
-        inside = pl.multiple_of(block * rows, rows)
-        met = jnp.where(speaker == core, mine_ref[pl.ds(start, rows)], theirs_ref[pl.ds(start, rows)])
-        met = jnp.where(chip == 0, pair_ref[pl.ds(inside, rows)], met)
+        met = jnp.where(
+            speaker == core, mine_ref[pl.ds((part + block) * size, size)], theirs_ref[pl.ds((part + block) * size, size)]
+        )
+        met = join(jnp.where(chip == 0, pair_ref[pl.ds(block * size, size)], met), order // SIDE)
         high, low = parts_of(met, exact)
         ready_ref[e, :rows] = high
         if not exact:
@@ -212,9 +227,9 @@
     image_ref[...] = image
 
 
-def shift_of(devices, start_ref, sums_ref, rows):
-    mean = sums_ref[0:1, SIDE : SIDE + 1] * (1.0 / devices)
-    return mean, start_ref[rows : rows + 1, SIDE : SIDE + 1] - mean
+def shift_of(devices, start_ref, sums_ref, size):
+    mean = sums_ref[1, 0:1, 0:1] * (1.0 / devices)
+    return mean, start_ref[size + 1, 0:1, 0:1] - mean
 
 
 def first_kernel(
@@ -222,25 +237,26 @@
     bundle_ref, keep_ref, products_ref,
 ):
     rows, order = image_ref.shape
-    signs = start_ref[:rows]
-    image = near_ref[...] + image_ref[...] + total_ref[...]
-    image += shift_of(devices, start_ref, sums_ref, rows)[1] * signs
-    bundle_ref[:rows] = image
+    size = rows * order // (PAD * SIDE)
+    signs = block_of(start_ref, image_ref.shape)
+    image = near_ref[...] + image_ref[...] + join(total_ref[...], order // SIDE)
+    image += shift_of(devices, start_ref, sums_ref, size)[1] * signs
+    put(bundle_ref, 0, image)
     vectors = halves(image)
     for e in range(high_ref.shape[0]):
         products_ref[e] = split_product(vectors, high_ref[e], low_ref[e], 0)
     both = mm_t(jnp.concatenate([signs, image], axis=0), image)
-    bundle_ref[rows : rows + PAD] = jnp.zeros((PAD, order), jnp.float32)
-    pack(bundle_ref, rows, 0, both[:rows])
-    pack(bundle_ref, rows, 1, both[rows:])
+    bundle_ref[size] = pack(both[:rows])
+    bundle_ref[size + 1] = pack(both[rows:])
     place_products(columns_ref, products_ref, bundle_ref, keep_ref)
 
 
 def root_kernel(sums_ref, start_ref, message_ref, root_ref, lines_ref):
     rows = root_ref.shape[0]
-    root = factor(unpack(sums_ref, 0, rows))[1]
+    shape = rows, lines_ref.shape[1] // 2
+    root = factor(unpack(sums_ref[0], rows))[1]
     root_ref[...] = root
-    lines_ref[...] = mm(root, jnp.concatenate([start_ref[:rows], message_ref[:rows]], axis=1))
+    lines_ref[...] = mm(root, jnp.concatenate([block_of(start_ref, shape), block_of(message_ref, shape)], axis=1))
 
 
 def second_kernel(
@@ -248,11 +264,12 @@
     basis_ref, result_ref, share_ref,
 ):
     rows, order = image_ref.shape
-    mean, shift = shift_of(devices, start_ref, first_sums_ref, rows)
+    mean, shift = shift_of(devices, start_ref, first_sums_ref, rows * order // (PAD * SIDE))
     root = root_ref[...]
-    alpha = mm_t(mm(root, unpack(sums_ref, 0, rows)), root)
-    gram = mm_t(mm(root, unpack(sums_ref, 1, rows)), root) - mm_t(alpha, alpha)
-    image = mm(root, near_ref[...] + image_ref[...] + total_ref[...] + shift * message_ref[:rows])
+    alpha = mm_t(mm(root, unpack(sums_ref[0], rows)), root)
+    gram = mm_t(mm(root, unpack(sums_ref[1], rows)), root) - mm_t(alpha, alpha)
+    image = near_ref[...] + image_ref[...] + join(total_ref[...], order // SIDE)
+    image = mm(root, image + shift * block_of(message_ref, image_ref.shape))
     first_basis, first = lines_ref[:, :order], lines_ref[:, order:]
     bent = mm(alpha, lines_ref[...])
     beta, inverse = factor(gram)
@@ -325,14 +342,14 @@
 
     def apply(bundle, keep, near_call, exact):
         partner = swapped(bundle)
-        own, its = bundle[:rows], partner[:rows]
-        payload = bundle[rows:top] + partner[rows:top]
+        own, its = bundle[:size], partner[:size]
+        payload = bundle[size:top] + partner[size:top]
         pair = jnp.concatenate([jnp.where(lower, own, its), jnp.where(lower, its, own), payload])
-        ahead = keep + partner[top:].reshape(keep.shape)
-        near_ahead = jnp.concatenate([ahead[0], ahead[1], payload])
-        third_ahead = jnp.concatenate([ahead[2], ahead[3]])
-        third_ahead = jnp.concatenate([jnp.where(both_lower, pair[: 2 * rows], third_ahead), payload])
-        fourth_ahead = jnp.concatenate([jnp.where(lower, pair[:rows], ahead[4]), payload])
+        ahead = keep + partner[top:]
+        near_ahead = jnp.concatenate([ahead[: 2 * size], payload])
+        third_ahead = jnp.where(both_lower, pair[: 2 * size], ahead[2 * size : 4 * size])
+        third_ahead = jnp.concatenate([third_ahead, payload])
+        fourth_ahead = jnp.concatenate([jnp.where(lower, pair[:size], ahead[4 * size : 5 * size]), payload])
         near = from_chips(pair, 1, 2)
         near_back = from_chips(near_ahead, -1, -2)
         third = from_chips(third_ahead, 3, -3)
@@ -342,14 +359,14 @@
         near, near_back, third, fourth, inner, turned = lax.optimization_barrier(
             (near, near_back, third, fourth, inner, turned)
         )
-        mine = jnp.concatenate([near[: 2 * rows], third[: 2 * rows], fourth[:rows]])
+        mine = jnp.concatenate([near[: 2 * size], third[: 2 * size], fourth[:size]])
         if devices == 16:
-            sums = near[2 * rows :] + near_back[2 * rows :] + third[2 * rows :]
-            sums = sums + jnp.where(lower_pad, payload + fourth[rows:], 0.0)
+            sums = near[2 * size :] + near_back[2 * size :] + third[2 * size :]
+            sums = sums + jnp.where(lower_notes, payload + fourth[size:], 0.0)
         else:
-            sums = jnp.where(lower_pad, whole(payload), 0.0)
-        first = near_back[:rows] + jnp.where(lower, 0.0, third[:rows] + fourth[:rows])
-        second = near_back[rows : 2 * rows] + jnp.where(lower, 0.0, third[rows : 2 * rows] + ahead[SLOTS - 1])
+            sums = jnp.where(lower_notes, whole(payload), 0.0)
+        first = near_back[:size] + jnp.where(lower, 0.0, third[:size] + fourth[:size])
+        second = near_back[size : 2 * size] + jnp.where(lower, 0.0, third[size : 2 * size] + ahead[5 * size :])
         other = jnp.concatenate([jnp.where(lower, second, first), sums])
         mine, other = lax.optimization_barrier((mine, other))
         theirs, other = swapped(mine), swapped(other)
@@ -360,17 +377,18 @@
             smem=1,
             scratch=(pltpu.VMEM((tiles, 2 * rows, order), jnp.bfloat16),),
         )
-        return inner, image, jnp.where(lower, first, second) + other[:rows], sums + other[rows:], turned
+        return inner, image, jnp.where(lower, first, second) + other[:size], sums + other[size:], turned
 
     tiles = forward.shape[0]
-    top = rows + PAD
-    bundles = (struct(top + SLOTS * rows, order), struct(SLOTS, rows, order))
+    size = rows * order // (PAD * SIDE)
+    top = size + NOTES
+    bundles = (struct(top + SLOTS * size, PAD, SIDE), struct(SLOTS * size, PAD, SIDE))
     products = pltpu.VMEM((tiles, rows, order), jnp.float32)
     split = pltpu.VMEM(forward.shape, jnp.bfloat16)
     split_diagonal = pltpu.VMEM(diagonal.shape, jnp.bfloat16)
     start, core, keep, high, low = call(
         begin_kernel,
-        (bundles[0], pltpu.VMEM((rows, order), jnp.int32), bundles[1], split, split),
+        (bundles[0], pltpu.VMEM((size, PAD, SIDE), jnp.int32), bundles[1], split, split),
         (tile_columns, probes, diagonal, forward),
         smem=1,
         hbm=3,
@@ -384,7 +402,7 @@
         ),
     )
     lower = core == 0
-    lower_pad = lower[:PAD]
+    lower_notes = lower[:NOTES]
     both_lower = jnp.concatenate([lower, lower])
 
     def first_near(bundle):

time: 69.2 us -> 67.1 us (0.970)
  waiting for transfers between devices: 27.5 us -> 25.7 us
    ppermute x8, waiting for transfers between devices: 18.2 us -> 16.4 us  [from_chips(): return lax.ppermute(block, 'col', route)]
where the time goes in v5:
time: 67.1 us; the launch traced here: 66.9 us
  waiting for transfers between devices  25.7 us (38%)
  starting transfers between devices  23.8 us (35%)
  Pallas kernels  16 us (24%)
  between operations  0.88 us (1%)
    ppermute x8, waiting for transfers between devices, from_chips(): return lax.ppermute(block, 'col', route)  16.4 us
    pallas_call x9, Pallas kernels, call(): pl.pallas_call(kernel, out_shape=out_shape, in_specs=[in_smem] * smem + [...  16 us
    ppermute x8, starting transfers between devices, from_chips(): return lax.ppermute(block, 'col', route)  15.2 us
    ppermute x12, waiting for transfers between devices, swapped(): return lax.ppermute(block, 'col', [(i ^ bits, i) for i in range(devices)])  9.32 us
    ppermute x12, starting transfers between devices, swapped(): return lax.ppermute(block, 'col', [(i ^ bits, i) for i in range(devices)])  8.56 us
  transfers between devices with their start and end apart: 20, of which 12 were waited for; matrix products, arithmetic and copies ran while one was open for 0% of the time, Pallas kernels for 4%

profile of v5, /device:TPU:0, one launch (start us, length us, event | category | flops | bytes accessed | tf_op | source)
XLA Modules:
  0.0 66.9 jit_solution(2875192269336532232)
XLA Ops:
  0.6 4.3 %shard_map.59 = (f32[114,8,128]{2,1,0:T(8,128)S(1)}, s32[16,8,128]{2,1,0:T(8,128)S(1)}, f32[96,8,128]{2,1,0:T(8,128)S(1)}, bf16[5,512,512]{2,1,0:T(8,128)(2,1)S(1)}, bf16[5,512,512]{2,1,0:T(8,128)(2,1)S(1)}) custom-call(s32[1,5]{1,0:T(1,128)} %columns_ref.7, s32[32,512]{1,0:T(8,128)} %probes_hbm.1, f32[512,512]{1,0:T(8,128)} %diagonal_ref.1, ...), custom_call_target="tpu_custom_call" | custom-call | flops 1 | bytes 1 | tf_op jit(solution)/shard_map/pallas_call | solution.py:312
  4.9 0.5 collective-permute-start
  5.4 1.5 %collective-permute-done = f32[114,8,128]{2,1,0:T(8,128)S(1)} collective-permute-done((f32[114,8,128]{2,1,0:T(8,128)S(1)}, f32[114,8,128]{2,1,0:T(8,128)S(1)}, u32[]{:S(2)}, u32[]{:S(2)}) %collective-permute-start) | collective-permute-done | bytes 466976 | tf_op jit(solution)/shard_map/ppermute | solution.py:329
  7.0 5.0 %collective-permute-start.3 = (f32[34,8,128]{2,1,0:T(8,128)S(1)}, f32[34,8,128]{2,1,0:T(8,128)S(1)}, u32[]{:S(2)}, u32[]{:S(2)}) collective-permute-start(f32[34,8,128]{2,1,0:T(8,128)S(1)} %get-tuple-element.101), channel_id=1, source_target_pairs={{6,0},{11,1},{8,2},{13,3},{10,4},{15,5},{12,6},{1,7},{14,8},{3,9},... | collective-permute-start | bytes 417800 | tf_op jit(solution)/shard_map/ppermute | solution.py:334
  12.0 1.5 %collective-permute-start.2 = (f32[34,8,128]{2,1,0:T(8,128)S(1)}, f32[34,8,128]{2,1,0:T(8,128)S(1)}, u32[]{:S(2)}, u32[]{:S(2)}) collective-permute-start(f32[34,8,128]{2,1,0:T(8,128)S(1)} %get-tuple-element.102), channel_id=1, source_target_pairs={{14,0},{13,1},{0,2},{15,3},{2,4},{1,5},{4,6},{3,7},{6,8},{5,9},{8,... | collective-permute-start | bytes 417800 | tf_op jit(solution)/shard_map/ppermute | solution.py:334
  13.5 3.2 %collective-permute-start.1 = (f32[34,8,128]{2,1,0:T(8,128)S(1)}, f32[34,8,128]{2,1,0:T(8,128)S(1)}, u32[]{:S(2)}, u32[]{:S(2)}) collective-permute-start(f32[34,8,128]{2,1,0:T(8,128)S(1)} %get-tuple-element.103.pair_ref), channel_id=1, source_target_pairs={{2,0},{5,1},{4,2},{7,3},{6,4},{9,5},{8,6},{11,7},{10,8},{13,9},{12... | collective-permute-start | bytes 417800 | tf_op jit(solution)/shard_map/ppermute | solution.py:334
  16.8 1.5 %shard_map.60 = (f32[32,512]{1,0:T(8,128)S(1)}, bf16[512,512]{1,0:T(8,128)(2,1)S(1)}, bf16[512,512]{1,0:T(8,128)(2,1)S(1)}, bf16[5,512,512]{2,1,0:T(8,128)(2,1)S(1)}, bf16[5,512,512]{2,1,0:T(8,128)(2,1)S(1)}) custom-call(f32[114,8,128]{2,1,0:T(8,128)S(1)} %get-tuple-element.46.bundle_ref.start_ref, f32[512,512]{1,0:T(8,128)S(1)} %copy-done, ...), custom_call_target="tpu_custom_call" | custom-call | flops 1 | bytes 1 | tf_op jit(solution)/shard_map/pallas_call | solution.py:312
  18.3 7.7 %collective-permute-done.4 = f32[18,8,128]{2,1,0:T(8,128)S(1)} collective-permute-done((f32[18,8,128]{2,1,0:T(8,128)S(1)}, f32[18,8,128]{2,1,0:T(8,128)S(1)}, u32[]{:S(2)}, u32[]{:S(2)}) %collective-permute-start.4) | collective-permute-done | bytes 73760 | tf_op jit(solution)/shard_map/ppermute | solution.py:334
  26.2 0.5 collective-permute-start.5
  26.7 0.8 %collective-permute-done.6 = f32[18,8,128]{2,1,0:T(8,128)S(1)} collective-permute-done((f32[18,8,128]{2,1,0:T(8,128)S(1)}, f32[18,8,128]{2,1,0:T(8,128)S(1)}, u32[]{:S(2)}, u32[]{:S(2)}) %collective-permute-start.6) | collective-permute-done | bytes 73760 | tf_op jit(solution)/shard_map/ppermute | solution.py:329
  28.0 1.7 %shard_map.61.image_ref = f32[32,512]{1,0:T(8,128)S(1)} custom-call(s32[1,5]{1,0:T(1,128)} %columns_ref.7, f32[34,8,128]{2,1,0:T(8,128)S(1)} %get-tuple-element.103.pair_ref, f32[80,8,128]{2,1,0:T(8,128)S(1)} %pad_maximum_fusion.mine_ref, f32[80,8,128]{2,1,0:T(8,128)S(1)} %collective-permute-done.5.theirs_ref, ...), custom_call_target="tpu_custom_call" | custom-call | flops 1 | bytes 1 | tf_op jit(solution)/shard_map/pallas_call | solution.py:312
  29.6 1.9 %shard_map.62 = (f32[114,8,128]{2,1,0:T(8,128)S(1)}, f32[96,8,128]{2,1,0:T(8,128)S(1)}) custom-call(s32[1,5]{1,0:T(1,128)} %columns_ref.7, f32[114,8,128]{2,1,0:T(8,128)S(1)} %get-tuple-element.46.bundle_ref.start_ref, f32[32,512]{1,0:T(8,128)S(1)} %get-tuple-element.54.near_ref, f32[32,512]{1,0:T(8,128)S(1)} %shard_map.61.image_ref, ...), custom_call_target="tpu_custom_call" | custom-call | flops 1 | bytes 1 | tf_op jit(solution)/shard_map/pallas_call | solution.py:312
  32.0 1.5 %collective-permute-done.7 = f32[114,8,128]{2,1,0:T(8,128)S(1)} collective-permute-done((f32[114,8,128]{2,1,0:T(8,128)S(1)}, f32[114,8,128]{2,1,0:T(8,128)S(1)}, u32[]{:S(2)}, u32[]{:S(2)}) %collective-permute-start.7) | collective-permute-done | bytes 466976 | tf_op jit(solution)/shard_map/ppermute | solution.py:329
  33.6 0.8 %collective-permute-start.10 = (f32[34,8,128]{2,1,0:T(8,128)S(1)}, f32[34,8,128]{2,1,0:T(8,128)S(1)}, u32[]{:S(2)}, u32[]{:S(2)}) collective-permute-start(f32[34,8,128]{2,1,0:T(8,128)S(1)} %get-tuple-element.98), channel_id=1, source_target_pairs={{6,0},{11,1},{8,2},{13,3},{10,4},{15,5},{12,6},{1,7},{14,8},{3,9},... | collective-permute-start | bytes 417800 | tf_op jit(solution)/shard_map/ppermute | solution.py:334
  34.4 2.5 %collective-permute-start.9 = (f32[34,8,128]{2,1,0:T(8,128)S(1)}, f32[34,8,128]{2,1,0:T(8,128)S(1)}, u32[]{:S(2)}, u32[]{:S(2)}) collective-permute-start(f32[34,8,128]{2,1,0:T(8,128)S(1)} %get-tuple-element.99), channel_id=1, source_target_pairs={{14,0},{13,1},{0,2},{15,3},{2,4},{1,5},{4,6},{3,7},{6,8},{5,9},{8,... | collective-permute-start | bytes 417800 | tf_op jit(solution)/shard_map/ppermute | solution.py:334
  36.9 2.2 %collective-permute-start.8 = (f32[34,8,128]{2,1,0:T(8,128)S(1)}, f32[34,8,128]{2,1,0:T(8,128)S(1)}, u32[]{:S(2)}, u32[]{:S(2)}) collective-permute-start(f32[34,8,128]{2,1,0:T(8,128)S(1)} %get-tuple-element.100.pair_ref), channel_id=1, source_target_pairs={{2,0},{5,1},{4,2},{7,3},{6,4},{9,5},{8,6},{11,7},{10,8},{13,9},{12... | collective-permute-start | bytes 417800 | tf_op jit(solution)/shard_map/ppermute | solution.py:334
  39.1 1.0 %shard_map.64 = (f32[32,32]{1,0:T(8,128)S(1)}, f32[32,1024]{1,0:T(8,128)S(1)}) custom-call(f32[2,8,128]{2,1,0:T(8,128)S(1)} %slice_add_fusion.8.sums_ref.first_sums_ref, f32[114,8,128]{2,1,0:T(8,128)S(1)} %get-tuple-element.46.bundle_ref.start_ref, f32[114,8,128]{2,1,0:T(8,128)S(1)} %get-tuple-element.65.bundle_ref.message_ref), custom_call_target="tpu_custom_call" | custom-call | flops 1 | bytes 1 | tf_op jit(solution)/shard_map/pallas_call | solution.py:312
  40.4 8.7 %collective-permute-done.11 = f32[18,8,128]{2,1,0:T(8,128)S(1)} collective-permute-done((f32[18,8,128]{2,1,0:T(8,128)S(1)}, f32[18,8,128]{2,1,0:T(8,128)S(1)}, u32[]{:S(2)}, u32[]{:S(2)}) %collective-permute-start.11) | collective-permute-done | bytes 73760 | tf_op jit(solution)/shard_map/ppermute | solution.py:334
  49.3 0.5 collective-permute-start.12
  49.8 0.8 %collective-permute-done.13 = f32[18,8,128]{2,1,0:T(8,128)S(1)} collective-permute-done((f32[18,8,128]{2,1,0:T(8,128)S(1)}, f32[18,8,128]{2,1,0:T(8,128)S(1)}, u32[]{:S(2)}, u32[]{:S(2)}) %collective-permute-start.13) | collective-permute-done | bytes 73760 | tf_op jit(solution)/shard_map/ppermute | solution.py:329
  50.6 0.5 collective-permute-done.12.theirs_ref
  51.0 1.7 %shard_map.65.image_ref = f32[32,512]{1,0:T(8,128)S(1)} custom-call(s32[1,5]{1,0:T(1,128)} %columns_ref.7, f32[34,8,128]{2,1,0:T(8,128)S(1)} %get-tuple-element.100.pair_ref, f32[80,8,128]{2,1,0:T(8,128)S(1)} %pad_maximum_fusion.1.mine_ref, f32[80,8,128]{2,1,0:T(8,128)S(1)} %collective-permute-done.12.theirs_ref, ...), custom_call_target="tpu_custom_call" | custom-call | flops 1 | bytes 1 | tf_op jit(solution)/shard_map/pallas_call | solution.py:312
  52.7 1.9 %shard_map.66 = (f32[32,512]{1,0:T(8,128)S(1)}, f32[32,512]{1,0:T(8,128)S(1)}, f32[32,128]{1,0:T(8,128)S(1)}) custom-call(f32[114,8,128]{2,1,0:T(8,128)S(1)} %get-tuple-element.46.bundle_ref.start_ref, f32[114,8,128]{2,1,0:T(8,128)S(1)} %get-tuple-element.65.bundle_ref.message_ref, f32[32,512]{1,0:T(8,128)S(1)} %shard_map.63.near_ref, ...), custom_call_target="tpu_custom_call" | custom-call | flops 1 | bytes 1 | tf_op jit(solution)/shard_map/pallas_call | solution.py:312
  54.7 2.0 %collective-permute-start.15 = (f32[32,128]{1,0:T(8,128)S(1)}, f32[32,128]{1,0:T(8,128)S(1)}, u32[]{:S(2)}, u32[]{:S(2)}) collective-permute-start(f32[32,128]{1,0:T(8,128)S(1)} %get-tuple-element.81), channel_id=1, source_target_pairs={{2,0},{3,1},{0,2},{1,3},{6,4},{7,5},{4,6},{5,7},{10,8},{11,9},{8,1... | collective-permute-start | bytes 49160 | tf_op jit(solution)/shard_map/ppermute | solution.py:329
  56.6 1.2 %collective-permute-done.16 = f32[32,128]{1,0:T(8,128)S(1)} collective-permute-done((f32[32,128]{1,0:T(8,128)S(1)}, f32[32,128]{1,0:T(8,128)S(1)}, u32[]{:S(2)}, u32[]{:S(2)}) %collective-permute-start.16) | collective-permute-done | bytes 16416 | tf_op jit(solution)/shard_map/ppermute | solution.py:329
  57.8 0.7 %collective-permute-done.15 = f32[32,128]{1,0:T(8,128)S(1)} collective-permute-done((f32[32,128]{1,0:T(8,128)S(1)}, f32[32,128]{1,0:T(8,128)S(1)}, u32[]{:S(2)}, u32[]{:S(2)}) %collective-permute-start.15) | collective-permute-done | bytes 16416 | tf_op jit(solution)/shard_map/ppermute | solution.py:329
  58.5 1.9 %collective-permute-start.19 = (f32[32,128]{1,0:T(8,128)S(1)}, f32[32,128]{1,0:T(8,128)S(1)}, u32[]{:S(2)}, u32[]{:S(2)}) collective-permute-start(f32[32,128]{1,0:T(8,128)S(1)} %add_add_fusion.1), channel_id=1, source_target_pairs={{12,0},{13,1},{14,2},{15,3},{8,4},{9,5},{10,6},{11,7},{4,8},{5,9},... | collective-permute-start | bytes 49160 | tf_op jit(solution)/shard_map/ppermute | solution.py:329
  60.4 0.7 %collective-permute-start.18 = (f32[32,128]{1,0:T(8,128)S(1)}, f32[32,128]{1,0:T(8,128)S(1)}, u32[]{:S(2)}, u32[]{:S(2)}) collective-permute-start(f32[32,128]{1,0:T(8,128)S(1)} %add_add_fusion.1), channel_id=1, source_target_pairs={{8,0},{9,1},{10,2},{11,3},{12,4},{13,5},{14,6},{15,7},{0,8},{1,9},... | collective-permute-start | bytes 49160 | tf_op jit(solution)/shard_map/ppermute | solution.py:329
  61.1 1.9 %collective-permute-start.17 = (f32[32,128]{1,0:T(8,128)S(1)}, f32[32,128]{1,0:T(8,128)S(1)}, u32[]{:S(2)}, u32[]{:S(2)}) collective-permute-start(f32[32,128]{1,0:T(8,128)S(1)} %add_add_fusion.1), channel_id=1, source_target_pairs={{4,0},{5,1},{6,2},{7,3},{0,4},{1,5},{2,6},{3,7},{12,8},{13,9},{14,... | collective-permute-start | bytes 49160 | tf_op jit(solution)/shard_map/ppermute | solution.py:329
  63.0 1.1 %collective-permute-done.19 = f32[32,128]{1,0:T(8,128)S(1)} collective-permute-done((f32[32,128]{1,0:T(8,128)S(1)}, f32[32,128]{1,0:T(8,128)S(1)}, u32[]{:S(2)}, u32[]{:S(2)}) %collective-permute-start.19) | collective-permute-done | bytes 16416 | tf_op jit(solution)/shard_map/ppermute | solution.py:329
  64.2 0.9 %collective-permute-done.18 = f32[32,128]{1,0:T(8,128)S(1)} collective-permute-done((f32[32,128]{1,0:T(8,128)S(1)}, f32[32,128]{1,0:T(8,128)S(1)}, u32[]{:S(2)}, u32[]{:S(2)}) %collective-permute-start.18) | collective-permute-done | bytes 16416 | tf_op jit(solution)/shard_map/ppermute | solution.py:329
  65.1 1.8 %shard_map.67 = (f32[32,512]{1,0:T(8,128)}, f32[4,32,32]{2,1,0:T(8,128)}) custom-call(f32[32,128]{1,0:T(8,128)S(1)} %add_add_fusion.share_ref, f32[32,512]{1,0:T(8,128)S(1)} %get-tuple-element.82.basis_ref, f32[32,512]{1,0:T(8,128)S(1)} %get-tuple-element.83.result_ref), custom_call_target="tpu_custom_call" | custom-call | flops 1 | bytes 1 | tf_op jit(solution)/shard_map/pallas_call | solution.py:312
  (50 shorter events, 2.0 us)
Async XLA Ops:
  4.9 11.9 %copy-start = (f32[512,512]{1,0:T(8,128)S(1)}, f32[512,512]{1,0:T(8,128)}, u32[]{:S(2)}) copy-start(f32[512,512]{1,0:T(8,128)} %diagonal_ref.1) | copy-start | bytes 3145732
  4.9 2.0 %collective-permute-start = (f32[114,8,128]{2,1,0:T(8,128)S(1)}, f32[114,8,128]{2,1,0:T(8,128)S(1)}, u32[]{:S(2)}, u32[]{:S(2)}) collective-permute-start(f32[114,8,128]{2,1,0:T(8,128)S(1)} %get-tuple-element.46.bundle_ref.start_ref), channel_id=1, source_target_pairs={{1,0},{0,1},{3,2},{2,3},{5,4},{4,5},{7,6},{6,7},{9,8},{8,9},{11,10... | collective-permute-start | bytes 1400840 | tf_op jit(solution)/shard_map/ppermute | solution.py:329
  7.0 19.0 %collective-permute-start.3 = (f32[34,8,128]{2,1,0:T(8,128)S(1)}, f32[34,8,128]{2,1,0:T(8,128)S(1)}, u32[]{:S(2)}, u32[]{:S(2)}) collective-permute-start(f32[34,8,128]{2,1,0:T(8,128)S(1)} %get-tuple-element.101), channel_id=1, source_target_pairs={{6,0},{11,1},{8,2},{13,3},{10,4},{15,5},{12,6},{1,7},{14,8},{3,9},... | collective-permute-start | bytes 417800 | tf_op jit(solution)/shard_map/ppermute | solution.py:334
  12.0 14.0 %collective-permute-start.2 = (f32[34,8,128]{2,1,0:T(8,128)S(1)}, f32[34,8,128]{2,1,0:T(8,128)S(1)}, u32[]{:S(2)}, u32[]{:S(2)}) collective-permute-start(f32[34,8,128]{2,1,0:T(8,128)S(1)} %get-tuple-element.102), channel_id=1, source_target_pairs={{14,0},{13,1},{0,2},{15,3},{2,4},{1,5},{4,6},{3,7},{6,8},{5,9},{8,... | collective-permute-start | bytes 417800 | tf_op jit(solution)/shard_map/ppermute | solution.py:334
  13.5 12.5 %collective-permute-start.1 = (f32[34,8,128]{2,1,0:T(8,128)S(1)}, f32[34,8,128]{2,1,0:T(8,128)S(1)}, u32[]{:S(2)}, u32[]{:S(2)}) collective-permute-start(f32[34,8,128]{2,1,0:T(8,128)S(1)} %get-tuple-element.103.pair_ref), channel_id=1, source_target_pairs={{2,0},{5,1},{4,2},{7,3},{6,4},{9,5},{8,6},{11,7},{10,8},{13,9},{12... | collective-permute-start | bytes 417800 | tf_op jit(solution)/shard_map/ppermute | solution.py:334
  16.7 9.3 %collective-permute-start.4 = (f32[18,8,128]{2,1,0:T(8,128)S(1)}, f32[18,8,128]{2,1,0:T(8,128)S(1)}, u32[]{:S(2)}, u32[]{:S(2)}) collective-permute-start(f32[18,8,128]{2,1,0:T(8,128)S(1)} %pad_maximum_fusion.8), channel_id=1, source_target_pairs={{8,0},{9,1},{10,2},{11,3},{12,4},{13,5},{14,6},{15,7},{0,8},{1,9},... | collective-permute-start | bytes 221192 | tf_op jit(solution)/shard_map/ppermute | solution.py:334
  26.2 1.3 %collective-permute-start.6 = (f32[18,8,128]{2,1,0:T(8,128)S(1)}, f32[18,8,128]{2,1,0:T(8,128)S(1)}, u32[]{:S(2)}, u32[]{:S(2)}) collective-permute-start(f32[18,8,128]{2,1,0:T(8,128)S(1)} %pad_maximum_fusion.9), channel_id=1, source_target_pairs={{1,0},{0,1},{3,2},{2,3},{5,4},{4,5},{7,6},{6,7},{9,8},{8,9},{11,10... | collective-permute-start | bytes 221192 | tf_op jit(solution)/shard_map/ppermute | solution.py:329
  26.2 1.8 %collective-permute-start.5 = (f32[80,8,128]{2,1,0:T(8,128)S(1)}, f32[80,8,128]{2,1,0:T(8,128)S(1)}, u32[]{:S(2)}, u32[]{:S(2)}) collective-permute-start(f32[80,8,128]{2,1,0:T(8,128)S(1)} %pad_maximum_fusion.mine_ref), channel_id=1, source_target_pairs={{1,0},{0,1},{3,2},{2,3},{5,4},{4,5},{7,6},{6,7},{9,8},{8,9},{11,10... | collective-permute-start | bytes 983048 | tf_op jit(solution)/shard_map/ppermute | solution.py:329
  31.6 1.9 %collective-permute-start.7 = (f32[114,8,128]{2,1,0:T(8,128)S(1)}, f32[114,8,128]{2,1,0:T(8,128)S(1)}, u32[]{:S(2)}, u32[]{:S(2)}) collective-permute-start(f32[114,8,128]{2,1,0:T(8,128)S(1)} %get-tuple-element.65.bundle_ref.message_ref), channel_id=1, source_target_pairs={{1,0},{0,1},{3,2},{2,3},{5,4},{4,5},{7,6},{6,7},{9,8},{8,9},{11,10... | collective-permute-start | bytes 1400840 | tf_op jit(solution)/shard_map/ppermute | solution.py:329
  33.6 15.4 %collective-permute-start.10 = (f32[34,8,128]{2,1,0:T(8,128)S(1)}, f32[34,8,128]{2,1,0:T(8,128)S(1)}, u32[]{:S(2)}, u32[]{:S(2)}) collective-permute-start(f32[34,8,128]{2,1,0:T(8,128)S(1)} %get-tuple-element.98), channel_id=1, source_target_pairs={{6,0},{11,1},{8,2},{13,3},{10,4},{15,5},{12,6},{1,7},{14,8},{3,9},... | collective-permute-start | bytes 417800 | tf_op jit(solution)/shard_map/ppermute | solution.py:334
  34.4 14.7 %collective-permute-start.9 = (f32[34,8,128]{2,1,0:T(8,128)S(1)}, f32[34,8,128]{2,1,0:T(8,128)S(1)}, u32[]{:S(2)}, u32[]{:S(2)}) collective-permute-start(f32[34,8,128]{2,1,0:T(8,128)S(1)} %get-tuple-element.99), channel_id=1, source_target_pairs={{14,0},{13,1},{0,2},{15,3},{2,4},{1,5},{4,6},{3,7},{6,8},{5,9},{8,... | collective-permute-start | bytes 417800 | tf_op jit(solution)/shard_map/ppermute | solution.py:334
  36.9 12.2 %collective-permute-start.8 = (f32[34,8,128]{2,1,0:T(8,128)S(1)}, f32[34,8,128]{2,1,0:T(8,128)S(1)}, u32[]{:S(2)}, u32[]{:S(2)}) collective-permute-start(f32[34,8,128]{2,1,0:T(8,128)S(1)} %get-tuple-element.100.pair_ref), channel_id=1, source_target_pairs={{2,0},{5,1},{4,2},{7,3},{6,4},{9,5},{8,6},{11,7},{10,8},{13,9},{12... | collective-permute-start | bytes 417800 | tf_op jit(solution)/shard_map/ppermute | solution.py:334
  39.1 9.9 %collective-permute-start.11 = (f32[18,8,128]{2,1,0:T(8,128)S(1)}, f32[18,8,128]{2,1,0:T(8,128)S(1)}, u32[]{:S(2)}, u32[]{:S(2)}) collective-permute-start(f32[18,8,128]{2,1,0:T(8,128)S(1)} %pad_maximum_fusion.10), channel_id=1, source_target_pairs={{8,0},{9,1},{10,2},{11,3},{12,4},{13,5},{14,6},{15,7},{0,8},{1,9},... | collective-permute-start | bytes 221192 | tf_op jit(solution)/shard_map/ppermute | solution.py:334
  49.2 1.3 %collective-permute-start.13 = (f32[18,8,128]{2,1,0:T(8,128)S(1)}, f32[18,8,128]{2,1,0:T(8,128)S(1)}, u32[]{:S(2)}, u32[]{:S(2)}) collective-permute-start(f32[18,8,128]{2,1,0:T(8,128)S(1)} %pad_maximum_fusion.11), channel_id=1, source_target_pairs={{1,0},{0,1},{3,2},{2,3},{5,4},{4,5},{7,6},{6,7},{9,8},{8,9},{11,10... | collective-permute-start | bytes 221192 | tf_op jit(solution)/shard_map/ppermute | solution.py:329
  49.3 1.8 %collective-permute-start.12 = (f32[80,8,128]{2,1,0:T(8,128)S(1)}, f32[80,8,128]{2,1,0:T(8,128)S(1)}, u32[]{:S(2)}, u32[]{:S(2)}) collective-permute-start(f32[80,8,128]{2,1,0:T(8,128)S(1)} %pad_maximum_fusion.1.mine_ref), channel_id=1, source_target_pairs={{1,0},{0,1},{3,2},{2,3},{5,4},{4,5},{7,6},{6,7},{9,8},{8,9},{11,10... | collective-permute-start | bytes 983048 | tf_op jit(solution)/shard_map/ppermute | solution.py:329
  54.6 3.2 %collective-permute-start.16 = (f32[32,128]{1,0:T(8,128)S(1)}, f32[32,128]{1,0:T(8,128)S(1)}, u32[]{:S(2)}, u32[]{:S(2)}) collective-permute-start(f32[32,128]{1,0:T(8,128)S(1)} %get-tuple-element.81), channel_id=1, source_target_pairs={{3,0},{2,1},{1,2},{0,3},{7,4},{6,5},{5,6},{4,7},{11,8},{10,9},{9,1... | collective-permute-start | bytes 49160 | tf_op jit(solution)/shard_map/ppermute | solution.py:329
  54.7 3.9 %collective-permute-start.15 = (f32[32,128]{1,0:T(8,128)S(1)}, f32[32,128]{1,0:T(8,128)S(1)}, u32[]{:S(2)}, u32[]{:S(2)}) collective-permute-start(f32[32,128]{1,0:T(8,128)S(1)} %get-tuple-element.81), channel_id=1, source_target_pairs={{2,0},{3,1},{0,2},{1,3},{6,4},{7,5},{4,6},{5,7},{10,8},{11,9},{8,1... | collective-permute-start | bytes 49160 | tf_op jit(solution)/shard_map/ppermute | solution.py:329
  56.6 1.9 %collective-permute-start.14 = (f32[32,128]{1,0:T(8,128)S(1)}, f32[32,128]{1,0:T(8,128)S(1)}, u32[]{:S(2)}, u32[]{:S(2)}) collective-permute-start(f32[32,128]{1,0:T(8,128)S(1)} %get-tuple-element.81), channel_id=1, source_target_pairs={{1,0},{0,1},{3,2},{2,3},{5,4},{4,5},{7,6},{6,7},{9,8},{8,9},{11,10... | collective-permute-start | bytes 49160 | tf_op jit(solution)/shard_map/ppermute | solution.py:329
  58.5 5.6 %collective-permute-start.19 = (f32[32,128]{1,0:T(8,128)S(1)}, f32[32,128]{1,0:T(8,128)S(1)}, u32[]{:S(2)}, u32[]{:S(2)}) collective-permute-start(f32[32,128]{1,0:T(8,128)S(1)} %add_add_fusion.1), channel_id=1, source_target_pairs={{12,0},{13,1},{14,2},{15,3},{8,4},{9,5},{10,6},{11,7},{4,8},{5,9},... | collective-permute-start | bytes 49160 | tf_op jit(solution)/shard_map/ppermute | solution.py:329
  60.4 4.6 %collective-permute-start.18 = (f32[32,128]{1,0:T(8,128)S(1)}, f32[32,128]{1,0:T(8,128)S(1)}, u32[]{:S(2)}, u32[]{:S(2)}) collective-permute-start(f32[32,128]{1,0:T(8,128)S(1)} %add_add_fusion.1), channel_id=1, source_target_pairs={{8,0},{9,1},{10,2},{11,3},{12,4},{13,5},{14,6},{15,7},{0,8},{1,9},... | collective-permute-start | bytes 49160 | tf_op jit(solution)/shard_map/ppermute | solution.py:329
  61.1 3.9 %collective-permute-start.17 = (f32[32,128]{1,0:T(8,128)S(1)}, f32[32,128]{1,0:T(8,128)S(1)}, u32[]{:S(2)}, u32[]{:S(2)}) collective-permute-start(f32[32,128]{1,0:T(8,128)S(1)} %add_add_fusion.1), channel_id=1, source_target_pairs={{4,0},{5,1},{6,2},{7,3},{0,4},{1,5},{2,6},{3,7},{12,8},{13,9},{14,... | collective-permute-start | bytes 49160 | tf_op jit(solution)/shard_map/ppermute | solution.py:329

commit v6 on v5

--- a/solution.py
+++ b/solution.py
@@ -11,7 +11,6 @@
 SIDE = 128
 PAD = 8
 SLOTS = 6
-NOTES = 2
 
 precise = lax.Precision.HIGHEST
 in_vmem = pl.BlockSpec(memory_space=pltpu.VMEM)
@@ -119,6 +118,10 @@
     return join(ref[: rows * order // (PAD * SIDE)], order // SIDE)
 
 
+def diagonal_of(side):
+    return lax.broadcasted_iota(jnp.int32, (side, side), 0) == lax.broadcasted_iota(jnp.int32, (side, side), 1)
+
+
 def place_of(columns_ref, e):
     devices = lax.axis_size("col")
     position = lax.axis_index("col")
@@ -129,7 +132,7 @@
 
 def place_products(columns_ref, products_ref, bundle_ref, keep_ref):
     size = keep_ref.shape[0] // SLOTS
-    start = size + NOTES
+    start = bundle_ref.shape[0] - keep_ref.shape[0]
     keep_ref[...] = jnp.zeros_like(keep_ref)
     bundle_ref[start:] = jnp.zeros_like(keep_ref)
     for e in range(products_ref.shape[0]):
@@ -173,8 +176,7 @@
         copies[1 + q].wait()
         trace += jnp.where(square, diagonal_ref[q], 0.0) * (1.0 / order)
     trace = jnp.sum(jnp.sum(trace, axis=0, keepdims=True), axis=1, keepdims=True)
-    bundle_ref[size] = pack(mm_t(signs, signs))
-    bundle_ref[size + 1] = jnp.broadcast_to(trace, (PAD, SIDE))
+    bundle_ref[size] = pack(jnp.where(diagonal_of(rows), trace, mm_t(signs, signs)))
     exact = (signs.astype(jnp.bfloat16), None)
     for e in range(tiles):
         copies[1 + squares + e].wait()
@@ -189,7 +191,7 @@
     bundle_ref, diagonal_ref, tile_high_ref, tile_low_ref, image_ref, high_ref, low_ref, turned_high_ref, turned_low_ref
 ):
     rows, order = image_ref.shape
-    trace = bundle_ref[rows * order // (PAD * SIDE) + 1, 0:1, 0:1]
+    trace = bundle_ref[rows * order // (PAD * SIDE), 0:1, 0:1]
     line = lax.broadcasted_iota(jnp.int32, (order, order), 0) == lax.broadcasted_iota(jnp.int32, (order, order), 1)
     high, low = halves(diagonal_ref[...] - jnp.where(line, trace, 0.0))
     high_ref[...] = high
@@ -204,8 +206,8 @@
     image_ref[...] = split_product(parts_of(block_of(bundle_ref, image_ref.shape), False), high_ref[...], low_ref[...], 0)
 
 
-def incoming_kernel(exact, columns_ref, pair_ref, mine_ref, theirs_ref, high_ref, low_ref, image_ref, ready_ref):
-    rows, order = image_ref.shape
+def incoming(shape, exact, columns_ref, pair_ref, mine_ref, theirs_ref, high_ref, low_ref, ready_ref):
+    rows, order = shape
     size = rows * order // (PAD * SIDE)
     tiles = high_ref.shape[0]
     for e in range(tiles):
@@ -220,26 +222,30 @@
         ready_ref[e, :rows] = high
         if not exact:
             ready_ref[e, rows:] = low
-    image = jnp.zeros(image_ref.shape, jnp.float32)
+    image = jnp.zeros(shape, jnp.float32)
     for e in range(tiles):
         vectors = ready_ref[e, :rows], None if exact else ready_ref[e, rows:]
         image += split_product(vectors, high_ref[e], low_ref[e], 0)
-    image_ref[...] = image
+    return image
 
 
 def shift_of(devices, start_ref, sums_ref, size):
-    mean = sums_ref[1, 0:1, 0:1] * (1.0 / devices)
-    return mean, start_ref[size + 1, 0:1, 0:1] - mean
+    mean = sums_ref[0, 0:1, 0:1] * (1.0 / devices)
+    return mean, start_ref[size, 0:1, 0:1] - mean
 
 
 def first_kernel(
-    devices, columns_ref, start_ref, near_ref, image_ref, total_ref, sums_ref, high_ref, low_ref,
-    bundle_ref, keep_ref, products_ref,
+    devices, columns_ref, start_ref, near_ref, total_ref, sums_ref, high_ref, low_ref,
+    pair_ref, mine_ref, theirs_ref, turned_high_ref, turned_low_ref,
+    bundle_ref, keep_ref, products_ref, ready_ref,
 ):
-    rows, order = image_ref.shape
+    rows, order = near_ref.shape
     size = rows * order // (PAD * SIDE)
-    signs = block_of(start_ref, image_ref.shape)
-    image = near_ref[...] + image_ref[...] + join(total_ref[...], order // SIDE)
+    signs = block_of(start_ref, near_ref.shape)
+    image = incoming(
+        near_ref.shape, True, columns_ref, pair_ref, mine_ref, theirs_ref, turned_high_ref, turned_low_ref, ready_ref
+    )
+    image += near_ref[...] + join(total_ref[...], order // SIDE)
     image += shift_of(devices, start_ref, sums_ref, size)[1] * signs
     put(bundle_ref, 0, image)
     vectors = halves(image)
@@ -251,25 +257,30 @@
     place_products(columns_ref, products_ref, bundle_ref, keep_ref)
 
 
-def root_kernel(sums_ref, start_ref, message_ref, root_ref, lines_ref):
+def root_kernel(devices, sums_ref, start_ref, message_ref, root_ref, lines_ref):
     rows = root_ref.shape[0]
     shape = rows, lines_ref.shape[1] // 2
-    root = factor(unpack(sums_ref[0], rows))[1]
+    square = devices * shape[1] * SCALE * SCALE
+    root = factor(jnp.where(diagonal_of(rows), square, unpack(sums_ref[0], rows)))[1]
     root_ref[...] = root
     lines_ref[...] = mm(root, jnp.concatenate([block_of(start_ref, shape), block_of(message_ref, shape)], axis=1))
 
 
 def second_kernel(
-    devices, start_ref, message_ref, near_ref, image_ref, total_ref, root_ref, lines_ref, first_sums_ref, sums_ref,
-    basis_ref, result_ref, share_ref,
+    devices, columns_ref, start_ref, message_ref, near_ref, total_ref, root_ref, lines_ref, first_sums_ref, sums_ref,
+    pair_ref, mine_ref, theirs_ref, turned_high_ref, turned_low_ref,
+    basis_ref, result_ref, share_ref, ready_ref,
 ):
-    rows, order = image_ref.shape
+    rows, order = near_ref.shape
     mean, shift = shift_of(devices, start_ref, first_sums_ref, rows * order // (PAD * SIDE))
     root = root_ref[...]
     alpha = mm_t(mm(root, unpack(sums_ref[0], rows)), root)
     gram = mm_t(mm(root, unpack(sums_ref[1], rows)), root) - mm_t(alpha, alpha)
-    image = near_ref[...] + image_ref[...] + join(total_ref[...], order // SIDE)
-    image = mm(root, image + shift * block_of(message_ref, image_ref.shape))
+    image = incoming(
+        near_ref.shape, False, columns_ref, pair_ref, mine_ref, theirs_ref, turned_high_ref, turned_low_ref, ready_ref
+    )
+    image += near_ref[...] + join(total_ref[...], order // SIDE)
+    image = mm(root, image + shift * block_of(message_ref, near_ref.shape))
     first_basis, first = lines_ref[:, :order], lines_ref[:, order:]
     bent = mm(alpha, lines_ref[...])
     beta, inverse = factor(gram)
@@ -340,7 +351,8 @@
             bits *= 2
         return sums
 
-    def apply(bundle, keep, near_call, exact):
+    def apply(bundle, keep, near_call):
+        top = bundle.shape[0] - keep.shape[0]
         partner = swapped(bundle)
         own, its = bundle[:size], partner[:size]
         payload = bundle[size:top] + partner[size:top]
@@ -362,33 +374,27 @@
         mine = jnp.concatenate([near[: 2 * size], third[: 2 * size], fourth[:size]])
         if devices == 16:
             sums = near[2 * size :] + near_back[2 * size :] + third[2 * size :]
-            sums = sums + jnp.where(lower_notes, payload + fourth[size:], 0.0)
+            sums = sums + jnp.where(lower[: top - size], payload + fourth[size:], 0.0)
         else:
-            sums = jnp.where(lower_notes, whole(payload), 0.0)
+            sums = jnp.where(lower[: top - size], whole(payload), 0.0)
         first = near_back[:size] + jnp.where(lower, 0.0, third[:size] + fourth[:size])
         second = near_back[size : 2 * size] + jnp.where(lower, 0.0, third[size : 2 * size] + ahead[5 * size :])
         other = jnp.concatenate([jnp.where(lower, second, first), sums])
         mine, other = lax.optimization_barrier((mine, other))
         theirs, other = swapped(mine), swapped(other)
-        image = call(
-            functools.partial(incoming_kernel, exact),
-            struct(rows, order),
-            (tile_columns, pair, mine, theirs, *turned[-2:]),
-            smem=1,
-            scratch=(pltpu.VMEM((tiles, 2 * rows, order), jnp.bfloat16),),
-        )
-        return inner, image, jnp.where(lower, first, second) + other[:size], sums + other[size:], turned
+        total = jnp.where(lower, first, second) + other[:size]
+        return inner, total, sums + other[size:], (pair, mine, theirs), turned
 
     tiles = forward.shape[0]
     size = rows * order // (PAD * SIDE)
-    top = size + NOTES
-    bundles = (struct(top + SLOTS * size, PAD, SIDE), struct(SLOTS * size, PAD, SIDE))
+    slots = struct(SLOTS * size, PAD, SIDE)
+    bundles = [struct(size + notes + SLOTS * size, PAD, SIDE) for notes in (1, 2)]
     products = pltpu.VMEM((tiles, rows, order), jnp.float32)
     split = pltpu.VMEM(forward.shape, jnp.bfloat16)
     split_diagonal = pltpu.VMEM(diagonal.shape, jnp.bfloat16)
     start, core, keep, high, low = call(
         begin_kernel,
-        (bundles[0], pltpu.VMEM((size, PAD, SIDE), jnp.int32), bundles[1], split, split),
+        (bundles[0], pltpu.VMEM((size, PAD, SIDE), jnp.int32), slots, split, split),
         (tile_columns, probes, diagonal, forward),
         smem=1,
         hbm=3,
@@ -402,7 +408,6 @@
         ),
     )
     lower = core == 0
-    lower_notes = lower[:NOTES]
     both_lower = jnp.concatenate([lower, lower])
 
     def first_near(bundle):
@@ -413,25 +418,33 @@
         )
         return made[0], made[1:]
 
-    inner, image, total, start_sums, turned = apply(start, keep, first_near, True)
+    inner, total, start_sums, met, turned = apply(start, keep, first_near)
     diagonal_high, diagonal_low, *turned = turned
+    ready = pltpu.VMEM((tiles, 2 * rows, order), jnp.bfloat16)
     message, keep = call(
         functools.partial(first_kernel, devices),
-        bundles,
-        (tile_columns, start, inner, image, total, start_sums, high, low),
+        (bundles[1], slots),
+        (tile_columns, start, inner, total, start_sums, high, low, *met, *turned),
         smem=1,
-        scratch=(products,),
-    )
+        scratch=(products, ready),
+    )
+
     def second_near(bundle):
         inner = call(second_near_kernel, struct(rows, order), (bundle, diagonal_high, diagonal_low))
-        ahead = call(root_kernel, (struct(rows, rows), struct(rows, 2 * order)), (start_sums, start, bundle))
-        return inner, (*ahead, *turned)
-
-    inner, image, total, sums, (root, lines, *_) = apply(message, keep, second_near, False)
+        ahead = call(
+            functools.partial(root_kernel, devices),
+            (struct(rows, rows), struct(rows, 2 * order)),
+            (start_sums, start, bundle),
+        )
+        return inner, ahead
+
+    inner, total, sums, met, (root, lines) = apply(message, keep, second_near)
     basis, result, share = call(
         functools.partial(second_kernel, devices),
         (struct(rows, order), struct(rows, order), struct(rows, SIDE)),
-        (start, message, inner, image, total, root, lines, start_sums, sums),
+        (tile_columns, start, message, inner, total, root, lines, start_sums, sums, *met, *turned),
+        smem=1,
+        scratch=(ready,),
     )
     bits = 1
     while bits < devices:

time: 67.1 us -> 65.7 us (0.979)
  Pallas kernels: 16 us -> 15 us
    pallas_call x9 -> x7, Pallas kernels: 16 us -> 15 us  [call(): pl.pallas_call(kernel, out_shape=out_shape, in_specs=[in_smem] * smem + [...]
where the time goes in v6:
time: 65.7 us; the launch traced here: 65.5 us
  waiting for transfers between devices  25.2 us (38%)
  starting transfers between devices  23.8 us (36%)
  Pallas kernels  15 us (23%)
  between operations  0.89 us (1%)
    ppermute x8, waiting for transfers between devices, from_chips(): return lax.ppermute(block, 'col', route)  15.9 us
    ppermute x8, starting transfers between devices, from_chips(): return lax.ppermute(block, 'col', route)  15.2 us
    pallas_call x7, Pallas kernels, call(): pl.pallas_call(kernel, out_shape=out_shape, in_specs=[in_smem] * smem + [...  15 us
    ppermute x12, waiting for transfers between devices, swapped(): return lax.ppermute(block, 'col', [(i ^ bits, i) for i in range(devices)])  9.27 us
    ppermute x12, starting transfers between devices, swapped(): return lax.ppermute(block, 'col', [(i ^ bits, i) for i in range(devices)])  8.62 us
  transfers between devices with their start and end apart: 20, of which 12 were waited for; matrix products, arithmetic and copies ran while one was open for 0% of the time, Pallas kernels for 4%

profile of v6, /device:TPU:0, one launch (start us, length us, event | category | flops | bytes accessed | tf_op | source)
XLA Modules:
  0.0 65.5 jit_solution(18180291548523997177)
XLA Ops:
  0.6 4.3 %shard_map.59 = (f32[113,8,128]{2,1,0:T(8,128)S(1)}, s32[16,8,128]{2,1,0:T(8,128)S(1)}, f32[96,8,128]{2,1,0:T(8,128)S(1)}, bf16[5,512,512]{2,1,0:T(8,128)(2,1)S(1)}, bf16[5,512,512]{2,1,0:T(8,128)(2,1)S(1)}) custom-call(s32[1,5]{1,0:T(1,128)} %columns_ref.5, s32[32,512]{1,0:T(8,128)} %probes_hbm.1, f32[512,512]{1,0:T(8,128)} %diagonal_ref.1, ...), custom_call_target="tpu_custom_call" | custom-call | flops 1 | bytes 1 | tf_op jit(solution)/shard_map/pallas_call | solution.py:323
  4.9 0.5 collective-permute-start
  5.4 1.4 %collective-permute-done = f32[113,8,128]{2,1,0:T(8,128)S(1)} collective-permute-done((f32[113,8,128]{2,1,0:T(8,128)S(1)}, f32[113,8,128]{2,1,0:T(8,128)S(1)}, u32[]{:S(2)}, u32[]{:S(2)}) %collective-permute-start) | collective-permute-done | bytes 462880 | tf_op jit(solution)/shard_map/ppermute | solution.py:340
  7.1 5.0 %collective-permute-start.3 = (f32[33,8,128]{2,1,0:T(8,128)S(1)}, f32[33,8,128]{2,1,0:T(8,128)S(1)}, u32[]{:S(2)}, u32[]{:S(2)}) collective-permute-start(f32[33,8,128]{2,1,0:T(8,128)S(1)} %get-tuple-element.97), channel_id=1, source_target_pairs={{6,0},{11,1},{8,2},{13,3},{10,4},{15,5},{12,6},{1,7},{14,8},{3,9},... | collective-permute-start | bytes 405512 | tf_op jit(solution)/shard_map/ppermute | solution.py:345
  12.0 1.5 %collective-permute-start.2 = (f32[33,8,128]{2,1,0:T(8,128)S(1)}, f32[33,8,128]{2,1,0:T(8,128)S(1)}, u32[]{:S(2)}, u32[]{:S(2)}) collective-permute-start(f32[33,8,128]{2,1,0:T(8,128)S(1)} %get-tuple-element.98), channel_id=1, source_target_pairs={{14,0},{13,1},{0,2},{15,3},{2,4},{1,5},{4,6},{3,7},{6,8},{5,9},{8,... | collective-permute-start | bytes 405512 | tf_op jit(solution)/shard_map/ppermute | solution.py:345
  13.5 3.2 %collective-permute-start.1 = (f32[33,8,128]{2,1,0:T(8,128)S(1)}, f32[33,8,128]{2,1,0:T(8,128)S(1)}, u32[]{:S(2)}, u32[]{:S(2)}) collective-permute-start(f32[33,8,128]{2,1,0:T(8,128)S(1)} %get-tuple-element.99.pair_ref), channel_id=1, source_target_pairs={{2,0},{5,1},{4,2},{7,3},{6,4},{9,5},{8,6},{11,7},{10,8},{13,9},{12... | collective-permute-start | bytes 405512 | tf_op jit(solution)/shard_map/ppermute | solution.py:345
  16.8 1.5 %shard_map.60 = (f32[32,512]{1,0:T(8,128)S(1)}, bf16[512,512]{1,0:T(8,128)(2,1)S(1)}, bf16[512,512]{1,0:T(8,128)(2,1)S(1)}, bf16[5,512,512]{2,1,0:T(8,128)(2,1)S(1)}, bf16[5,512,512]{2,1,0:T(8,128)(2,1)S(1)}) custom-call(f32[113,8,128]{2,1,0:T(8,128)S(1)} %get-tuple-element.44.bundle_ref.start_ref, f32[512,512]{1,0:T(8,128)S(1)} %copy-done, ...), custom_call_target="tpu_custom_call" | custom-call | flops 1 | bytes 1 | tf_op jit(solution)/shard_map/pallas_call | solution.py:323
  18.3 7.3 %collective-permute-done.4 = f32[17,8,128]{2,1,0:T(8,128)S(1)} collective-permute-done((f32[17,8,128]{2,1,0:T(8,128)S(1)}, f32[17,8,128]{2,1,0:T(8,128)S(1)}, u32[]{:S(2)}, u32[]{:S(2)}) %collective-permute-start.4) | collective-permute-done | bytes 69664 | tf_op jit(solution)/shard_map/ppermute | solution.py:345
  25.8 0.5 collective-permute-start.6
  26.3 0.7 %collective-permute-done.5 = f32[17,8,128]{2,1,0:T(8,128)S(1)} collective-permute-done((f32[17,8,128]{2,1,0:T(8,128)S(1)}, f32[17,8,128]{2,1,0:T(8,128)S(1)}, u32[]{:S(2)}, u32[]{:S(2)}) %collective-permute-start.5) | collective-permute-done | bytes 69664 | tf_op jit(solution)/shard_map/ppermute | solution.py:340
  27.1 0.5 collective-permute-done.6.theirs_ref
  27.5 3.0 %shard_map.61 = (f32[114,8,128]{2,1,0:T(8,128)S(1)}, f32[96,8,128]{2,1,0:T(8,128)S(1)}) custom-call(s32[1,5]{1,0:T(1,128)} %columns_ref.5, f32[113,8,128]{2,1,0:T(8,128)S(1)} %get-tuple-element.44.bundle_ref.start_ref, f32[32,512]{1,0:T(8,128)S(1)} %get-tuple-element.52.near_ref, f32[16,8,128]{2,1,0:T(8,128)S(1)} %slice_add_fusion.4.total_ref, ...), custom_call_target="tpu_custom_call" | custom-call | flops 1 | bytes 1 | tf_op jit(solution)/shard_map/pallas_call | solution.py:323
  30.6 0.4 collective-permute-start.7
  31.0 1.5 %collective-permute-done.7 = f32[114,8,128]{2,1,0:T(8,128)S(1)} collective-permute-done((f32[114,8,128]{2,1,0:T(8,128)S(1)}, f32[114,8,128]{2,1,0:T(8,128)S(1)}, u32[]{:S(2)}, u32[]{:S(2)}) %collective-permute-start.7) | collective-permute-done | bytes 466976 | tf_op jit(solution)/shard_map/ppermute | solution.py:340
  32.6 0.8 %collective-permute-start.10 = (f32[34,8,128]{2,1,0:T(8,128)S(1)}, f32[34,8,128]{2,1,0:T(8,128)S(1)}, u32[]{:S(2)}, u32[]{:S(2)}) collective-permute-start(f32[34,8,128]{2,1,0:T(8,128)S(1)} %get-tuple-element.94), channel_id=1, source_target_pairs={{6,0},{11,1},{8,2},{13,3},{10,4},{15,5},{12,6},{1,7},{14,8},{3,9},... | collective-permute-start | bytes 417800 | tf_op jit(solution)/shard_map/ppermute | solution.py:345
  33.4 2.5 %collective-permute-start.9 = (f32[34,8,128]{2,1,0:T(8,128)S(1)}, f32[34,8,128]{2,1,0:T(8,128)S(1)}, u32[]{:S(2)}, u32[]{:S(2)}) collective-permute-start(f32[34,8,128]{2,1,0:T(8,128)S(1)} %get-tuple-element.95), channel_id=1, source_target_pairs={{14,0},{13,1},{0,2},{15,3},{2,4},{1,5},{4,6},{3,7},{6,8},{5,9},{8,... | collective-permute-start | bytes 417800 | tf_op jit(solution)/shard_map/ppermute | solution.py:345
  35.9 2.2 %collective-permute-start.8 = (f32[34,8,128]{2,1,0:T(8,128)S(1)}, f32[34,8,128]{2,1,0:T(8,128)S(1)}, u32[]{:S(2)}, u32[]{:S(2)}) collective-permute-start(f32[34,8,128]{2,1,0:T(8,128)S(1)} %get-tuple-element.96.pair_ref), channel_id=1, source_target_pairs={{2,0},{5,1},{4,2},{7,3},{6,4},{9,5},{8,6},{11,7},{10,8},{13,9},{12... | collective-permute-start | bytes 417800 | tf_op jit(solution)/shard_map/ppermute | solution.py:345
  38.2 1.0 %shard_map.63 = (f32[32,32]{1,0:T(8,128)S(1)}, f32[32,1024]{1,0:T(8,128)S(1)}) custom-call(f32[1,8,128]{2,1,0:T(8,128)S(1)} %slice_add_fusion.8.sums_ref.first_sums_ref, f32[113,8,128]{2,1,0:T(8,128)S(1)} %get-tuple-element.44.bundle_ref.start_ref, f32[114,8,128]{2,1,0:T(8,128)S(1)} %get-tuple-element.63.bundle_ref.message_ref), custom_call_target="tpu_custom_call" | custom-call | flops 1 | bytes 1 | tf_op jit(solution)/shard_map/pallas_call | solution.py:323
  39.4 8.6 %collective-permute-done.11 = f32[18,8,128]{2,1,0:T(8,128)S(1)} collective-permute-done((f32[18,8,128]{2,1,0:T(8,128)S(1)}, f32[18,8,128]{2,1,0:T(8,128)S(1)}, u32[]{:S(2)}, u32[]{:S(2)}) %collective-permute-start.11) | collective-permute-done | bytes 73760 | tf_op jit(solution)/shard_map/ppermute | solution.py:345
  48.3 0.5 collective-permute-start.13
  48.8 0.8 %collective-permute-done.12 = f32[18,8,128]{2,1,0:T(8,128)S(1)} collective-permute-done((f32[18,8,128]{2,1,0:T(8,128)S(1)}, f32[18,8,128]{2,1,0:T(8,128)S(1)}, u32[]{:S(2)}, u32[]{:S(2)}) %collective-permute-start.12) | collective-permute-done | bytes 73760 | tf_op jit(solution)/shard_map/ppermute | solution.py:340
  49.6 0.5 collective-permute-done.13.theirs_ref
  50.1 3.1 %shard_map.64 = (f32[32,512]{1,0:T(8,128)S(1)}, f32[32,512]{1,0:T(8,128)S(1)}, f32[32,128]{1,0:T(8,128)S(1)}) custom-call(s32[1,5]{1,0:T(1,128)} %columns_ref.5, f32[113,8,128]{2,1,0:T(8,128)S(1)} %get-tuple-element.44.bundle_ref.start_ref, f32[114,8,128]{2,1,0:T(8,128)S(1)} %get-tuple-element.63.bundle_ref.message_ref, f32[32,512]{1,0:T(8,128)S(1)} %shard_map.62.near_ref, ...), custom_call_target="tpu_custom_call" | custom-call | flops 1 | bytes 1 | tf_op jit(solution)/shard_map/pallas_call | solution.py:323
  53.3 2.0 %collective-permute-start.15 = (f32[32,128]{1,0:T(8,128)S(1)}, f32[32,128]{1,0:T(8,128)S(1)}, u32[]{:S(2)}, u32[]{:S(2)}) collective-permute-start(f32[32,128]{1,0:T(8,128)S(1)} %get-tuple-element.77), channel_id=1, source_target_pairs={{2,0},{3,1},{0,2},{1,3},{6,4},{7,5},{4,6},{5,7},{10,8},{11,9},{8,1... | collective-permute-start | bytes 49160 | tf_op jit(solution)/shard_map/ppermute | solution.py:340
  55.3 1.2 %collective-permute-done.16 = f32[32,128]{1,0:T(8,128)S(1)} collective-permute-done((f32[32,128]{1,0:T(8,128)S(1)}, f32[32,128]{1,0:T(8,128)S(1)}, u32[]{:S(2)}, u32[]{:S(2)}) %collective-permute-start.16) | collective-permute-done | bytes 16416 | tf_op jit(solution)/shard_map/ppermute | solution.py:340
  56.4 0.7 %collective-permute-done.15 = f32[32,128]{1,0:T(8,128)S(1)} collective-permute-done((f32[32,128]{1,0:T(8,128)S(1)}, f32[32,128]{1,0:T(8,128)S(1)}, u32[]{:S(2)}, u32[]{:S(2)}) %collective-permute-start.15) | collective-permute-done | bytes 16416 | tf_op jit(solution)/shard_map/ppermute | solution.py:340
  57.2 1.9 %collective-permute-start.19 = (f32[32,128]{1,0:T(8,128)S(1)}, f32[32,128]{1,0:T(8,128)S(1)}, u32[]{:S(2)}, u32[]{:S(2)}) collective-permute-start(f32[32,128]{1,0:T(8,128)S(1)} %add_add_fusion.1), channel_id=1, source_target_pairs={{12,0},{13,1},{14,2},{15,3},{8,4},{9,5},{10,6},{11,7},{4,8},{5,9},... | collective-permute-start | bytes 49160 | tf_op jit(solution)/shard_map/ppermute | solution.py:340
  59.0 0.7 %collective-permute-start.18 = (f32[32,128]{1,0:T(8,128)S(1)}, f32[32,128]{1,0:T(8,128)S(1)}, u32[]{:S(2)}, u32[]{:S(2)}) collective-permute-start(f32[32,128]{1,0:T(8,128)S(1)} %add_add_fusion.1), channel_id=1, source_target_pairs={{8,0},{9,1},{10,2},{11,3},{12,4},{13,5},{14,6},{15,7},{0,8},{1,9},... | collective-permute-start | bytes 49160 | tf_op jit(solution)/shard_map/ppermute | solution.py:340
  59.7 1.9 %collective-permute-start.17 = (f32[32,128]{1,0:T(8,128)S(1)}, f32[32,128]{1,0:T(8,128)S(1)}, u32[]{:S(2)}, u32[]{:S(2)}) collective-permute-start(f32[32,128]{1,0:T(8,128)S(1)} %add_add_fusion.1), channel_id=1, source_target_pairs={{4,0},{5,1},{6,2},{7,3},{0,4},{1,5},{2,6},{3,7},{12,8},{13,9},{14,... | collective-permute-start | bytes 49160 | tf_op jit(solution)/shard_map/ppermute | solution.py:340
  61.6 1.1 %collective-permute-done.19 = f32[32,128]{1,0:T(8,128)S(1)} collective-permute-done((f32[32,128]{1,0:T(8,128)S(1)}, f32[32,128]{1,0:T(8,128)S(1)}, u32[]{:S(2)}, u32[]{:S(2)}) %collective-permute-start.19) | collective-permute-done | bytes 16416 | tf_op jit(solution)/shard_map/ppermute | solution.py:340
  62.8 0.9 %collective-permute-done.18 = f32[32,128]{1,0:T(8,128)S(1)} collective-permute-done((f32[32,128]{1,0:T(8,128)S(1)}, f32[32,128]{1,0:T(8,128)S(1)}, u32[]{:S(2)}, u32[]{:S(2)}) %collective-permute-start.18) | collective-permute-done | bytes 16416 | tf_op jit(solution)/shard_map/ppermute | solution.py:340
  63.7 1.8 %shard_map.65 = (f32[32,512]{1,0:T(8,128)}, f32[4,32,32]{2,1,0:T(8,128)}) custom-call(f32[32,128]{1,0:T(8,128)S(1)} %add_add_fusion.share_ref, f32[32,512]{1,0:T(8,128)S(1)} %get-tuple-element.78.basis_ref, f32[32,512]{1,0:T(8,128)S(1)} %get-tuple-element.79.result_ref), custom_call_target="tpu_custom_call" | custom-call | flops 1 | bytes 1 | tf_op jit(solution)/shard_map/pallas_call | solution.py:323
  (48 shorter events, 1.1 us)
Async XLA Ops:
  4.9 11.9 %copy-start = (f32[512,512]{1,0:T(8,128)S(1)}, f32[512,512]{1,0:T(8,128)}, u32[]{:S(2)}) copy-start(f32[512,512]{1,0:T(8,128)} %diagonal_ref.1) | copy-start | bytes 3145732
  4.9 2.0 %collective-permute-start = (f32[113,8,128]{2,1,0:T(8,128)S(1)}, f32[113,8,128]{2,1,0:T(8,128)S(1)}, u32[]{:S(2)}, u32[]{:S(2)}) collective-permute-start(f32[113,8,128]{2,1,0:T(8,128)S(1)} %get-tuple-element.44.bundle_ref.start_ref), channel_id=1, source_target_pairs={{1,0},{0,1},{3,2},{2,3},{5,4},{4,5},{7,6},{6,7},{9,8},{8,9},{11,10... | collective-permute-start | bytes 1388552 | tf_op jit(solution)/shard_map/ppermute | solution.py:340
  7.1 18.5 %collective-permute-start.3 = (f32[33,8,128]{2,1,0:T(8,128)S(1)}, f32[33,8,128]{2,1,0:T(8,128)S(1)}, u32[]{:S(2)}, u32[]{:S(2)}) collective-permute-start(f32[33,8,128]{2,1,0:T(8,128)S(1)} %get-tuple-element.97), channel_id=1, source_target_pairs={{6,0},{11,1},{8,2},{13,3},{10,4},{15,5},{12,6},{1,7},{14,8},{3,9},... | collective-permute-start | bytes 405512 | tf_op jit(solution)/shard_map/ppermute | solution.py:345
  12.0 13.6 %collective-permute-start.2 = (f32[33,8,128]{2,1,0:T(8,128)S(1)}, f32[33,8,128]{2,1,0:T(8,128)S(1)}, u32[]{:S(2)}, u32[]{:S(2)}) collective-permute-start(f32[33,8,128]{2,1,0:T(8,128)S(1)} %get-tuple-element.98), channel_id=1, source_target_pairs={{14,0},{13,1},{0,2},{15,3},{2,4},{1,5},{4,6},{3,7},{6,8},{5,9},{8,... | collective-permute-start | bytes 405512 | tf_op jit(solution)/shard_map/ppermute | solution.py:345
  13.5 12.1 %collective-permute-start.1 = (f32[33,8,128]{2,1,0:T(8,128)S(1)}, f32[33,8,128]{2,1,0:T(8,128)S(1)}, u32[]{:S(2)}, u32[]{:S(2)}) collective-permute-start(f32[33,8,128]{2,1,0:T(8,128)S(1)} %get-tuple-element.99.pair_ref), channel_id=1, source_target_pairs={{2,0},{5,1},{4,2},{7,3},{6,4},{9,5},{8,6},{11,7},{10,8},{13,9},{12... | collective-permute-start | bytes 405512 | tf_op jit(solution)/shard_map/ppermute | solution.py:345
  16.7 8.8 %collective-permute-start.4 = (f32[17,8,128]{2,1,0:T(8,128)S(1)}, f32[17,8,128]{2,1,0:T(8,128)S(1)}, u32[]{:S(2)}, u32[]{:S(2)}) collective-permute-start(f32[17,8,128]{2,1,0:T(8,128)S(1)} %pad_maximum_fusion.10), channel_id=1, source_target_pairs={{8,0},{9,1},{10,2},{11,3},{12,4},{13,5},{14,6},{15,7},{0,8},{1,9},... | collective-permute-start | bytes 208904 | tf_op jit(solution)/shard_map/ppermute | solution.py:345
  25.7 1.3 %collective-permute-start.5 = (f32[17,8,128]{2,1,0:T(8,128)S(1)}, f32[17,8,128]{2,1,0:T(8,128)S(1)}, u32[]{:S(2)}, u32[]{:S(2)}) collective-permute-start(f32[17,8,128]{2,1,0:T(8,128)S(1)} %pad_maximum_fusion.11), channel_id=1, source_target_pairs={{1,0},{0,1},{3,2},{2,3},{5,4},{4,5},{7,6},{6,7},{9,8},{8,9},{11,10... | collective-permute-start | bytes 208904 | tf_op jit(solution)/shard_map/ppermute | solution.py:340
  25.8 1.8 %collective-permute-start.6 = (f32[80,8,128]{2,1,0:T(8,128)S(1)}, f32[80,8,128]{2,1,0:T(8,128)S(1)}, u32[]{:S(2)}, u32[]{:S(2)}) collective-permute-start(f32[80,8,128]{2,1,0:T(8,128)S(1)} %pad_maximum_fusion.mine_ref), channel_id=1, source_target_pairs={{1,0},{0,1},{3,2},{2,3},{5,4},{4,5},{7,6},{6,7},{9,8},{8,9},{11,10... | collective-permute-start | bytes 983048 | tf_op jit(solution)/shard_map/ppermute | solution.py:340
  30.6 1.9 %collective-permute-start.7 = (f32[114,8,128]{2,1,0:T(8,128)S(1)}, f32[114,8,128]{2,1,0:T(8,128)S(1)}, u32[]{:S(2)}, u32[]{:S(2)}) collective-permute-start(f32[114,8,128]{2,1,0:T(8,128)S(1)} %get-tuple-element.63.bundle_ref.message_ref), channel_id=1, source_target_pairs={{1,0},{0,1},{3,2},{2,3},{5,4},{4,5},{7,6},{6,7},{9,8},{8,9},{11,10... | collective-permute-start | bytes 1400840 | tf_op jit(solution)/shard_map/ppermute | solution.py:340
  32.6 15.4 %collective-permute-start.10 = (f32[34,8,128]{2,1,0:T(8,128)S(1)}, f32[34,8,128]{2,1,0:T(8,128)S(1)}, u32[]{:S(2)}, u32[]{:S(2)}) collective-permute-start(f32[34,8,128]{2,1,0:T(8,128)S(1)} %get-tuple-element.94), channel_id=1, source_target_pairs={{6,0},{11,1},{8,2},{13,3},{10,4},{15,5},{12,6},{1,7},{14,8},{3,9},... | collective-permute-start | bytes 417800 | tf_op jit(solution)/shard_map/ppermute | solution.py:345
  33.4 14.7 %collective-permute-start.9 = (f32[34,8,128]{2,1,0:T(8,128)S(1)}, f32[34,8,128]{2,1,0:T(8,128)S(1)}, u32[]{:S(2)}, u32[]{:S(2)}) collective-permute-start(f32[34,8,128]{2,1,0:T(8,128)S(1)} %get-tuple-element.95), channel_id=1, source_target_pairs={{14,0},{13,1},{0,2},{15,3},{2,4},{1,5},{4,6},{3,7},{6,8},{5,9},{8,... | collective-permute-start | bytes 417800 | tf_op jit(solution)/shard_map/ppermute | solution.py:345
  35.9 12.2 %collective-permute-start.8 = (f32[34,8,128]{2,1,0:T(8,128)S(1)}, f32[34,8,128]{2,1,0:T(8,128)S(1)}, u32[]{:S(2)}, u32[]{:S(2)}) collective-permute-start(f32[34,8,128]{2,1,0:T(8,128)S(1)} %get-tuple-element.96.pair_ref), channel_id=1, source_target_pairs={{2,0},{5,1},{4,2},{7,3},{6,4},{9,5},{8,6},{11,7},{10,8},{13,9},{12... | collective-permute-start | bytes 417800 | tf_op jit(solution)/shard_map/ppermute | solution.py:345
  38.1 9.9 %collective-permute-start.11 = (f32[18,8,128]{2,1,0:T(8,128)S(1)}, f32[18,8,128]{2,1,0:T(8,128)S(1)}, u32[]{:S(2)}, u32[]{:S(2)}) collective-permute-start(f32[18,8,128]{2,1,0:T(8,128)S(1)} %pad_maximum_fusion.8), channel_id=1, source_target_pairs={{8,0},{9,1},{10,2},{11,3},{12,4},{13,5},{14,6},{15,7},{0,8},{1,9},... | collective-permute-start | bytes 221192 | tf_op jit(solution)/shard_map/ppermute | solution.py:345
  48.2 1.3 %collective-permute-start.12 = (f32[18,8,128]{2,1,0:T(8,128)S(1)}, f32[18,8,128]{2,1,0:T(8,128)S(1)}, u32[]{:S(2)}, u32[]{:S(2)}) collective-permute-start(f32[18,8,128]{2,1,0:T(8,128)S(1)} %pad_maximum_fusion.9), channel_id=1, source_target_pairs={{1,0},{0,1},{3,2},{2,3},{5,4},{4,5},{7,6},{6,7},{9,8},{8,9},{11,10... | collective-permute-start | bytes 221192 | tf_op jit(solution)/shard_map/ppermute | solution.py:340
  48.3 1.8 %collective-permute-start.13 = (f32[80,8,128]{2,1,0:T(8,128)S(1)}, f32[80,8,128]{2,1,0:T(8,128)S(1)}, u32[]{:S(2)}, u32[]{:S(2)}) collective-permute-start(f32[80,8,128]{2,1,0:T(8,128)S(1)} %pad_maximum_fusion.1.mine_ref), channel_id=1, source_target_pairs={{1,0},{0,1},{3,2},{2,3},{5,4},{4,5},{7,6},{6,7},{9,8},{8,9},{11,10... | collective-permute-start | bytes 983048 | tf_op jit(solution)/shard_map/ppermute | solution.py:340
  53.2 3.2 %collective-permute-start.16 = (f32[32,128]{1,0:T(8,128)S(1)}, f32[32,128]{1,0:T(8,128)S(1)}, u32[]{:S(2)}, u32[]{:S(2)}) collective-permute-start(f32[32,128]{1,0:T(8,128)S(1)} %get-tuple-element.77), channel_id=1, source_target_pairs={{3,0},{2,1},{1,2},{0,3},{7,4},{6,5},{5,6},{4,7},{11,8},{10,9},{9,1... | collective-permute-start | bytes 49160 | tf_op jit(solution)/shard_map/ppermute | solution.py:340
  53.3 3.9 %collective-permute-start.15 = (f32[32,128]{1,0:T(8,128)S(1)}, f32[32,128]{1,0:T(8,128)S(1)}, u32[]{:S(2)}, u32[]{:S(2)}) collective-permute-start(f32[32,128]{1,0:T(8,128)S(1)} %get-tuple-element.77), channel_id=1, source_target_pairs={{2,0},{3,1},{0,2},{1,3},{6,4},{7,5},{4,6},{5,7},{10,8},{11,9},{8,1... | collective-permute-start | bytes 49160 | tf_op jit(solution)/shard_map/ppermute | solution.py:340
  55.3 1.9 %collective-permute-start.14 = (f32[32,128]{1,0:T(8,128)S(1)}, f32[32,128]{1,0:T(8,128)S(1)}, u32[]{:S(2)}, u32[]{:S(2)}) collective-permute-start(f32[32,128]{1,0:T(8,128)S(1)} %get-tuple-element.77), channel_id=1, source_target_pairs={{1,0},{0,1},{3,2},{2,3},{5,4},{4,5},{7,6},{6,7},{9,8},{8,9},{11,10... | collective-permute-start | bytes 49160 | tf_op jit(solution)/shard_map/ppermute | solution.py:340
  57.2 5.6 %collective-permute-start.19 = (f32[32,128]{1,0:T(8,128)S(1)}, f32[32,128]{1,0:T(8,128)S(1)}, u32[]{:S(2)}, u32[]{:S(2)}) collective-permute-start(f32[32,128]{1,0:T(8,128)S(1)} %add_add_fusion.1), channel_id=1, source_target_pairs={{12,0},{13,1},{14,2},{15,3},{8,4},{9,5},{10,6},{11,7},{4,8},{5,9},... | collective-permute-start | bytes 49160 | tf_op jit(solution)/shard_map/ppermute | solution.py:340
  59.0 4.6 %collective-permute-start.18 = (f32[32,128]{1,0:T(8,128)S(1)}, f32[32,128]{1,0:T(8,128)S(1)}, u32[]{:S(2)}, u32[]{:S(2)}) collective-permute-start(f32[32,128]{1,0:T(8,128)S(1)} %add_add_fusion.1), channel_id=1, source_target_pairs={{8,0},{9,1},{10,2},{11,3},{12,4},{13,5},{14,6},{15,7},{0,8},{1,9},... | collective-permute-start | bytes 49160 | tf_op jit(solution)/shard_map/ppermute | solution.py:340
  59.7 3.9 %collective-permute-start.17 = (f32[32,128]{1,0:T(8,128)S(1)}, f32[32,128]{1,0:T(8,128)S(1)}, u32[]{:S(2)}, u32[]{:S(2)}) collective-permute-start(f32[32,128]{1,0:T(8,128)S(1)} %add_add_fusion.1), channel_id=1, source_target_pairs={{4,0},{5,1},{6,2},{7,3},{0,4},{1,5},{2,6},{3,7},{12,8},{13,9},{14,... | collective-permute-start | bytes 49160 | tf_op jit(solution)/shard_map/ppermute | solution.py:340

commit v7 on v6

--- a/solution.py
+++ b/solution.py
@@ -446,15 +446,14 @@
         smem=1,
         scratch=(ready,),
     )
-    bits = 1
-    while bits < devices:
-        if 4 * bits <= devices:
-            one, two, three = (swapped(share, bits * j) for j in (1, 2, 3))
-            share = (share + one) + (two + three)
-            bits *= 4
-        else:
-            share = share + swapped(share, bits)
-            bits *= 2
+    low = 1
+    strides = []
+    while low < devices:
+        strides.append((low, (1, 2, 3) if 4 * low <= devices else (1,)))
+        low *= 4 if 4 * low <= devices else 2
+    for bits, steps in reversed(strides):
+        got = [swapped(share, bits * j) for j in steps]
+        share = share + got[0] if len(got) == 1 else (share + got[0]) + (got[1] + got[2])
     outs = (jax.ShapeDtypeStruct((rows, order), jnp.float32), jax.ShapeDtypeStruct((4, rows, rows), jnp.float32))
     return call(last_kernel, outs, (share, basis, result))
 

time: 65.7 us -> 65.4 us (level)
  transfers between devices with their start and end apart: 20 -> 20, of which waited for: 12 -> 13; matrix products, arithmetic and copies ran while one was open for 0% -> 0% of each run, Pallas kernels for 4% -> 4%
where the time goes in v7:
time: 65.4 us; the launch traced here: 65.2 us
  waiting for transfers between devices  25 us (38%)
  starting transfers between devices  23.7 us (36%)
  Pallas kernels  15 us (23%)
  between operations  0.89 us (1%)
    ppermute x8, waiting for transfers between devices, from_chips(): return lax.ppermute(block, 'col', route)  15.9 us
    ppermute x8, starting transfers between devices, from_chips(): return lax.ppermute(block, 'col', route)  15.2 us
    pallas_call x7, Pallas kernels, call(): pl.pallas_call(kernel, out_shape=out_shape, in_specs=[in_smem] * smem + [...  15 us
    ppermute x12, waiting for transfers between devices, swapped(): return lax.ppermute(block, 'col', [(i ^ bits, i) for i in range(devices)])  9.11 us
    ppermute x12, starting transfers between devices, swapped(): return lax.ppermute(block, 'col', [(i ^ bits, i) for i in range(devices)])  8.49 us
  transfers between devices with their start and end apart: 20, of which 13 were waited for; matrix products, arithmetic and copies ran while one was open for 0% of the time, Pallas kernels for 4%

profile of v7, /device:TPU:0, one launch (start us, length us, event | category | flops | bytes accessed | tf_op | source)
XLA Modules:
  0.0 65.2 jit_solution(16474312579504782514)
XLA Ops:
  0.6 4.2 %shard_map.59 = (f32[113,8,128]{2,1,0:T(8,128)S(1)}, s32[16,8,128]{2,1,0:T(8,128)S(1)}, f32[96,8,128]{2,1,0:T(8,128)S(1)}, bf16[5,512,512]{2,1,0:T(8,128)(2,1)S(1)}, bf16[5,512,512]{2,1,0:T(8,128)(2,1)S(1)}) custom-call(s32[1,5]{1,0:T(1,128)} %columns_ref.5, s32[32,512]{1,0:T(8,128)} %probes_hbm.1, f32[512,512]{1,0:T(8,128)} %diagonal_ref.1, ...), custom_call_target="tpu_custom_call" | custom-call | flops 1 | bytes 1 | tf_op jit(solution)/shard_map/pallas_call | solution.py:323
  4.9 0.5 collective-permute-start
  5.4 1.4 %collective-permute-done = f32[113,8,128]{2,1,0:T(8,128)S(1)} collective-permute-done((f32[113,8,128]{2,1,0:T(8,128)S(1)}, f32[113,8,128]{2,1,0:T(8,128)S(1)}, u32[]{:S(2)}, u32[]{:S(2)}) %collective-permute-start) | collective-permute-done | bytes 462880 | tf_op jit(solution)/shard_map/ppermute | solution.py:340
  7.0 5.0 %collective-permute-start.3 = (f32[33,8,128]{2,1,0:T(8,128)S(1)}, f32[33,8,128]{2,1,0:T(8,128)S(1)}, u32[]{:S(2)}, u32[]{:S(2)}) collective-permute-start(f32[33,8,128]{2,1,0:T(8,128)S(1)} %get-tuple-element.97), channel_id=1, source_target_pairs={{6,0},{11,1},{8,2},{13,3},{10,4},{15,5},{12,6},{1,7},{14,8},{3,9},... | collective-permute-start | bytes 405512 | tf_op jit(solution)/shard_map/ppermute | solution.py:345
  12.0 1.5 %collective-permute-start.2 = (f32[33,8,128]{2,1,0:T(8,128)S(1)}, f32[33,8,128]{2,1,0:T(8,128)S(1)}, u32[]{:S(2)}, u32[]{:S(2)}) collective-permute-start(f32[33,8,128]{2,1,0:T(8,128)S(1)} %get-tuple-element.98), channel_id=1, source_target_pairs={{14,0},{13,1},{0,2},{15,3},{2,4},{1,5},{4,6},{3,7},{6,8},{5,9},{8,... | collective-permute-start | bytes 405512 | tf_op jit(solution)/shard_map/ppermute | solution.py:345
  13.5 3.2 %collective-permute-start.1 = (f32[33,8,128]{2,1,0:T(8,128)S(1)}, f32[33,8,128]{2,1,0:T(8,128)S(1)}, u32[]{:S(2)}, u32[]{:S(2)}) collective-permute-start(f32[33,8,128]{2,1,0:T(8,128)S(1)} %get-tuple-element.99.pair_ref), channel_id=1, source_target_pairs={{2,0},{5,1},{4,2},{7,3},{6,4},{9,5},{8,6},{11,7},{10,8},{13,9},{12... | collective-permute-start | bytes 405512 | tf_op jit(solution)/shard_map/ppermute | solution.py:345
  16.8 1.5 %shard_map.60 = (f32[32,512]{1,0:T(8,128)S(1)}, bf16[512,512]{1,0:T(8,128)(2,1)S(1)}, bf16[512,512]{1,0:T(8,128)(2,1)S(1)}, bf16[5,512,512]{2,1,0:T(8,128)(2,1)S(1)}, bf16[5,512,512]{2,1,0:T(8,128)(2,1)S(1)}) custom-call(f32[113,8,128]{2,1,0:T(8,128)S(1)} %get-tuple-element.44.bundle_ref.start_ref, f32[512,512]{1,0:T(8,128)S(1)} %copy-done, ...), custom_call_target="tpu_custom_call" | custom-call | flops 1 | bytes 1 | tf_op jit(solution)/shard_map/pallas_call | solution.py:323
  18.3 7.3 %collective-permute-done.4 = f32[17,8,128]{2,1,0:T(8,128)S(1)} collective-permute-done((f32[17,8,128]{2,1,0:T(8,128)S(1)}, f32[17,8,128]{2,1,0:T(8,128)S(1)}, u32[]{:S(2)}, u32[]{:S(2)}) %collective-permute-start.4) | collective-permute-done | bytes 69664 | tf_op jit(solution)/shard_map/ppermute | solution.py:345
  25.8 0.5 collective-permute-start.6
  26.3 0.7 %collective-permute-done.5 = f32[17,8,128]{2,1,0:T(8,128)S(1)} collective-permute-done((f32[17,8,128]{2,1,0:T(8,128)S(1)}, f32[17,8,128]{2,1,0:T(8,128)S(1)}, u32[]{:S(2)}, u32[]{:S(2)}) %collective-permute-start.5) | collective-permute-done | bytes 69664 | tf_op jit(solution)/shard_map/ppermute | solution.py:340
  27.1 0.5 collective-permute-done.6.theirs_ref
  27.5 3.0 %shard_map.61 = (f32[114,8,128]{2,1,0:T(8,128)S(1)}, f32[96,8,128]{2,1,0:T(8,128)S(1)}) custom-call(s32[1,5]{1,0:T(1,128)} %columns_ref.5, f32[113,8,128]{2,1,0:T(8,128)S(1)} %get-tuple-element.44.bundle_ref.start_ref, f32[32,512]{1,0:T(8,128)S(1)} %get-tuple-element.52.near_ref, f32[16,8,128]{2,1,0:T(8,128)S(1)} %slice_add_fusion.4.total_ref, ...), custom_call_target="tpu_custom_call" | custom-call | flops 1 | bytes 1 | tf_op jit(solution)/shard_map/pallas_call | solution.py:323
  30.6 0.4 collective-permute-start.7
  31.0 1.5 %collective-permute-done.7 = f32[114,8,128]{2,1,0:T(8,128)S(1)} collective-permute-done((f32[114,8,128]{2,1,0:T(8,128)S(1)}, f32[114,8,128]{2,1,0:T(8,128)S(1)}, u32[]{:S(2)}, u32[]{:S(2)}) %collective-permute-start.7) | collective-permute-done | bytes 466976 | tf_op jit(solution)/shard_map/ppermute | solution.py:340
  32.6 0.8 %collective-permute-start.10 = (f32[34,8,128]{2,1,0:T(8,128)S(1)}, f32[34,8,128]{2,1,0:T(8,128)S(1)}, u32[]{:S(2)}, u32[]{:S(2)}) collective-permute-start(f32[34,8,128]{2,1,0:T(8,128)S(1)} %get-tuple-element.94), channel_id=1, source_target_pairs={{6,0},{11,1},{8,2},{13,3},{10,4},{15,5},{12,6},{1,7},{14,8},{3,9},... | collective-permute-start | bytes 417800 | tf_op jit(solution)/shard_map/ppermute | solution.py:345
  33.4 2.5 %collective-permute-start.9 = (f32[34,8,128]{2,1,0:T(8,128)S(1)}, f32[34,8,128]{2,1,0:T(8,128)S(1)}, u32[]{:S(2)}, u32[]{:S(2)}) collective-permute-start(f32[34,8,128]{2,1,0:T(8,128)S(1)} %get-tuple-element.95), channel_id=1, source_target_pairs={{14,0},{13,1},{0,2},{15,3},{2,4},{1,5},{4,6},{3,7},{6,8},{5,9},{8,... | collective-permute-start | bytes 417800 | tf_op jit(solution)/shard_map/ppermute | solution.py:345
  35.9 2.2 %collective-permute-start.8 = (f32[34,8,128]{2,1,0:T(8,128)S(1)}, f32[34,8,128]{2,1,0:T(8,128)S(1)}, u32[]{:S(2)}, u32[]{:S(2)}) collective-permute-start(f32[34,8,128]{2,1,0:T(8,128)S(1)} %get-tuple-element.96.pair_ref), channel_id=1, source_target_pairs={{2,0},{5,1},{4,2},{7,3},{6,4},{9,5},{8,6},{11,7},{10,8},{13,9},{12... | collective-permute-start | bytes 417800 | tf_op jit(solution)/shard_map/ppermute | solution.py:345
  38.2 1.0 %shard_map.63 = (f32[32,32]{1,0:T(8,128)S(1)}, f32[32,1024]{1,0:T(8,128)S(1)}) custom-call(f32[1,8,128]{2,1,0:T(8,128)S(1)} %slice_add_fusion.8.sums_ref.first_sums_ref, f32[113,8,128]{2,1,0:T(8,128)S(1)} %get-tuple-element.44.bundle_ref.start_ref, f32[114,8,128]{2,1,0:T(8,128)S(1)} %get-tuple-element.63.bundle_ref.message_ref), custom_call_target="tpu_custom_call" | custom-call | flops 1 | bytes 1 | tf_op jit(solution)/shard_map/pallas_call | solution.py:323
  39.4 8.6 %collective-permute-done.11 = f32[18,8,128]{2,1,0:T(8,128)S(1)} collective-permute-done((f32[18,8,128]{2,1,0:T(8,128)S(1)}, f32[18,8,128]{2,1,0:T(8,128)S(1)}, u32[]{:S(2)}, u32[]{:S(2)}) %collective-permute-start.11) | collective-permute-done | bytes 73760 | tf_op jit(solution)/shard_map/ppermute | solution.py:345
  48.3 0.5 collective-permute-start.13
  48.8 0.8 %collective-permute-done.12 = f32[18,8,128]{2,1,0:T(8,128)S(1)} collective-permute-done((f32[18,8,128]{2,1,0:T(8,128)S(1)}, f32[18,8,128]{2,1,0:T(8,128)S(1)}, u32[]{:S(2)}, u32[]{:S(2)}) %collective-permute-start.12) | collective-permute-done | bytes 73760 | tf_op jit(solution)/shard_map/ppermute | solution.py:340
  49.6 0.5 collective-permute-done.13.theirs_ref
  50.1 3.1 %shard_map.64 = (f32[32,512]{1,0:T(8,128)S(1)}, f32[32,512]{1,0:T(8,128)S(1)}, f32[32,128]{1,0:T(8,128)S(1)}) custom-call(s32[1,5]{1,0:T(1,128)} %columns_ref.5, f32[113,8,128]{2,1,0:T(8,128)S(1)} %get-tuple-element.44.bundle_ref.start_ref, f32[114,8,128]{2,1,0:T(8,128)S(1)} %get-tuple-element.63.bundle_ref.message_ref, f32[32,512]{1,0:T(8,128)S(1)} %shard_map.62.near_ref, ...), custom_call_target="tpu_custom_call" | custom-call | flops 1 | bytes 1 | tf_op jit(solution)/shard_map/pallas_call | solution.py:323
  53.2 1.5 %collective-permute-start.16 = (f32[32,128]{1,0:T(8,128)S(1)}, f32[32,128]{1,0:T(8,128)S(1)}, u32[]{:S(2)}, u32[]{:S(2)}) collective-permute-start(f32[32,128]{1,0:T(8,128)S(1)} %get-tuple-element.77), channel_id=1, source_target_pairs={{12,0},{13,1},{14,2},{15,3},{8,4},{9,5},{10,6},{11,7},{4,8},{5,9},... | collective-permute-start | bytes 49160 | tf_op jit(solution)/shard_map/ppermute | solution.py:340
  54.7 3.0 %collective-permute-start.14 = (f32[32,128]{1,0:T(8,128)S(1)}, f32[32,128]{1,0:T(8,128)S(1)}, u32[]{:S(2)}, u32[]{:S(2)}) collective-permute-start(f32[32,128]{1,0:T(8,128)S(1)} %get-tuple-element.77), channel_id=1, source_target_pairs={{4,0},{5,1},{6,2},{7,3},{0,4},{1,5},{2,6},{3,7},{12,8},{13,9},{14,... | collective-permute-start | bytes 49160 | tf_op jit(solution)/shard_map/ppermute | solution.py:340
  57.7 1.2 %collective-permute-done.16 = f32[32,128]{1,0:T(8,128)S(1)} collective-permute-done((f32[32,128]{1,0:T(8,128)S(1)}, f32[32,128]{1,0:T(8,128)S(1)}, u32[]{:S(2)}, u32[]{:S(2)}) %collective-permute-start.16) | collective-permute-done | bytes 16416 | tf_op jit(solution)/shard_map/ppermute | solution.py:340
  58.8 0.5 collective-permute-done.15
  59.6 0.9 %collective-permute-start.18 = (f32[32,128]{1,0:T(8,128)S(1)}, f32[32,128]{1,0:T(8,128)S(1)}, u32[]{:S(2)}, u32[]{:S(2)}) collective-permute-start(f32[32,128]{1,0:T(8,128)S(1)} %add_add_fusion.1), channel_id=1, source_target_pairs={{2,0},{3,1},{0,2},{1,3},{6,4},{7,5},{4,6},{5,7},{10,8},{11,9},{8,1... | collective-permute-start | bytes 49160 | tf_op jit(solution)/shard_map/ppermute | solution.py:340
  60.5 0.9 %collective-permute-start.17 = (f32[32,128]{1,0:T(8,128)S(1)}, f32[32,128]{1,0:T(8,128)S(1)}, u32[]{:S(2)}, u32[]{:S(2)}) collective-permute-start(f32[32,128]{1,0:T(8,128)S(1)} %add_add_fusion.1), channel_id=1, source_target_pairs={{1,0},{0,1},{3,2},{2,3},{5,4},{4,5},{7,6},{6,7},{9,8},{8,9},{11,10... | collective-permute-start | bytes 49160 | tf_op jit(solution)/shard_map/ppermute | solution.py:340
  61.4 1.3 %collective-permute-done.19 = f32[32,128]{1,0:T(8,128)S(1)} collective-permute-done((f32[32,128]{1,0:T(8,128)S(1)}, f32[32,128]{1,0:T(8,128)S(1)}, u32[]{:S(2)}, u32[]{:S(2)}) %collective-permute-start.19) | collective-permute-done | bytes 16416 | tf_op jit(solution)/shard_map/ppermute | solution.py:340
  62.7 0.7 %collective-permute-done.18 = f32[32,128]{1,0:T(8,128)S(1)} collective-permute-done((f32[32,128]{1,0:T(8,128)S(1)}, f32[32,128]{1,0:T(8,128)S(1)}, u32[]{:S(2)}, u32[]{:S(2)}) %collective-permute-start.18) | collective-permute-done | bytes 16416 | tf_op jit(solution)/shard_map/ppermute | solution.py:340
  63.4 1.8 %shard_map.65 = (f32[32,512]{1,0:T(8,128)}, f32[4,32,32]{2,1,0:T(8,128)}) custom-call(f32[32,128]{1,0:T(8,128)S(1)} %add_add_fusion.share_ref, f32[32,512]{1,0:T(8,128)S(1)} %get-tuple-element.78.basis_ref, f32[32,512]{1,0:T(8,128)S(1)} %get-tuple-element.79.result_ref), custom_call_target="tpu_custom_call" | custom-call | flops 1 | bytes 1 | tf_op jit(solution)/shard_map/pallas_call | solution.py:323
  (48 shorter events, 1.3 us)
Async XLA Ops:
  4.9 11.9 %copy-start = (f32[512,512]{1,0:T(8,128)S(1)}, f32[512,512]{1,0:T(8,128)}, u32[]{:S(2)}) copy-start(f32[512,512]{1,0:T(8,128)} %diagonal_ref.1) | copy-start | bytes 3145732
  4.9 2.0 %collective-permute-start = (f32[113,8,128]{2,1,0:T(8,128)S(1)}, f32[113,8,128]{2,1,0:T(8,128)S(1)}, u32[]{:S(2)}, u32[]{:S(2)}) collective-permute-start(f32[113,8,128]{2,1,0:T(8,128)S(1)} %get-tuple-element.44.bundle_ref.start_ref), channel_id=1, source_target_pairs={{1,0},{0,1},{3,2},{2,3},{5,4},{4,5},{7,6},{6,7},{9,8},{8,9},{11,10... | collective-permute-start | bytes 1388552 | tf_op jit(solution)/shard_map/ppermute | solution.py:340
  7.0 18.5 %collective-permute-start.3 = (f32[33,8,128]{2,1,0:T(8,128)S(1)}, f32[33,8,128]{2,1,0:T(8,128)S(1)}, u32[]{:S(2)}, u32[]{:S(2)}) collective-permute-start(f32[33,8,128]{2,1,0:T(8,128)S(1)} %get-tuple-element.97), channel_id=1, source_target_pairs={{6,0},{11,1},{8,2},{13,3},{10,4},{15,5},{12,6},{1,7},{14,8},{3,9},... | collective-permute-start | bytes 405512 | tf_op jit(solution)/shard_map/ppermute | solution.py:345
  12.0 13.6 %collective-permute-start.2 = (f32[33,8,128]{2,1,0:T(8,128)S(1)}, f32[33,8,128]{2,1,0:T(8,128)S(1)}, u32[]{:S(2)}, u32[]{:S(2)}) collective-permute-start(f32[33,8,128]{2,1,0:T(8,128)S(1)} %get-tuple-element.98), channel_id=1, source_target_pairs={{14,0},{13,1},{0,2},{15,3},{2,4},{1,5},{4,6},{3,7},{6,8},{5,9},{8,... | collective-permute-start | bytes 405512 | tf_op jit(solution)/shard_map/ppermute | solution.py:345
  13.5 12.0 %collective-permute-start.1 = (f32[33,8,128]{2,1,0:T(8,128)S(1)}, f32[33,8,128]{2,1,0:T(8,128)S(1)}, u32[]{:S(2)}, u32[]{:S(2)}) collective-permute-start(f32[33,8,128]{2,1,0:T(8,128)S(1)} %get-tuple-element.99.pair_ref), channel_id=1, source_target_pairs={{2,0},{5,1},{4,2},{7,3},{6,4},{9,5},{8,6},{11,7},{10,8},{13,9},{12... | collective-permute-start | bytes 405512 | tf_op jit(solution)/shard_map/ppermute | solution.py:345
  16.7 8.8 %collective-permute-start.4 = (f32[17,8,128]{2,1,0:T(8,128)S(1)}, f32[17,8,128]{2,1,0:T(8,128)S(1)}, u32[]{:S(2)}, u32[]{:S(2)}) collective-permute-start(f32[17,8,128]{2,1,0:T(8,128)S(1)} %pad_maximum_fusion.10), channel_id=1, source_target_pairs={{8,0},{9,1},{10,2},{11,3},{12,4},{13,5},{14,6},{15,7},{0,8},{1,9},... | collective-permute-start | bytes 208904 | tf_op jit(solution)/shard_map/ppermute | solution.py:345
  25.7 1.3 %collective-permute-start.5 = (f32[17,8,128]{2,1,0:T(8,128)S(1)}, f32[17,8,128]{2,1,0:T(8,128)S(1)}, u32[]{:S(2)}, u32[]{:S(2)}) collective-permute-start(f32[17,8,128]{2,1,0:T(8,128)S(1)} %pad_maximum_fusion.11), channel_id=1, source_target_pairs={{1,0},{0,1},{3,2},{2,3},{5,4},{4,5},{7,6},{6,7},{9,8},{8,9},{11,10... | collective-permute-start | bytes 208904 | tf_op jit(solution)/shard_map/ppermute | solution.py:340
  25.8 1.8 %collective-permute-start.6 = (f32[80,8,128]{2,1,0:T(8,128)S(1)}, f32[80,8,128]{2,1,0:T(8,128)S(1)}, u32[]{:S(2)}, u32[]{:S(2)}) collective-permute-start(f32[80,8,128]{2,1,0:T(8,128)S(1)} %pad_maximum_fusion.mine_ref), channel_id=1, source_target_pairs={{1,0},{0,1},{3,2},{2,3},{5,4},{4,5},{7,6},{6,7},{9,8},{8,9},{11,10... | collective-permute-start | bytes 983048 | tf_op jit(solution)/shard_map/ppermute | solution.py:340
  30.6 1.9 %collective-permute-start.7 = (f32[114,8,128]{2,1,0:T(8,128)S(1)}, f32[114,8,128]{2,1,0:T(8,128)S(1)}, u32[]{:S(2)}, u32[]{:S(2)}) collective-permute-start(f32[114,8,128]{2,1,0:T(8,128)S(1)} %get-tuple-element.63.bundle_ref.message_ref), channel_id=1, source_target_pairs={{1,0},{0,1},{3,2},{2,3},{5,4},{4,5},{7,6},{6,7},{9,8},{8,9},{11,10... | collective-permute-start | bytes 1400840 | tf_op jit(solution)/shard_map/ppermute | solution.py:340
  32.6 15.4 %collective-permute-start.10 = (f32[34,8,128]{2,1,0:T(8,128)S(1)}, f32[34,8,128]{2,1,0:T(8,128)S(1)}, u32[]{:S(2)}, u32[]{:S(2)}) collective-permute-start(f32[34,8,128]{2,1,0:T(8,128)S(1)} %get-tuple-element.94), channel_id=1, source_target_pairs={{6,0},{11,1},{8,2},{13,3},{10,4},{15,5},{12,6},{1,7},{14,8},{3,9},... | collective-permute-start | bytes 417800 | tf_op jit(solution)/shard_map/ppermute | solution.py:345
  33.4 14.7 %collective-permute-start.9 = (f32[34,8,128]{2,1,0:T(8,128)S(1)}, f32[34,8,128]{2,1,0:T(8,128)S(1)}, u32[]{:S(2)}, u32[]{:S(2)}) collective-permute-start(f32[34,8,128]{2,1,0:T(8,128)S(1)} %get-tuple-element.95), channel_id=1, source_target_pairs={{14,0},{13,1},{0,2},{15,3},{2,4},{1,5},{4,6},{3,7},{6,8},{5,9},{8,... | collective-permute-start | bytes 417800 | tf_op jit(solution)/shard_map/ppermute | solution.py:345
  35.9 12.2 %collective-permute-start.8 = (f32[34,8,128]{2,1,0:T(8,128)S(1)}, f32[34,8,128]{2,1,0:T(8,128)S(1)}, u32[]{:S(2)}, u32[]{:S(2)}) collective-permute-start(f32[34,8,128]{2,1,0:T(8,128)S(1)} %get-tuple-element.96.pair_ref), channel_id=1, source_target_pairs={{2,0},{5,1},{4,2},{7,3},{6,4},{9,5},{8,6},{11,7},{10,8},{13,9},{12... | collective-permute-start | bytes 417800 | tf_op jit(solution)/shard_map/ppermute | solution.py:345
  38.1 9.9 %collective-permute-start.11 = (f32[18,8,128]{2,1,0:T(8,128)S(1)}, f32[18,8,128]{2,1,0:T(8,128)S(1)}, u32[]{:S(2)}, u32[]{:S(2)}) collective-permute-start(f32[18,8,128]{2,1,0:T(8,128)S(1)} %pad_maximum_fusion.8), channel_id=1, source_target_pairs={{8,0},{9,1},{10,2},{11,3},{12,4},{13,5},{14,6},{15,7},{0,8},{1,9},... | collective-permute-start | bytes 221192 | tf_op jit(solution)/shard_map/ppermute | solution.py:345
  48.2 1.3 %collective-permute-start.12 = (f32[18,8,128]{2,1,0:T(8,128)S(1)}, f32[18,8,128]{2,1,0:T(8,128)S(1)}, u32[]{:S(2)}, u32[]{:S(2)}) collective-permute-start(f32[18,8,128]{2,1,0:T(8,128)S(1)} %pad_maximum_fusion.9), channel_id=1, source_target_pairs={{1,0},{0,1},{3,2},{2,3},{5,4},{4,5},{7,6},{6,7},{9,8},{8,9},{11,10... | collective-permute-start | bytes 221192 | tf_op jit(solution)/shard_map/ppermute | solution.py:340
  48.3 1.8 %collective-permute-start.13 = (f32[80,8,128]{2,1,0:T(8,128)S(1)}, f32[80,8,128]{2,1,0:T(8,128)S(1)}, u32[]{:S(2)}, u32[]{:S(2)}) collective-permute-start(f32[80,8,128]{2,1,0:T(8,128)S(1)} %pad_maximum_fusion.1.mine_ref), channel_id=1, source_target_pairs={{1,0},{0,1},{3,2},{2,3},{5,4},{4,5},{7,6},{6,7},{9,8},{8,9},{11,10... | collective-permute-start | bytes 983048 | tf_op jit(solution)/shard_map/ppermute | solution.py:340
  53.2 5.6 %collective-permute-start.16 = (f32[32,128]{1,0:T(8,128)S(1)}, f32[32,128]{1,0:T(8,128)S(1)}, u32[]{:S(2)}, u32[]{:S(2)}) collective-permute-start(f32[32,128]{1,0:T(8,128)S(1)} %get-tuple-element.77), channel_id=1, source_target_pairs={{12,0},{13,1},{14,2},{15,3},{8,4},{9,5},{10,6},{11,7},{4,8},{5,9},... | collective-permute-start | bytes 49160 | tf_op jit(solution)/shard_map/ppermute | solution.py:340
  54.7 4.6 %collective-permute-start.15 = (f32[32,128]{1,0:T(8,128)S(1)}, f32[32,128]{1,0:T(8,128)S(1)}, u32[]{:S(2)}, u32[]{:S(2)}) collective-permute-start(f32[32,128]{1,0:T(8,128)S(1)} %get-tuple-element.77), channel_id=1, source_target_pairs={{8,0},{9,1},{10,2},{11,3},{12,4},{13,5},{14,6},{15,7},{0,8},{1,9},... | collective-permute-start | bytes 49160 | tf_op jit(solution)/shard_map/ppermute | solution.py:340
  54.7 4.8 %collective-permute-start.14 = (f32[32,128]{1,0:T(8,128)S(1)}, f32[32,128]{1,0:T(8,128)S(1)}, u32[]{:S(2)}, u32[]{:S(2)}) collective-permute-start(f32[32,128]{1,0:T(8,128)S(1)} %get-tuple-element.77), channel_id=1, source_target_pairs={{4,0},{5,1},{6,2},{7,3},{0,4},{1,5},{2,6},{3,7},{12,8},{13,9},{14,... | collective-permute-start | bytes 49160 | tf_op jit(solution)/shard_map/ppermute | solution.py:340
  59.5 3.2 %collective-permute-start.19 = (f32[32,128]{1,0:T(8,128)S(1)}, f32[32,128]{1,0:T(8,128)S(1)}, u32[]{:S(2)}, u32[]{:S(2)}) collective-permute-start(f32[32,128]{1,0:T(8,128)S(1)} %add_add_fusion.1), channel_id=1, source_target_pairs={{3,0},{2,1},{1,2},{0,3},{7,4},{6,5},{5,6},{4,7},{11,8},{10,9},{9,1... | collective-permute-start | bytes 49160 | tf_op jit(solution)/shard_map/ppermute | solution.py:340
  59.6 3.8 %collective-permute-start.18 = (f32[32,128]{1,0:T(8,128)S(1)}, f32[32,128]{1,0:T(8,128)S(1)}, u32[]{:S(2)}, u32[]{:S(2)}) collective-permute-start(f32[32,128]{1,0:T(8,128)S(1)} %add_add_fusion.1), channel_id=1, source_target_pairs={{2,0},{3,1},{0,2},{1,3},{6,4},{7,5},{4,6},{5,7},{10,8},{11,9},{8,1... | collective-permute-start | bytes 49160 | tf_op jit(solution)/shard_map/ppermute | solution.py:340
  60.5 2.9 %collective-permute-start.17 = (f32[32,128]{1,0:T(8,128)S(1)}, f32[32,128]{1,0:T(8,128)S(1)}, u32[]{:S(2)}, u32[]{:S(2)}) collective-permute-start(f32[32,128]{1,0:T(8,128)S(1)} %add_add_fusion.1), channel_id=1, source_target_pairs={{1,0},{0,1},{3,2},{2,3},{5,4},{4,5},{7,6},{6,7},{9,8},{8,9},{11,10... | collective-permute-start | bytes 49160 | tf_op jit(solution)/shard_map/ppermute | solution.py:340
